TPU v7x, 32 devices: a whole 2x2x4 slice. The times are simulated.
32 devices in a mesh: groups: 2 (over x), dom: 16 (over z, y, core).
Axes of the slice: x: 2, y: 2, z: 4, core: 2. Of those that a mesh axis runs over, the one named last changes fastest.
Arguments:
- particle_places: float32 [16, 3, 3072], P('groups', None, 'dom'), parts along dimension 0, may hold values from 0 to 48, as said below
- particle_speeds: float32 [16, 3, 3072], P('groups', None, 'dom'), parts along dimension 0, may hold values from -7 to 7
- thermal_targets: float32 [16], P('groups'), parts along dimension 0, may hold values from 0.5 to 2
- element_features: bfloat16 [6144, 128], P(('groups', 'dom')), parts along dimension 0, may hold values from -4 to 4
- swap_counterpart_slot: int32 [16], P('groups'), parts along dimension 0, may hold values from 0 to 7, as said below
- swap_approval_flags: int32 [16], P('groups'), parts along dimension 0, may hold values from 0 to 1, as said below
- initial_signal_projector: bfloat16 [128, 128], replicated, may hold values from -0.5 to 0.5
- initial_distance_filter: float32 [8, 128], replicated, may hold values from -2 to 2
- initial_directional_scales: float32 [128], replicated, may hold values from 0.5 to 1.5
- invariant_revision_matrix: bfloat16 [128, 128], replicated, may hold values from -0.5 to 0.5
- magnitude_revision_matrix: bfloat16 [128, 128], replicated, may hold values from -0.5 to 0.5
- later_signal_projector: bfloat16 [128, 128], replicated, may hold values from -0.5 to 0.5
- later_directional_scales: float32 [128], replicated, may hold values from 0.5 to 1.5
- push_output_matrix: float32 [128], replicated, may hold values from -0.5 to 0.5
Outputs:
- positions_new: float32 [16, 3, 3072], P('groups', None, 'dom'), parts along dimension 0
- velocities_new: float32 [16, 3, 3072], P('groups', None, 'dom'), parts along dimension 0
- forces_new: float32 [16, 3, 3072], P('groups', None, 'dom'), parts along dimension 0
There are 2 independent parts, one for each index of `groups`. A program takes and returns all parts, laid end to end along the dimension named above; an argument that names none is the same for every part. Nothing has to cross between parts.
Inputs may be any that keep to these rules, and one draw needn't show every extreme that they name: `particle_places`: the atoms of cell k have x and y in [0, 1) and z in [k, k + 1). `swap_counterpart_slot`: an involution that pairs neighbouring replicas, either (0, 1), (2, 3), ... or (1, 2), (3, 4), ..., a replica left without a pair being its own partner. `swap_approval_flags`: equal for the two replicas of a pair, 0 for a replica that is its own partner.
All inputs are finite; a program needn't handle non-finite values.
Results may differ from a plain program's by a relative error of at most 0.012.
The roundings to bfloat16 on the way count: a program that leaves them out, or rounds other values in their place, can miss the bound.
Values may be sent and summed in bfloat16 or wider, within the bound.
No kernel may reach another device: no remote copies, remote signals or barrier semaphores. Data moves between devices by JAX's collectives and lax.ppermute only.
A program may use at most 64 MiB of HBM per device.

v0:
```python
import jax
import jax.numpy as jnp
from jax import lax
from jax.sharding import PartitionSpec as P

NA = 64
HC = 1
STEPS = 4


step_time = 0.05
motion_work_lower_limit = 1e-06


def with_halo(cells, sides, width):
    for axis, dim in sides:
        count = lax.axis_size(axis)
        head = lax.slice_in_dim(cells, 0, width, axis=dim)
        tail = lax.slice_in_dim(cells, cells.shape[dim] - width, cells.shape[dim], axis=dim)
        cells = jnp.concatenate(
            [
                lax.ppermute(tail, axis, [(i, (i + 1) % count) for i in range(count)]),
                cells,
                lax.ppermute(head, axis, [((i + 1) % count, i) for i in range(count)]),
            ],
            axis=dim,
        )
    return cells


def radial_rows(own_coords, part_coords, basis_count):
    displacement = part_coords[:, :, :, None, :] - own_coords[:, :, :, :, None]
    squared = jnp.sum(displacement * displacement, axis=1)
    envelope = jnp.where(squared < 1.0, (1.0 - squared) * (1.0 - squared), 0.0)
    vectors = jnp.moveaxis(displacement * envelope[:, None], 1, 3)
    if basis_count == 0:
        return vectors.astype(jnp.bfloat16)
    centers = jnp.arange(basis_count, dtype=jnp.float32) / (basis_count - 1)
    sharpness = 2.0 * (basis_count - 1) * (basis_count - 1)
    offset = squared[:, :, :, None, :] - centers[:, None]
    gaussians = jnp.exp(-sharpness * offset * offset) * envelope[:, :, :, None, :]
    return jnp.concatenate([gaussians, vectors], axis=3).astype(jnp.bfloat16)


def coord_windows(location_triples, first_cell, cell_count):
    leading = location_triples.shape[:2]
    own_coords = location_triples[:, :, first_cell * NA : (first_cell + cell_count) * NA].reshape(
        leading + (cell_count, NA)
    )
    pieces = []
    for neighbor in range(2 * HC + 1):
        begin_atom = (first_cell - HC + neighbor) * NA
        pieces.append(
            location_triples[:, :, begin_atom : begin_atom + cell_count * NA].reshape(
                leading + (cell_count, NA)
            )
        )
    return (own_coords, jnp.concatenate(pieces, axis=3))


def feature_windows(features, first_cell, cell_count):
    leading = features.shape[:-2]
    channels = features.shape[-1]
    pieces = []
    for neighbor in range(2 * HC + 1):
        begin_atom = (first_cell - HC + neighbor) * NA
        pieces.append(
            features[..., begin_atom : begin_atom + cell_count * NA, :].reshape(
                leading + (cell_count, NA, channels)
            )
        )
    return jnp.concatenate(pieces, axis=-2)


def periodic_shift(extended, halo_cells):
    own_index = lax.axis_index("dom")
    local_cells = extended.shape[2] // NA - 2 * halo_cells
    total_cells = local_cells * lax.axis_size("dom")
    cell_number = (
        own_index * local_cells - halo_cells + jnp.arange(extended.shape[2], dtype=jnp.int32) // NA
    )
    wrap_shift = (
        jnp.where(cell_number < 0, -1.0, 0.0) + jnp.where(cell_number >= total_cells, 1.0, 0.0)
    ) * total_cells
    axis_mask = jnp.array([0.0, 0.0, 1.0], jnp.float32)
    return extended + axis_mask[None, :, None] * wrap_shift[None, None, :]


def layer_one(
    location_triples,
    first_cell,
    cell_count,
    first_table,
    self_rows,
    initial_distance_filter,
    initial_directional_scales,
    invariant_revision_matrix,
    magnitude_revision_matrix,
):
    replicas = location_triples.shape[0]
    channels = invariant_revision_matrix.shape[0]
    basis_count = initial_distance_filter.shape[0]
    own_coords, part_coords = coord_windows(location_triples, first_cell, cell_count)
    single_row_count = radial_rows(own_coords, part_coords, basis_count)
    exchange_mate = feature_windows(first_table, first_cell, cell_count)
    reduced_sum = jnp.einsum(
        "vyegd,ydm->vyegm", single_row_count, exchange_mate, preferred_element_type=jnp.float32
    )
    scalar = jnp.sum(reduced_sum[:, :, :, :basis_count] * initial_distance_filter, axis=3)
    vector_one = reduced_sum[:, :, :, basis_count:] * initial_directional_scales
    norm_square = jnp.sum(vector_one * vector_one, axis=3)
    update = jnp.dot(
        scalar.astype(jnp.bfloat16).reshape(-1, channels),
        invariant_revision_matrix,
        preferred_element_type=jnp.float32,
    )
    update = update + jnp.dot(
        norm_square.astype(jnp.bfloat16).reshape(-1, channels),
        magnitude_revision_matrix,
        preferred_element_type=jnp.float32,
    )
    hidden = self_rows.astype(jnp.float32)[None] + jax.nn.silu(update).reshape(
        replicas, cell_count * NA, channels
    )
    return (hidden.astype(jnp.bfloat16), vector_one)


def layer_two(location_triples, first_cell, cell_count, second_table, later_directional_scales):
    own_coords, part_coords = coord_windows(location_triples, first_cell, cell_count)
    rows_two = radial_rows(own_coords, part_coords, 0)
    exchange_mate = feature_windows(second_table, first_cell, cell_count)
    reduced_sum = jnp.einsum(
        "rcaxb,rcbf->rcaxf", rows_two, exchange_mate, preferred_element_type=jnp.float32
    )
    return reduced_sum * later_directional_scales


def readout(vectors, push_output_matrix):
    reduced_sum = jnp.sum(vectors * push_output_matrix, axis=4)
    return jnp.transpose(reduced_sum, (0, 3, 1, 2)).reshape(reduced_sum.shape[0], 3, -1)


def on_device(
    particle_places,
    particle_speeds,
    thermal_targets,
    element_features,
    swap_counterpart_slot,
    swap_approval_flags,
    initial_signal_projector,
    initial_distance_filter,
    initial_directional_scales,
    invariant_revision_matrix,
    magnitude_revision_matrix,
    later_signal_projector,
    later_directional_scales,
    push_output_matrix,
):
    replicas = particle_places.shape[0]
    local_cells = particle_places.shape[2] // NA
    channels = initial_signal_projector.shape[0]
    particle_number_overall = local_cells * lax.axis_size("dom") * NA
    near_species = with_halo(element_features, (("dom", 0),), HC * NA)
    first_table = jnp.dot(
        near_species, initial_signal_projector, preferred_element_type=jnp.float32
    ).astype(jnp.bfloat16)

    def evaluate(location_triples):
        near_coords = periodic_shift(with_halo(location_triples, (("dom", 2),), HC * NA), HC)
        hidden, vector_one = layer_one(
            near_coords,
            HC,
            local_cells,
            first_table,
            element_features,
            initial_distance_filter,
            initial_directional_scales,
            invariant_revision_matrix,
            magnitude_revision_matrix,
        )
        second_own = (
            jnp.dot(
                hidden.reshape(-1, channels),
                later_signal_projector,
                preferred_element_type=jnp.float32,
            )
            .astype(jnp.bfloat16)
            .reshape(replicas, -1, channels)
        )
        second_table = with_halo(second_own, (("dom", 1),), HC * NA)
        vector_two = layer_two(near_coords, HC, local_cells, second_table, later_directional_scales)
        return readout(vector_one + vector_two, push_output_matrix)

    location_triples = particle_places
    speed_entry = particle_speeds
    present_push = evaluate(location_triples)
    for step_index in range(STEPS):
        half_velocity = speed_entry + 0.5 * step_time * present_push
        location_triples = location_triples + step_time * half_velocity
        present_push = evaluate(location_triples)
        speed_entry = half_velocity + 0.5 * step_time * present_push
        motion_work_amount = lax.psum(jnp.sum(speed_entry * speed_entry, axis=(1, 2)), "dom")
        stretch_multiplier = jnp.sqrt(
            thermal_targets
            / (motion_work_amount / (3.0 * particle_number_overall) + motion_work_lower_limit)
        )
        speed_entry = speed_entry * stretch_multiplier[:, None, None]
    ladder_slot = jnp.arange(thermal_targets.shape[0], dtype=jnp.int32)
    source = jnp.where(swap_approval_flags > 0, swap_counterpart_slot, ladder_slot)
    selected_entries = (source[:, None] == ladder_slot[None, :]).astype(jnp.float32)

    def select_entries(values):
        return jnp.sum(selected_entries[:, :, None, None] * values[None], axis=1)

    thermal_ratio = jnp.sqrt(
        thermal_targets / jnp.sum(selected_entries * thermal_targets[None, :], axis=1)
    )
    atom_cell = (
        lax.axis_index("dom") * local_cells
        + jnp.arange(particle_places.shape[2], dtype=jnp.int32) // NA
    ).astype(jnp.float32)
    cell_floor = jnp.array([0.0, 0.0, 1.0], jnp.float32)[:, None] * atom_cell[None, :]
    return (
        select_entries(location_triples) - cell_floor[None],
        select_entries(speed_entry) * thermal_ratio[:, None, None],
        select_entries(present_push),
    )


def solution(mesh):
    return jax.shard_map(
        on_device,
        mesh=mesh,
        in_specs=(
            P("groups", None, "dom"),
            P("groups", None, "dom"),
            P("groups"),
            P(("groups", "dom"), None),
            P("groups"),
            P("groups"),
            P(),
            P(),
            P(),
            P(),
            P(),
            P(),
            P(),
            P(),
        ),
        out_specs=(P("groups", None, "dom"), P("groups", None, "dom"), P("groups", None, "dom")),
        check_vma=False,
    )
```

profile of v0, /device:TPU:0, one launch (start us, length us, event | category | flops | bytes accessed | tf_op | source)
XLA Modules:
  0.0 299.5 jit_solution(10295217078353361649)
XLA Ops:
  1.8 5.0 %collective-permute-start.3 = (f32[8,3,64]{2,0,1:T(8,128)S(1)}, f32[8,3,64]{2,0,1:T(8,128)S(1)}, u32[]{:S(2)}, u32[]{:S(2)}) collective-permute-start(f32[8,3,64]{2,0,1:T(8,128)S(1)} %get-tuple-element.66), channel_id=1, source_target_pairs={{1,0},{2,1},{3,2},{4,3},{5,4},{6,5},{7,6},{8,7},{9,8},{10,9},{11,1... | collective-permute-start | bytes 18440 | tf_op jit(solution)/shard_map/ppermute | solution.py:24
  7.6 4.4 %collective-permute-start.1 = (bf16[64,128]{1,0:T(8,128)(2,1)S(1)}, bf16[64,128]{1,0:T(8,128)(2,1)S(1)}, u32[]{:S(2)}, u32[]{:S(2)}) collective-permute-start(bf16[64,128]{1,0:T(8,128)(2,1)S(1)} %get-tuple-element.41), channel_id=1, source_target_pairs={{1,0},{2,1},{3,2},{4,3},{5,4},{6,5},{7,6},{8,7},{9,8},{10,9},{11,1... | collective-permute-start | bytes 49160 | tf_op jit(solution)/shard_map/ppermute | solution.py:24
  15.7 5.1 %fusion.2 = bf16[8,3,64,8,192]{4,2,3,0,1:T(8,128)(2,1)} fusion(f32[8]{0:T(128)S(1)} %iota_multiply_fusion, f32[8,3,64,192]{3,2,1,0:T(8,128)S(1)} %multiply_reduce_fusion.4), kind=kLoop, calls=%fused_computation.7 | loop fusion | flops 12976128 | bytes 5898272 | tf_op jit(solution)/shard_map/convert.8
  22.2 5.0 %fusion.52 = f32[8,3,64,11,128]{4,2,3,0,1:T(8,128)S(1)} fusion(bf16[8,3,64,3,192]{4,2,3,0,1:T(8,128)(2,1)S(1)} %multiply_convert_fusion.4, bf16[8,3,64,8,192]{4,2,3,0,1:T(8,128)(2,1)} %fusion.2, bf16[3,64,128]{2,1,0:T(8,128)(2,1)S(1)} %bitcast.203, bf16[3,64,128]{2,1,0:T(8,128)(2,1)S(1)} %bitcast.208, bf16[3,64,128]{2,1,0:T(8,128)(2,1)S(1)} %bitcast.198), kind=kOutput, calls=%fused_computation.64 | convolution fusion | flops 843890688 | bytes 15286272 | tf_op jit(solution)/shard_map/vyegd,ydm->vyegm/dot_general | solution.py:106
  29.6 4.4 %collective-permute-start.5 = (bf16[8,64,128]{2,1,0:T(8,128)(2,1)S(1)}, bf16[8,64,128]{2,1,0:T(8,128)(2,1)S(1)}, u32[]{:S(2)}, u32[]{:S(2)}) collective-permute-start(bf16[8,64,128]{2,1,0:T(8,128)(2,1)S(1)} %get-tuple-element.36), channel_id=1, source_target_pairs={{1,0},{2,1},{3,2},{4,3},{5,4},{6,5},{7,6},{8,7},{9,8},{10,9},{11,1... | collective-permute-start | bytes 393224 | tf_op jit(solution)/shard_map/ppermute | solution.py:24
  39.1 4.8 %collective-permute-start.7 = (f32[8,3,64]{2,0,1:T(8,128)S(1)}, f32[8,3,64]{2,0,1:T(8,128)S(1)}, u32[]{:S(2)}, u32[]{:S(2)}) collective-permute-start(f32[8,3,64]{2,0,1:T(8,128)S(1)} %get-tuple-element.64), channel_id=1, source_target_pairs={{1,0},{2,1},{3,2},{4,3},{5,4},{6,5},{7,6},{8,7},{9,8},{10,9},{11,1... | collective-permute-start | bytes 18440 | tf_op jit(solution)/shard_map/ppermute | solution.py:24
  46.6 5.1 %fusion.5 = bf16[8,3,64,8,192]{4,2,3,0,1:T(8,128)(2,1)} fusion(f32[8]{0:T(128)S(1)} %iota_multiply_fusion, f32[8,3,64,192]{3,2,1,0:T(8,128)S(1)} %multiply_reduce_fusion.3), kind=kLoop, calls=%fused_computation.10 | loop fusion | flops 12976128 | bytes 5898272 | tf_op jit(solution)/shard_map/convert.6
  53.0 5.0 %fusion.49 = f32[8,3,64,11,128]{4,2,3,0,1:T(8,128)S(1)} fusion(bf16[8,3,64,3,192]{4,2,3,0,1:T(8,128)(2,1)S(1)} %multiply_convert_fusion.3, bf16[8,3,64,8,192]{4,2,3,0,1:T(8,128)(2,1)} %fusion.5, bf16[3,64,128]{2,1,0:T(8,128)(2,1)S(1)} %bitcast.204, bf16[3,64,128]{2,1,0:T(8,128)(2,1)S(1)} %bitcast.209, bf16[3,64,128]{2,1,0:T(8,128)(2,1)S(1)} %bitcast.199), kind=kOutput, calls=%fused_computation.63 | convolution fusion | flops 843890688 | bytes 15286272 | tf_op jit(solution)/shard_map/vyegd,ydm->vyegm/dot_general | solution.py:106
  60.2 4.5 %collective-permute-start.9 = (bf16[8,64,128]{2,1,0:T(8,128)(2,1)S(1)}, bf16[8,64,128]{2,1,0:T(8,128)(2,1)S(1)}, u32[]{:S(2)}, u32[]{:S(2)}) collective-permute-start(bf16[8,64,128]{2,1,0:T(8,128)(2,1)S(1)} %get-tuple-element.32), channel_id=1, source_target_pairs={{1,0},{2,1},{3,2},{4,3},{5,4},{6,5},{7,6},{8,7},{9,8},{10,9},{11,1... | collective-permute-start | bytes 393224 | tf_op jit(solution)/shard_map/ppermute | solution.py:24
  69.7 33.9 %psum.28 = f32[8]{0:T(128)S(1)} all-reduce(f32[8]{0:T(128)S(1)} %get-tuple-element.13), channel_id=1, replica_groups=mesh['groups'=2,'dom'=16] {'dom'}, use_global_device_ids=true, to_apply=%region_9.10 | all-reduce | flops 8 | bytes 64 | tf_op jit(solution)/shard_map/psum | solution.py:202
  103.8 4.4 %collective-permute-start.11 = (f32[8,3,64]{2,0,1:T(8,128)S(1)}, f32[8,3,64]{2,0,1:T(8,128)S(1)}, u32[]{:S(2)}, u32[]{:S(2)}) collective-permute-start(f32[8,3,64]{2,0,1:T(8,128)S(1)} %get-tuple-element.62), channel_id=1, source_target_pairs={{1,0},{2,1},{3,2},{4,3},{5,4},{6,5},{7,6},{8,7},{9,8},{10,9},{11,1... | collective-permute-start | bytes 18440 | tf_op jit(solution)/shard_map/ppermute | solution.py:24
  110.9 5.1 %fusion.8 = bf16[8,3,64,8,192]{4,2,3,0,1:T(8,128)(2,1)} fusion(f32[8]{0:T(128)S(1)} %iota_multiply_fusion, f32[8,3,64,192]{3,2,1,0:T(8,128)S(1)} %multiply_reduce_fusion.2), kind=kLoop, calls=%fused_computation.13 | loop fusion | flops 12976128 | bytes 5898272 | tf_op jit(solution)/shard_map/convert.4
  117.3 5.0 %fusion.46 = f32[8,3,64,11,128]{4,2,3,0,1:T(8,128)S(1)} fusion(bf16[8,3,64,3,192]{4,2,3,0,1:T(8,128)(2,1)S(1)} %multiply_convert_fusion.2, bf16[8,3,64,8,192]{4,2,3,0,1:T(8,128)(2,1)} %fusion.8, bf16[3,64,128]{2,1,0:T(8,128)(2,1)S(1)} %bitcast.205, bf16[3,64,128]{2,1,0:T(8,128)(2,1)S(1)} %bitcast.210, bf16[3,64,128]{2,1,0:T(8,128)(2,1)S(1)} %bitcast.200), kind=kOutput, calls=%fused_computation.62 | convolution fusion | flops 843890688 | bytes 15286272 | tf_op jit(solution)/shard_map/vyegd,ydm->vyegm/dot_general | solution.py:106
  124.5 4.5 %collective-permute-start.13 = (bf16[8,64,128]{2,1,0:T(8,128)(2,1)S(1)}, bf16[8,64,128]{2,1,0:T(8,128)(2,1)S(1)}, u32[]{:S(2)}, u32[]{:S(2)}) collective-permute-start(bf16[8,64,128]{2,1,0:T(8,128)(2,1)S(1)} %get-tuple-element.28), channel_id=1, source_target_pairs={{1,0},{2,1},{3,2},{4,3},{5,4},{6,5},{7,6},{8,7},{9,8},{10,9},{11,1... | collective-permute-start | bytes 393224 | tf_op jit(solution)/shard_map/ppermute | solution.py:24
  134.0 34.0 %psum.29 = f32[8]{0:T(128)S(1)} all-reduce(f32[8]{0:T(128)S(1)} %get-tuple-element.11), channel_id=1, replica_groups=mesh['groups'=2,'dom'=16] {'dom'}, use_global_device_ids=true, to_apply=%region_15.16 | all-reduce | flops 8 | bytes 64 | tf_op jit(solution)/shard_map/psum | solution.py:202
  168.1 4.4 %collective-permute-start.15 = (f32[8,3,64]{2,0,1:T(8,128)S(1)}, f32[8,3,64]{2,0,1:T(8,128)S(1)}, u32[]{:S(2)}, u32[]{:S(2)}) collective-permute-start(f32[8,3,64]{2,0,1:T(8,128)S(1)} %get-tuple-element.60), channel_id=1, source_target_pairs={{1,0},{2,1},{3,2},{4,3},{5,4},{6,5},{7,6},{8,7},{9,8},{10,9},{11,1... | collective-permute-start | bytes 18440 | tf_op jit(solution)/shard_map/ppermute | solution.py:24
  175.3 5.1 %fusion.11 = bf16[8,3,64,8,192]{4,2,3,0,1:T(8,128)(2,1)} fusion(f32[8]{0:T(128)S(1)} %iota_multiply_fusion, f32[8,3,64,192]{3,2,1,0:T(8,128)S(1)} %multiply_reduce_fusion.1), kind=kLoop, calls=%fused_computation.16 | loop fusion | flops 12976128 | bytes 5898272 | tf_op jit(solution)/shard_map/convert.2
  181.7 5.0 %fusion.43 = f32[8,3,64,11,128]{4,2,3,0,1:T(8,128)S(1)} fusion(bf16[8,3,64,3,192]{4,2,3,0,1:T(8,128)(2,1)S(1)} %multiply_convert_fusion.1, bf16[8,3,64,8,192]{4,2,3,0,1:T(8,128)(2,1)} %fusion.11, bf16[3,64,128]{2,1,0:T(8,128)(2,1)S(1)} %bitcast.206, bf16[3,64,128]{2,1,0:T(8,128)(2,1)S(1)} %bitcast.211, bf16[3,64,128]{2,1,0:T(8,128)(2,1)S(1)} %bitcast.201), kind=kOutput, calls=%fused_computation.61 | convolution fusion | flops 843890688 | bytes 15286272 | tf_op jit(solution)/shard_map/vyegd,ydm->vyegm/dot_general | solution.py:106
  189.1 4.5 %collective-permute-start.17 = (bf16[8,64,128]{2,1,0:T(8,128)(2,1)S(1)}, bf16[8,64,128]{2,1,0:T(8,128)(2,1)S(1)}, u32[]{:S(2)}, u32[]{:S(2)}) collective-permute-start(bf16[8,64,128]{2,1,0:T(8,128)(2,1)S(1)} %get-tuple-element.24), channel_id=1, source_target_pairs={{1,0},{2,1},{3,2},{4,3},{5,4},{6,5},{7,6},{8,7},{9,8},{10,9},{11,1... | collective-permute-start | bytes 393224 | tf_op jit(solution)/shard_map/ppermute | solution.py:24
  198.8 33.9 %psum.30 = f32[8]{0:T(128)S(1)} all-reduce(f32[8]{0:T(128)S(1)} %multiply_reduce_fusion.19), channel_id=1, replica_groups=mesh['groups'=2,'dom'=16] {'dom'}, use_global_device_ids=true, to_apply=%region_21.22 | all-reduce | flops 8 | bytes 64 | tf_op jit(solution)/shard_map/psum | solution.py:202
  240.0 5.1 %fusion.14 = bf16[8,3,64,8,192]{4,2,3,0,1:T(8,128)(2,1)} fusion(f32[8]{0:T(128)S(1)} %iota_multiply_fusion, f32[8,3,64,192]{3,2,1,0:T(8,128)S(1)} %multiply_reduce_fusion), kind=kLoop, calls=%fused_computation.19 | loop fusion | flops 12976128 | bytes 5898272 | tf_op jit(solution)/shard_map/convert
  246.4 5.0 %fusion.40 = f32[8,3,64,11,128]{4,2,3,0,1:T(8,128)S(1)} fusion(bf16[8,3,64,3,192]{4,2,3,0,1:T(8,128)(2,1)S(1)} %multiply_convert_fusion, bf16[8,3,64,8,192]{4,2,3,0,1:T(8,128)(2,1)} %fusion.14, bf16[3,64,128]{2,1,0:T(8,128)(2,1)S(1)} %bitcast.207, bf16[3,64,128]{2,1,0:T(8,128)(2,1)S(1)} %bitcast.212, bf16[3,64,128]{2,1,0:T(8,128)(2,1)S(1)} %bitcast.202), kind=kOutput, calls=%fused_computation.60 | convolution fusion | flops 843890688 | bytes 15286272 | tf_op jit(solution)/shard_map/vyegd,ydm->vyegm/dot_general | solution.py:106
  253.6 4.5 %collective-permute-start.21 = (bf16[8,64,128]{2,1,0:T(8,128)(2,1)S(1)}, bf16[8,64,128]{2,1,0:T(8,128)(2,1)S(1)}, u32[]{:S(2)}, u32[]{:S(2)}) collective-permute-start(bf16[8,64,128]{2,1,0:T(8,128)(2,1)S(1)} %get-tuple-element.20), channel_id=1, source_target_pairs={{1,0},{2,1},{3,2},{4,3},{5,4},{6,5},{7,6},{8,7},{9,8},{10,9},{11,1... | collective-permute-start | bytes 393224 | tf_op jit(solution)/shard_map/ppermute | solution.py:24
  263.2 34.0 %psum.31 = f32[8]{0:T(128)S(1)} all-reduce(f32[8]{0:T(128)S(1)} %multiply_reduce_fusion.18), channel_id=1, replica_groups=mesh['groups'=2,'dom'=16] {'dom'}, use_global_device_ids=true, to_apply=%region_28.29 | all-reduce | flops 8 | bytes 64 | tf_op jit(solution)/shard_map/psum | solution.py:202
  (213 shorter events, 65.9 us)
Async XLA Ops:
  1.4 12.2 %collective-permute-start.2 = (f32[8,3,64]{2,0,1:T(8,128)S(1)}, f32[8,3,64]{2,0,1:T(8,128)S(1)}, u32[]{:S(2)}, u32[]{:S(2)}) collective-permute-start(f32[8,3,64]{2,0,1:T(8,128)S(1)} %get-tuple-element.65), channel_id=1, source_target_pairs={{0,1},{1,2},{2,3},{3,4},{4,5},{5,6},{6,7},{7,8},{8,9},{9,10},{10,1... | collective-permute-start | bytes 18440 | tf_op jit(solution)/shard_map/ppermute | solution.py:22
  1.8 11.7 %collective-permute-start.3 = (f32[8,3,64]{2,0,1:T(8,128)S(1)}, f32[8,3,64]{2,0,1:T(8,128)S(1)}, u32[]{:S(2)}, u32[]{:S(2)}) collective-permute-start(f32[8,3,64]{2,0,1:T(8,128)S(1)} %get-tuple-element.66), channel_id=1, source_target_pairs={{1,0},{2,1},{3,2},{4,3},{5,4},{6,5},{7,6},{8,7},{9,8},{10,9},{11,1... | collective-permute-start | bytes 18440 | tf_op jit(solution)/shard_map/ppermute | solution.py:24
  7.6 14.4 %collective-permute-start = (bf16[64,128]{1,0:T(8,128)(2,1)S(1)}, bf16[64,128]{1,0:T(8,128)(2,1)S(1)}, u32[]{:S(2)}, u32[]{:S(2)}) collective-permute-start(bf16[64,128]{1,0:T(8,128)(2,1)S(1)} %get-tuple-element.40), channel_id=1, source_target_pairs={{0,1},{1,2},{2,3},{3,4},{4,5},{5,6},{6,7},{7,8},{8,9},{9,10},{10,1... | collective-permute-start | bytes 49160 | tf_op jit(solution)/shard_map/ppermute | solution.py:22
  7.6 14.4 %collective-permute-start.1 = (bf16[64,128]{1,0:T(8,128)(2,1)S(1)}, bf16[64,128]{1,0:T(8,128)(2,1)S(1)}, u32[]{:S(2)}, u32[]{:S(2)}) collective-permute-start(bf16[64,128]{1,0:T(8,128)(2,1)S(1)} %get-tuple-element.41), channel_id=1, source_target_pairs={{1,0},{2,1},{3,2},{4,3},{5,4},{6,5},{7,6},{8,7},{9,8},{10,9},{11,1... | collective-permute-start | bytes 49160 | tf_op jit(solution)/shard_map/ppermute | solution.py:24
  29.6 7.1 %collective-permute-start.4 = (bf16[8,64,128]{2,1,0:T(8,128)(2,1)S(1)}, bf16[8,64,128]{2,1,0:T(8,128)(2,1)S(1)}, u32[]{:S(2)}, u32[]{:S(2)}) collective-permute-start(bf16[8,64,128]{2,1,0:T(8,128)(2,1)S(1)} %get-tuple-element.35), channel_id=1, source_target_pairs={{0,1},{1,2},{2,3},{3,4},{4,5},{5,6},{6,7},{7,8},{8,9},{9,10},{10,1... | collective-permute-start | bytes 393224 | tf_op jit(solution)/shard_map/ppermute | solution.py:22
  29.6 7.1 %collective-permute-start.5 = (bf16[8,64,128]{2,1,0:T(8,128)(2,1)S(1)}, bf16[8,64,128]{2,1,0:T(8,128)(2,1)S(1)}, u32[]{:S(2)}, u32[]{:S(2)}) collective-permute-start(bf16[8,64,128]{2,1,0:T(8,128)(2,1)S(1)} %get-tuple-element.36), channel_id=1, source_target_pairs={{1,0},{2,1},{3,2},{4,3},{5,4},{6,5},{7,6},{8,7},{9,8},{10,9},{11,1... | collective-permute-start | bytes 393224 | tf_op jit(solution)/shard_map/ppermute | solution.py:24
  39.1 6.0 %collective-permute-start.6 = (f32[8,3,64]{2,0,1:T(8,128)S(1)}, f32[8,3,64]{2,0,1:T(8,128)S(1)}, u32[]{:S(2)}, u32[]{:S(2)}) collective-permute-start(f32[8,3,64]{2,0,1:T(8,128)S(1)} %get-tuple-element.63), channel_id=1, source_target_pairs={{0,1},{1,2},{2,3},{3,4},{4,5},{5,6},{6,7},{7,8},{8,9},{9,10},{10,1... | collective-permute-start | bytes 18440 | tf_op jit(solution)/shard_map/ppermute | solution.py:22
  39.1 6.2 %collective-permute-start.7 = (f32[8,3,64]{2,0,1:T(8,128)S(1)}, f32[8,3,64]{2,0,1:T(8,128)S(1)}, u32[]{:S(2)}, u32[]{:S(2)}) collective-permute-start(f32[8,3,64]{2,0,1:T(8,128)S(1)} %get-tuple-element.64), channel_id=1, source_target_pairs={{1,0},{2,1},{3,2},{4,3},{5,4},{6,5},{7,6},{8,7},{9,8},{10,9},{11,1... | collective-permute-start | bytes 18440 | tf_op jit(solution)/shard_map/ppermute | solution.py:24
  60.1 7.1 %collective-permute-start.8 = (bf16[8,64,128]{2,1,0:T(8,128)(2,1)S(1)}, bf16[8,64,128]{2,1,0:T(8,128)(2,1)S(1)}, u32[]{:S(2)}, u32[]{:S(2)}) collective-permute-start(bf16[8,64,128]{2,1,0:T(8,128)(2,1)S(1)} %get-tuple-element.31), channel_id=1, source_target_pairs={{0,1},{1,2},{2,3},{3,4},{4,5},{5,6},{6,7},{7,8},{8,9},{9,10},{10,1... | collective-permute-start | bytes 393224 | tf_op jit(solution)/shard_map/ppermute | solution.py:22
  60.2 7.1 %collective-permute-start.9 = (bf16[8,64,128]{2,1,0:T(8,128)(2,1)S(1)}, bf16[8,64,128]{2,1,0:T(8,128)(2,1)S(1)}, u32[]{:S(2)}, u32[]{:S(2)}) collective-permute-start(bf16[8,64,128]{2,1,0:T(8,128)(2,1)S(1)} %get-tuple-element.32), channel_id=1, source_target_pairs={{1,0},{2,1},{3,2},{4,3},{5,4},{6,5},{7,6},{8,7},{9,8},{10,9},{11,1... | collective-permute-start | bytes 393224 | tf_op jit(solution)/shard_map/ppermute | solution.py:24
  103.7 5.9 %collective-permute-start.10 = (f32[8,3,64]{2,0,1:T(8,128)S(1)}, f32[8,3,64]{2,0,1:T(8,128)S(1)}, u32[]{:S(2)}, u32[]{:S(2)}) collective-permute-start(f32[8,3,64]{2,0,1:T(8,128)S(1)} %get-tuple-element.61), channel_id=1, source_target_pairs={{0,1},{1,2},{2,3},{3,4},{4,5},{5,6},{6,7},{7,8},{8,9},{9,10},{10,1... | collective-permute-start | bytes 18440 | tf_op jit(solution)/shard_map/ppermute | solution.py:22
  103.8 5.8 %collective-permute-start.11 = (f32[8,3,64]{2,0,1:T(8,128)S(1)}, f32[8,3,64]{2,0,1:T(8,128)S(1)}, u32[]{:S(2)}, u32[]{:S(2)}) collective-permute-start(f32[8,3,64]{2,0,1:T(8,128)S(1)} %get-tuple-element.62), channel_id=1, source_target_pairs={{1,0},{2,1},{3,2},{4,3},{5,4},{6,5},{7,6},{8,7},{9,8},{10,9},{11,1... | collective-permute-start | bytes 18440 | tf_op jit(solution)/shard_map/ppermute | solution.py:24
  124.4 7.1 %collective-permute-start.12 = (bf16[8,64,128]{2,1,0:T(8,128)(2,1)S(1)}, bf16[8,64,128]{2,1,0:T(8,128)(2,1)S(1)}, u32[]{:S(2)}, u32[]{:S(2)}) collective-permute-start(bf16[8,64,128]{2,1,0:T(8,128)(2,1)S(1)} %get-tuple-element.27), channel_id=1, source_target_pairs={{0,1},{1,2},{2,3},{3,4},{4,5},{5,6},{6,7},{7,8},{8,9},{9,10},{10,1... | collective-permute-start | bytes 393224 | tf_op jit(solution)/shard_map/ppermute | solution.py:22
  124.5 7.1 %collective-permute-start.13 = (bf16[8,64,128]{2,1,0:T(8,128)(2,1)S(1)}, bf16[8,64,128]{2,1,0:T(8,128)(2,1)S(1)}, u32[]{:S(2)}, u32[]{:S(2)}) collective-permute-start(bf16[8,64,128]{2,1,0:T(8,128)(2,1)S(1)} %get-tuple-element.28), channel_id=1, source_target_pairs={{1,0},{2,1},{3,2},{4,3},{5,4},{6,5},{7,6},{8,7},{9,8},{10,9},{11,1... | collective-permute-start | bytes 393224 | tf_op jit(solution)/shard_map/ppermute | solution.py:24
  168.1 5.9 %collective-permute-start.14 = (f32[8,3,64]{2,0,1:T(8,128)S(1)}, f32[8,3,64]{2,0,1:T(8,128)S(1)}, u32[]{:S(2)}, u32[]{:S(2)}) collective-permute-start(f32[8,3,64]{2,0,1:T(8,128)S(1)} %get-tuple-element.59), channel_id=1, source_target_pairs={{0,1},{1,2},{2,3},{3,4},{4,5},{5,6},{6,7},{7,8},{8,9},{9,10},{10,1... | collective-permute-start | bytes 18440 | tf_op jit(solution)/shard_map/ppermute | solution.py:22
  168.1 5.8 %collective-permute-start.15 = (f32[8,3,64]{2,0,1:T(8,128)S(1)}, f32[8,3,64]{2,0,1:T(8,128)S(1)}, u32[]{:S(2)}, u32[]{:S(2)}) collective-permute-start(f32[8,3,64]{2,0,1:T(8,128)S(1)} %get-tuple-element.60), channel_id=1, source_target_pairs={{1,0},{2,1},{3,2},{4,3},{5,4},{6,5},{7,6},{8,7},{9,8},{10,9},{11,1... | collective-permute-start | bytes 18440 | tf_op jit(solution)/shard_map/ppermute | solution.py:24
  188.8 7.4 %collective-permute-start.16 = (bf16[8,64,128]{2,1,0:T(8,128)(2,1)S(1)}, bf16[8,64,128]{2,1,0:T(8,128)(2,1)S(1)}, u32[]{:S(2)}, u32[]{:S(2)}) collective-permute-start(bf16[8,64,128]{2,1,0:T(8,128)(2,1)S(1)} %get-tuple-element.23), channel_id=1, source_target_pairs={{0,1},{1,2},{2,3},{3,4},{4,5},{5,6},{6,7},{7,8},{8,9},{9,10},{10,1... | collective-permute-start | bytes 393224 | tf_op jit(solution)/shard_map/ppermute | solution.py:22
  189.1 7.1 %collective-permute-start.17 = (bf16[8,64,128]{2,1,0:T(8,128)(2,1)S(1)}, bf16[8,64,128]{2,1,0:T(8,128)(2,1)S(1)}, u32[]{:S(2)}, u32[]{:S(2)}) collective-permute-start(bf16[8,64,128]{2,1,0:T(8,128)(2,1)S(1)} %get-tuple-element.24), channel_id=1, source_target_pairs={{1,0},{2,1},{3,2},{4,3},{5,4},{6,5},{7,6},{8,7},{9,8},{10,9},{11,1... | collective-permute-start | bytes 393224 | tf_op jit(solution)/shard_map/ppermute | solution.py:24
  196.3 41.0 %copy-start.11 = (s32[8]{0:T(128)S(1)}, s32[8]{0:T(128)}, u32[]{:S(2)}) copy-start(s32[8]{0:T(128)} %param.24) | copy-start | bytes 100
  196.3 41.0 %copy-start.12 = (s32[8]{0:T(128)S(1)}, s32[8]{0:T(128)}, u32[]{:S(2)}) copy-start(s32[8]{0:T(128)} %param.25) | copy-start | bytes 100
  232.8 5.9 %collective-permute-start.18 = (f32[8,3,64]{2,0,1:T(8,128)S(1)}, f32[8,3,64]{2,0,1:T(8,128)S(1)}, u32[]{:S(2)}, u32[]{:S(2)}) collective-permute-start(f32[8,3,64]{2,0,1:T(8,128)S(1)} %get-tuple-element.57), channel_id=1, source_target_pairs={{0,1},{1,2},{2,3},{3,4},{4,5},{5,6},{6,7},{7,8},{8,9},{9,10},{10,1... | collective-permute-start | bytes 18440 | tf_op jit(solution)/shard_map/ppermute | solution.py:22
  232.9 5.8 %collective-permute-start.19 = (f32[8,3,64]{2,0,1:T(8,128)S(1)}, f32[8,3,64]{2,0,1:T(8,128)S(1)}, u32[]{:S(2)}, u32[]{:S(2)}) collective-permute-start(f32[8,3,64]{2,0,1:T(8,128)S(1)} %get-tuple-element.58), channel_id=1, source_target_pairs={{1,0},{2,1},{3,2},{4,3},{5,4},{6,5},{7,6},{8,7},{9,8},{10,9},{11,1... | collective-permute-start | bytes 18440 | tf_op jit(solution)/shard_map/ppermute | solution.py:24
  253.5 7.1 %collective-permute-start.20 = (bf16[8,64,128]{2,1,0:T(8,128)(2,1)S(1)}, bf16[8,64,128]{2,1,0:T(8,128)(2,1)S(1)}, u32[]{:S(2)}, u32[]{:S(2)}) collective-permute-start(bf16[8,64,128]{2,1,0:T(8,128)(2,1)S(1)} %get-tuple-element.19), channel_id=1, source_target_pairs={{0,1},{1,2},{2,3},{3,4},{4,5},{5,6},{6,7},{7,8},{8,9},{9,10},{10,1... | collective-permute-start | bytes 393224 | tf_op jit(solution)/shard_map/ppermute | solution.py:22
  253.6 7.1 %collective-permute-start.21 = (bf16[8,64,128]{2,1,0:T(8,128)(2,1)S(1)}, bf16[8,64,128]{2,1,0:T(8,128)(2,1)S(1)}, u32[]{:S(2)}, u32[]{:S(2)}) collective-permute-start(bf16[8,64,128]{2,1,0:T(8,128)(2,1)S(1)} %get-tuple-element.20), channel_id=1, source_target_pairs={{1,0},{2,1},{3,2},{4,3},{5,4},{6,5},{7,6},{8,7},{9,8},{10,9},{11,1... | collective-permute-start | bytes 393224 | tf_op jit(solution)/shard_map/ppermute | solution.py:24
  (13 other events, 97.0 us)
where the time goes:
time: 300 us; the launch traced here: 299 us
  blocking collectives  136 us (45%)
  starting transfers between devices  51 us (17%)
  other arithmetic  46 us (15%)
  matrix products  39.7 us (13%)
  waiting for transfers between devices  18.6 us (6%)
  local copies, waits for them, and re-layouts  6.62 us (2%)
    psum x4, blocking collectives, on_device(): lax.psum(jnp.sum(speed_entry * speed_entry, axis=(1, 2)), 'dom')  136 us
    ppermute x11, starting transfers between devices, with_halo(): lax.ppermute(head, axis, [((i + 1) % count, i) for i in range(count)])  49.8 us
    another operation x10, other arithmetic  31.5 us
    dot_general x5, matrix products, layer_one(): jnp.einsum('vyegd,ydm->vyegm', single_row_count, exchange_mate, preferred...  25.2 us
    ppermute x11, waiting for transfers between devices, with_halo(): lax.ppermute(tail, axis, [(i, (i + 1) % count) for i in range(count)])  18.3 us
    dot_general x5, matrix products, layer_two(): jnp.einsum('rcaxb,rcbf->rcaxf', rows_two, exchange_mate, preferred_elemen...  9.99 us
  transfers between devices with their start and end apart: 22, of which 10 were waited for; matrix products, arithmetic and copies ran while one was open for 4% of the time, Pallas kernels for 0%

commit v1 on v0

v1 whole, which is shorter than its diff:
```python
import functools
import math

import jax
import jax.numpy as jnp
from jax import lax
from jax.experimental import pallas as pl
from jax.experimental.pallas import tpu as pltpu
from jax.sharding import PartitionSpec as P

NA = 64
PAIR = 2 * NA
STEPS = 4

step_time = 0.05
motion_work_lower_limit = 1e-06
LOG2E = math.log2(math.e)


def dot(a, b):
    return jnp.dot(a, b, preferred_element_type=jnp.float32)


def dot_rows(a, b):
    return lax.dot_general(a, b, (((1,), (1,)), ((), ())), preferred_element_type=jnp.float32)


def pieces(value, count):
    width = value.shape[1]
    row = lax.broadcasted_iota(jnp.int32, (16, width), 0)
    tile = jnp.zeros((16, width), jnp.float32)
    for index in range(count):
        part = value.astype(jnp.bfloat16).astype(jnp.float32)
        tile = jnp.where(row == index, part, tile)
        value = value - part
    return tile.astype(jnp.bfloat16)


def swap_halves(first, second):
    low = lax.broadcasted_iota(jnp.int32, first.shape, first.ndim - 1) < NA
    return pltpu.roll(jnp.where(low, second, first), NA, first.ndim - 1)


def basis(displacement, basis_count):
    dx, dy, dz = displacement
    rest = jnp.maximum(1.0 - (dx * dx + dy * dy + dz * dz), 0.0)
    envelope = rest * rest
    vectors = [dx * envelope, dy * envelope, dz * envelope]
    span = basis_count - 1
    rate = 2.0 * span * LOG2E
    offset = 0.5 - rest
    center = jnp.exp2((-2.0 * span * span * LOG2E) * (offset * offset)) * envelope
    slope = rate * offset
    up = jnp.exp2(slope)
    down = jnp.exp2(-slope)
    up_two = up * up
    down_two = down * down
    rising = [center * up]
    falling = [center * down]
    for _ in range(basis_count // 2 - 1):
        rising.append(rising[-1] * up_two)
        falling.append(falling[-1] * down_two)
    return falling[::-1] + rising, vectors


def simulate(
    thermal_ref,
    x_ref,
    v_ref,
    feat_ref,
    first_ref,
    filter_ref,
    scale_one_ref,
    mix_ref,
    later_ref,
    scale_two_ref,
    push_ref,
    x_out,
    v_out,
    g_out,
    table,
    h_rows,
    e_rows,
    radial_0,
    radial_1,
    vec_rows,
    w_rows,
    u_rows,
    f_rows,
    v_rows,
    g_rows,
):
    atoms = x_ref.shape[1]
    pairs = atoms // PAIR
    cells = float(atoms // NA)
    basis_count = filter_ref.shape[0]
    channels = filter_ref.shape[1]
    lane = lax.broadcasted_iota(jnp.int32, (1, PAIR), 1)
    low = lane < NA
    sub = lax.broadcasted_iota(jnp.int32, (8, PAIR), 0)
    z_only = (sub == 2).astype(jnp.float32)

    def make_table(q, _):
        rows = dot(feat_ref[pl.ds(q * PAIR, PAIR), :], first_ref[...]).astype(jnp.bfloat16)
        table[pl.ds(NA + q * PAIR, PAIR), :] = rows
        return 0

    lax.fori_loop(0, pairs, make_table, 0, unroll=2)
    table[0:NA, :] = table[atoms : atoms + NA, :]
    table[atoms + NA : atoms + PAIR, :] = table[NA:PAIR, :]
    push = push_ref[...]
    push_one = pieces(push * scale_one_ref[...], 2)
    push_two = pieces(
        jnp.sum(dot_rows(pieces(push * scale_two_ref[...], 3), later_ref[...]), axis=0, keepdims=True), 2
    )

    def make_w(q, _):
        w = dot_rows(push_one, table[pl.ds(NA + q * PAIR, PAIR), :])
        w_rows[q] = jnp.broadcast_to(w[0:1] + w[1:2], (8, PAIR))
        return 0

    lax.fori_loop(0, pairs, make_w, 0, unroll=2)
    span = basis_count - 1
    order = lax.broadcasted_iota(jnp.int32, (basis_count, 1), 0).astype(jnp.float32) - 0.5 * span
    filters = filter_ref[...] * jnp.exp(-2.0 * order * order)
    scale_square = scale_one_ref[...] * scale_one_ref[...]

    zero_rows = jnp.zeros((5, PAIR), jnp.float32)

    def load(q, _):
        at = pl.ds(q * PAIR, PAIR)
        h_rows[q + 1] = jnp.concatenate([x_ref[:, at], zero_rows], axis=0)
        v_rows[q] = jnp.concatenate([v_ref[:, at], zero_rows], axis=0)
        return 0

    for q in range(pairs):
        at = slice(q * PAIR, (q + 1) * PAIR)
        h_rows[q + 1] = jnp.concatenate([x_ref[:, at], zero_rows], axis=0)
        v_rows[q] = jnp.concatenate([v_ref[:, at], zero_rows], axis=0)
    g_rows[...] = jnp.zeros(g_rows.shape, jnp.float32)

    def make_rows(q, radial):
        columns = jnp.transpose(h_rows[q + 1])
        before = e_rows[q]
        after = e_rows[q + 1]
        across = jnp.where(low, after, before)
        for chunk in range(NA // 16):
            start = chunk * 16
            own_a = [columns[start : start + 16, c : c + 1] for c in range(3)]
            own_b = [columns[NA + start : NA + start + 16, c : c + 1] for c in range(3)]
            own_a = [jnp.broadcast_to(o, (16, PAIR)) for o in own_a]
            own_b = [jnp.broadcast_to(o, (16, PAIR)) for o in own_b]
            blocks = (
                ([before[c : c + 1] - own_a[c] for c in range(3)], ((0, 0),)),
                ([across[c : c + 1] - jnp.where(low, own_a[c], own_b[c]) for c in range(3)], ((0, 1), (1, 0))),
                ([after[c : c + 1] - own_b[c] for c in range(3)], ((1, 1),)),
            )
            for displacement, places in blocks:
                radials, vectors = basis(displacement, basis_count)
                for index, value in enumerate(radials):
                    value = value.astype(jnp.bfloat16)
                    for own, half in places:
                        radial[
                            own, index * NA + start : index * NA + start + 16, half * PAIR : (half + 1) * PAIR
                        ] = value
                for c, value in enumerate(vectors):
                    value = value.astype(jnp.bfloat16)
                    for own, half in places:
                        at = c * PAIR + own * NA + start
                        vec_rows[q, at : at + 16, half * PAIR : (half + 1) * PAIR] = value

    blank = jnp.zeros((NA, channels), jnp.bfloat16)

    def use_rows(q, radial):
        near = table[pl.ds(pl.multiple_of(q * PAIR, PAIR), 2 * PAIR), :]
        signals = (
            jnp.concatenate([near[: 3 * NA], blank], axis=0),
            jnp.concatenate([blank, near[NA:]], axis=0),
        )
        scalars, norms = [], []
        for own in range(2):
            vectors = jnp.concatenate(
                [vec_rows[q, c * PAIR + own * NA : c * PAIR + own * NA + NA, :] for c in range(3)], axis=0
            )
            vectors = dot(vectors, signals[own])
            norm = vectors[:NA] * vectors[:NA]
            for c in range(1, 3):
                part = vectors[c * NA : (c + 1) * NA]
                norm = norm + part * part
            norms.append((norm * scale_square).astype(jnp.bfloat16))
            sums = dot(radial[own], signals[own])
            scalar = sums[:NA] * filters[0:1]
            for k in range(1, basis_count):
                scalar = scalar + sums[k * NA : (k + 1) * NA] * filters[k : k + 1]
            scalars.append(scalar.astype(jnp.bfloat16))
        messages = jnp.concatenate(
            [jnp.concatenate(scalars, axis=0), jnp.concatenate(norms, axis=0)], axis=1
        )
        half = 0.5 * dot(messages, mix_ref[...])
        own_features = feat_ref[pl.ds(pl.multiple_of(q * PAIR, PAIR), PAIR), :].astype(jnp.float32)
        hidden = (own_features + (half + half * jnp.tanh(half))).astype(jnp.bfloat16)
        u = dot_rows(push_two, hidden)
        u_rows[q + 1] = jnp.broadcast_to(u[0:1] + u[1:2], (8, PAIR)) + w_rows[q]

    row16 = lax.broadcasted_iota(jnp.int32, (16, 2 * PAIR), 0)

    def make_force(q, _):
        before = swap_halves(u_rows[q], u_rows[q + 1])
        after = swap_halves(u_rows[q + 1], u_rows[q + 2])
        first = jnp.concatenate([before, jnp.where(low, after, 0.0)], axis=1)
        second = jnp.concatenate([jnp.where(low, 0.0, before), after], axis=1)
        first = jnp.concatenate([first, first], axis=0)
        second = jnp.concatenate([second, second], axis=0)
        value = jnp.where(row16 < 8, first, second)
        high = value.astype(jnp.bfloat16).astype(jnp.float32)
        value = jnp.where((row16 & 7) == 0, high, jnp.where((row16 & 7) == 1, value - high, 0.0))
        sums = dot_rows(value.astype(jnp.bfloat16), vec_rows[q])
        tile = jnp.zeros((8, PAIR), jnp.float32)
        for c in range(3):
            part = sums[:, c * PAIR : (c + 1) * PAIR]
            part = jnp.sum(jnp.where(low, part[:8], part[8:]), axis=0, keepdims=True)
            tile = jnp.where(sub == c, part, tile)
        f_rows[q] = tile
        return 0

    def step(n, _):
        dt = jnp.where(n == 0, 0.0, step_time).astype(jnp.float32)
        h = v_rows[...] + (0.5 * dt) * g_rows[...]
        v_rows[...] = h
        h_rows[1 : pairs + 1] = h_rows[1 : pairs + 1] + dt * h
        h_rows[0] = h_rows[pairs] - cells * z_only
        h_rows[pairs + 1] = h_rows[1] + cells * z_only

        def shift(q, _):
            e_rows[q] = swap_halves(h_rows[q], h_rows[q + 1])
            return 0

        lax.fori_loop(0, pairs + 1, shift, 0)
        make_rows(0, radial_0)

        def two(i, _):
            q = 2 * i
            use_rows(q, radial_0)
            make_rows(q + 1, radial_1)
            use_rows(q + 1, radial_1)
            make_rows(jnp.minimum(q + 2, pairs - 1), radial_0)
            return 0

        lax.fori_loop(0, pairs // 2, two, 0)
        u_rows[0] = u_rows[pairs]
        u_rows[pairs + 1] = u_rows[1]
        lax.fori_loop(0, pairs, make_force, 0, unroll=2)
        g = f_rows[...]
        g_rows[...] = g
        v = v_rows[...] + (0.5 * dt) * g
        kinetic = jnp.sum(v * v, axis=0)
        kinetic = jnp.sum(jnp.sum(kinetic, axis=1, keepdims=True), axis=0, keepdims=True)
        stretch = jnp.sqrt(thermal_ref[0, 0] / (kinetic / (3.0 * atoms) + motion_work_lower_limit))
        stretch = jnp.where(n == 0, 1.0, stretch)
        v_rows[...] = v * stretch
        return 0

    lax.fori_loop(0, STEPS + 1, step, 0)
    for q in range(pairs):
        at = slice(q * PAIR, (q + 1) * PAIR)
        x_out[:, at] = h_rows[q + 1, 0:3, :]
        v_out[:, at] = v_rows[q, 0:3, :]
        g_out[:, at] = g_rows[q, 0:3, :]


def run_replica(thermal, x, v, features, weights):
    atoms = x.shape[1]
    channels = features.shape[1]
    pairs = atoms // PAIR
    basis_count = weights[1].shape[0]
    out = jax.ShapeDtypeStruct((3, atoms), jnp.float32)
    vmem = pl.BlockSpec(memory_space=pltpu.VMEM)
    tiles = pltpu.VMEM((pairs, 8, PAIR), jnp.float32)
    tiles_two = pltpu.VMEM((pairs + 2, 8, PAIR), jnp.float32)
    radial = pltpu.VMEM((2, basis_count * NA, 2 * PAIR), jnp.bfloat16)
    return pl.pallas_call(
        simulate,
        out_shape=(out, out, out),
        in_specs=[pl.BlockSpec(memory_space=pltpu.SMEM)] + [vmem] * 10,
        out_specs=(vmem, vmem, vmem),
        scratch_shapes=[
            pltpu.VMEM((atoms + PAIR, channels), jnp.bfloat16),
            tiles_two,
            tiles_two,
            radial,
            radial,
            pltpu.VMEM((pairs, 3 * PAIR, 2 * PAIR), jnp.bfloat16),
            tiles,
            tiles_two,
            tiles,
            tiles,
            tiles,
        ],
        compiler_params=pltpu.CompilerParams(vmem_limit_bytes=50 * 1024 * 1024),
    )(thermal, x, v, features, *weights)


def on_device(
    particle_places,
    particle_speeds,
    thermal_targets,
    element_features,
    swap_counterpart_slot,
    swap_approval_flags,
    initial_signal_projector,
    initial_distance_filter,
    initial_directional_scales,
    invariant_revision_matrix,
    magnitude_revision_matrix,
    later_signal_projector,
    later_directional_scales,
    push_output_matrix,
):
    replicas = particle_places.shape[0]
    local_atoms = particle_places.shape[2]
    local_cells = local_atoms // NA
    devices = lax.axis_size("dom")
    own = lax.axis_index("dom")
    per_replica = devices // replicas
    bits = devices.bit_length() - 1
    replica_bits = replicas.bit_length() - 1

    def trade(value, mask):
        return lax.ppermute(value, "dom", [(i, i ^ mask) for i in range(devices)])

    state = jnp.concatenate([particle_places, particle_speeds], axis=1)
    features = element_features
    for level in range(bits):
        mask = devices >> (level + 1)
        upper = (own & mask) > 0
        if level < replica_bits:
            half = state.shape[0] // 2
            keep = jnp.where(upper, state[half:], state[:half])
            send = jnp.where(upper, state[:half], state[half:])
        else:
            keep = send = state
        got = trade(send, mask)
        got_features = trade(features, mask)
        axis = 1 + level
        state = jnp.stack([jnp.where(upper, got, keep), jnp.where(upper, keep, got)], axis=axis)
        features = jnp.stack(
            [jnp.where(upper, got_features, features), jnp.where(upper, features, got_features)], axis=level
        )
        if level + 1 < bits:
            state, features = lax.optimization_barrier((state, features))
    state = state.reshape(devices, 6, local_atoms).transpose(1, 0, 2).reshape(6, devices * local_atoms)
    features = features.reshape(devices * local_atoms, -1)
    thermal = lax.dynamic_slice(thermal_targets, (own // per_replica,), (1,)).reshape(1, 1)
    weights = (
        initial_signal_projector,
        initial_distance_filter,
        initial_directional_scales[None],
        jnp.concatenate([invariant_revision_matrix, magnitude_revision_matrix], axis=0),
        later_signal_projector,
        later_directional_scales[None],
        push_output_matrix[None],
    )
    x, v, g = run_replica(thermal, state[:3], state[3:], features, weights)

    state = jnp.concatenate([x, v, g], axis=0).reshape(9, replicas, per_replica, local_atoms)
    state = lax.dynamic_index_in_dim(state, own % per_replica, 2, keepdims=False)
    state = state.transpose(1, 0, 2)[:, None]
    for level in range(replica_bits):
        mask = devices >> (level + 1)
        upper = (own & mask) > 0
        half = state.shape[0] // 2
        keep = jnp.where(upper, state[half:], state[:half])
        send = jnp.where(upper, state[:half], state[half:])
        got = trade(send, mask)
        state = jnp.stack([jnp.where(upper, got, keep), jnp.where(upper, keep, got)], axis=1 + level)
    state = state.reshape(replicas, 3, 3, local_atoms)

    ladder_slot = jnp.arange(replicas, dtype=jnp.int32)
    source = jnp.where(swap_approval_flags > 0, swap_counterpart_slot, ladder_slot)
    chosen = source[:, None] == ladder_slot[None, :]
    state = jnp.sum(jnp.where(chosen[:, :, None, None, None], state[None], 0.0), axis=1)
    thermal_source = jnp.sum(jnp.where(chosen, thermal_targets[None, :], 0.0), axis=1)
    thermal_ratio = jnp.sqrt(thermal_targets / thermal_source)
    atom_cell = (own * local_cells + jnp.arange(local_atoms, dtype=jnp.int32) // NA).astype(jnp.float32)
    cell_floor = jnp.array([0.0, 0.0, 1.0], jnp.float32)[:, None] * atom_cell[None, :]
    return (
        state[:, 0] - cell_floor[None],
        state[:, 1] * thermal_ratio[:, None, None],
        state[:, 2],
    )


def solution(mesh):
    return jax.shard_map(
        on_device,
        mesh=mesh,
        in_specs=(
            P("groups", None, "dom"),
            P("groups", None, "dom"),
            P("groups"),
            P(("groups", "dom"), None),
            P("groups"),
            P("groups"),
            P(),
            P(),
            P(),
            P(),
            P(),
            P(),
            P(),
            P(),
        ),
        out_specs=(P("groups", None, "dom"), P("groups", None, "dom"), P("groups", None, "dom")),
        check_vma=False,
    )
```

time: 300 us -> 153 us (0.51)
  blocking collectives: 136 us -> 0 us
  Pallas kernels: 0 us -> 107 us
  other arithmetic: 46 us -> 1.59 us
  matrix products: 39.7 us -> 0 us
  starting transfers between devices: 51 us -> 11.6 us
  waiting for transfers between devices: 18.6 us -> 25.3 us
    psum x4 -> x0, blocking collectives: 136 us -> none  [on_device(): lax.psum(jnp.sum(speed_entry * speed_entry, axis=(1, 2)), 'dom')]
    pallas_call x0 -> x1, Pallas kernels: none -> 107 us  [run_replica(): pl.pallas_call(simulate, out_shape=(out, out, out), in_specs=[pl.BlockSpe...]
    dot_general x26 -> x0, matrix products: 39.7 us -> none  [the longest x5 25.2 us: layer_one(): jnp.einsum('vyegd,ydm->vyegm', single_row_count, exchange_mate, preferred...]
    ppermute x22 -> x11, starting transfers between devices: 51 us -> 11.6 us  [trade(): return lax.ppermute(value, 'dom', [(i, i ^ mask) for i in range(devices)])]
    another operation x10 -> x18, other arithmetic: 31.5 us -> 0.55 us  [the longest x10 0.29 us: on_device(): jnp.stack([jnp.where(upper, got, keep), jnp.where(upper, keep, got)], axi...]
    reduce_sum x21 -> x2, other arithmetic: 10.1 us -> 0.44 us  [the longest x1 0.26 us: on_device(): jnp.sum(jnp.where(chosen[:, :, None, None, None], state[None], 0.0), axis=1)]
    ppermute x22 -> x11, waiting for transfers between devices: 18.6 us -> 25.3 us  [trade(): return lax.ppermute(value, 'dom', [(i, i ^ mask) for i in range(devices)])]
  transfers between devices with their start and end apart: 22 -> 11, of which waited for: 10 -> 10; matrix products, arithmetic and copies ran while one was open for 4% -> 1% of each run, Pallas kernels for 0% -> 0%
where the time goes in v1:
time: 153 us
  Pallas kernels  107 us (70%)
  waiting for transfers between devices  25.3 us (17%)
  starting transfers between devices  11.6 us (8%)
  local copies, waits for them, and re-layouts  5.97 us (4%)
  other arithmetic  1.59 us (1%)
    pallas_call x1, Pallas kernels, run_replica(): pl.pallas_call(simulate, out_shape=(out, out, out), in_specs=[pl.BlockSpe...  107 us
    ppermute x11, waiting for transfers between devices, trade(): return lax.ppermute(value, 'dom', [(i, i ^ mask) for i in range(devices)])  25.3 us
    ppermute x11, starting transfers between devices, trade(): return lax.ppermute(value, 'dom', [(i, i ^ mask) for i in range(devices)])  11.6 us
    unnamed x33, local copies, waits for them, and re-layouts  4.59 us
  transfers between devices with their start and end apart: 11, of which 10 were waited for; matrix products, arithmetic and copies ran while one was open for 1% of the time, Pallas kernels for 0%

profile of v1, /device:TPU:0, one launch (start us, length us, event | category | flops | bytes accessed | tf_op | source)
XLA Modules:
  0.0 152.6 jit_solution(10164293852613847985)
XLA Ops:
  0.6 0.7 constant_dynamic-update-slice_fusion.1
  1.4 4.1 %collective-permute-start = (f32[4,6,192]{2,0,1:T(4,128)S(1)}, f32[4,6,192]{2,0,1:T(4,128)S(1)}, u32[]{:S(2)}, u32[]{:S(2)}) collective-permute-start(f32[4,6,192]{2,0,1:T(4,128)S(1)} %slice_select_fusion.2), channel_id=1, source_target_pairs={{0,8},{1,9},{2,10},{3,11},{4,12},{5,13},{6,14},{7,15},{8,0},{9,1},... | collective-permute-start | bytes 55304 | tf_op jit(solution)/shard_map/ppermute | solution.py:329
  5.5 0.7 collective-permute-start.1
  6.2 1.1 collective-permute-done
  7.4 3.3 %collective-permute-done.1 = bf16[192,128]{1,0:T(8,128)(2,1)S(1)} collective-permute-done((bf16[192,128]{1,0:T(8,128)(2,1)S(1)}, bf16[192,128]{1,0:T(8,128)(2,1)S(1)}, u32[]{:S(2)}, u32[]{:S(2)}) %collective-permute-start.1) | collective-permute-done | bytes 49184 | tf_op jit(solution)/shard_map/ppermute | solution.py:329
  10.7 1.5 collective-permute-start.2
  12.9 1.7 %collective-permute-done.2 = f32[2,2,6,192]{3,0,2,1:T(2,128)S(1)} collective-permute-done((f32[2,2,6,192]{3,0,2,1:T(2,128)S(1)}, f32[2,2,6,192]{3,0,2,1:T(2,128)S(1)}, u32[]{:S(2)}, u32[]{:S(2)}) %collective-permute-start.2) | collective-permute-done | bytes 18464 | tf_op jit(solution)/shard_map/ppermute | solution.py:329
  14.7 2.3 %collective-permute-done.3 = bf16[2,192,128]{2,1,0:T(8,128)(2,1)S(1)} collective-permute-done((bf16[2,192,128]{2,1,0:T(8,128)(2,1)S(1)}, bf16[2,192,128]{2,1,0:T(8,128)(2,1)S(1)}, u32[]{:S(2)}, u32[]{:S(2)}) %collective-permute-start.3) | collective-permute-done | bytes 98336 | tf_op jit(solution)/shard_map/ppermute | solution.py:329
  17.0 1.6 %collective-permute-start.4 = (f32[1,2,2,6,192]{4,0,3,1,2:T(1,128)S(1)}, f32[1,2,2,6,192]{4,0,3,1,2:T(1,128)S(1)}, u32[]{:S(2)}, u32[]{:S(2)}) collective-permute-start(f32[1,2,2,6,192]{4,0,3,1,2:T(1,128)S(1)} %broadcast_select_fusion.7), channel_id=1, source_target_pairs={{0,2},{1,3},{2,0},{3,1},{4,6},{5,7},{6,4},{7,5},{8,10},{9,11},{10,... | collective-permute-start | bytes 55304 | tf_op jit(solution)/shard_map/ppermute | solution.py:329
  19.2 1.7 %collective-permute-done.4 = f32[1,2,2,6,192]{4,0,3,1,2:T(1,128)S(1)} collective-permute-done((f32[1,2,2,6,192]{4,0,3,1,2:T(1,128)S(1)}, f32[1,2,2,6,192]{4,0,3,1,2:T(1,128)S(1)}, u32[]{:S(2)}, u32[]{:S(2)}) %collective-permute-start.4) | collective-permute-done | bytes 18464 | tf_op jit(solution)/shard_map/ppermute | solution.py:329
  21.0 3.3 %collective-permute-done.5 = bf16[2,2,192,128]{3,2,0,1:T(8,128)(2,1)S(1)} collective-permute-done((bf16[2,2,192,128]{3,2,0,1:T(8,128)(2,1)S(1)}, bf16[2,2,192,128]{3,2,0,1:T(8,128)(2,1)S(1)}, u32[]{:S(2)}, u32[]{:S(2)}) %collective-permute-start.5) | collective-permute-done | bytes 196640 | tf_op jit(solution)/shard_map/ppermute | solution.py:329
  24.6 0.6 copy-done.7
  25.2 0.6 copy-done.13
  25.9 0.6 dynamic_slice.7
  26.9 1.2 collective-permute-done.7
  28.4 0.6 copy-done
  29.1 107.1 %shard_map.166 = (f32[3,3072]{1,0:T(4,128)S(1)}, f32[3,3072]{1,0:T(4,128)S(1)}, f32[3,3072]{1,0:T(4,128)S(1)}) custom-call(f32[1,1]{1,0:T(1,128)} %bitcast.thermal_ref, f32[3,3072]{1,0:T(4,128)S(1)} %slice.78.x_ref, f32[3,3072]{1,0:T(4,128)S(1)} %slice.80.v_ref, bf16[3072,128]{1,0:T(8,128)(2,1)S(1)} %bitcast.80, bf16[128,128]{1,0:T(8,128)(2,1)S(1)} %copy-done, ...), custom_call_target="tpu_custom_call" | custom-call | tf_op jit(solution)/shard_map/pallas_call | solution.py:281
  136.6 1.6 %collective-permute-start.8 = (f32[4,1,9,192]{3,0,2,1:T(4,128)S(1)}, f32[4,1,9,192]{3,0,2,1:T(4,128)S(1)}, u32[]{:S(2)}, u32[]{:S(2)}) collective-permute-start(f32[4,1,9,192]{3,0,2,1:T(4,128)S(1)} %select_bitcast_fusion.12), channel_id=1, source_target_pairs={{0,8},{1,9},{2,10},{3,11},{4,12},{5,13},{6,14},{7,15},{8,0},{9,1},... | collective-permute-start | bytes 82952 | tf_op jit(solution)/shard_map/ppermute | solution.py:329
  138.3 3.6 %collective-permute-done.8 = f32[4,1,9,192]{3,0,2,1:T(4,128)S(1)} collective-permute-done((f32[4,1,9,192]{3,0,2,1:T(4,128)S(1)}, f32[4,1,9,192]{3,0,2,1:T(4,128)S(1)}, u32[]{:S(2)}, u32[]{:S(2)}) %collective-permute-start.8) | collective-permute-done | bytes 27680 | tf_op jit(solution)/shard_map/ppermute | solution.py:329
  142.4 3.6 %collective-permute-done.9 = f32[2,2,1,9,192]{4,0,3,2,1:T(2,128)S(1)} collective-permute-done((f32[2,2,1,9,192]{4,0,3,2,1:T(2,128)S(1)}, f32[2,2,1,9,192]{4,0,3,2,1:T(2,128)S(1)}, u32[]{:S(2)}, u32[]{:S(2)}) %collective-permute-start.9) | collective-permute-done | bytes 27680 | tf_op jit(solution)/shard_map/ppermute | solution.py:329
  146.7 3.4 %collective-permute-done.10 = f32[1,2,2,1,9,192]{5,0,4,1,3,2:T(1,128)S(1)} collective-permute-done((f32[1,2,2,1,9,192]{5,0,4,1,3,2:T(1,128)S(1)}, f32[1,2,2,1,9,192]{5,0,4,1,3,2:T(1,128)S(1)}, u32[]{:S(2)}, u32[]{:S(2)}) %collective-permute-start.10) | collective-permute-done | bytes 27680 | tf_op jit(solution)/shard_map/ppermute | solution.py:329
  150.8 0.6 copy.103
  151.4 0.6 copy.104
  152.0 0.6 copy.105
  (84 shorter events, 4.6 us)
Async XLA Ops:
  0.6 0.8 copy-start.9
  1.4 4.1 %copy-start.6 = (bf16[192,128]{1,0:T(8,128)(2,1)S(1)}, bf16[192,128]{1,0:T(8,128)(2,1)}, u32[]{:S(2)}) copy-start(bf16[192,128]{1,0:T(8,128)(2,1)} %param.18) | copy-start | bytes 147460
  1.4 5.9 %collective-permute-start = (f32[4,6,192]{2,0,1:T(4,128)S(1)}, f32[4,6,192]{2,0,1:T(4,128)S(1)}, u32[]{:S(2)}, u32[]{:S(2)}) collective-permute-start(f32[4,6,192]{2,0,1:T(4,128)S(1)} %slice_select_fusion.2), channel_id=1, source_target_pairs={{0,8},{1,9},{2,10},{3,11},{4,12},{5,13},{6,14},{7,15},{8,0},{9,1},... | collective-permute-start | bytes 55304 | tf_op jit(solution)/shard_map/ppermute | solution.py:329
  5.5 5.1 %collective-permute-start.1 = (bf16[192,128]{1,0:T(8,128)(2,1)S(1)}, bf16[192,128]{1,0:T(8,128)(2,1)S(1)}, u32[]{:S(2)}, u32[]{:S(2)}) collective-permute-start(bf16[192,128]{1,0:T(8,128)(2,1)S(1)} %copy-done.6), channel_id=1, source_target_pairs={{0,8},{1,9},{2,10},{3,11},{4,12},{5,13},{6,14},{7,15},{8,0},{9,1},... | collective-permute-start | bytes 147464 | tf_op jit(solution)/shard_map/ppermute | solution.py:329
  10.7 1.6 %copy-start.10 = (f32[3]{0:T(128)S(1)}, f32[3]{0:T(128)}, u32[]{:S(2)}) copy-start(f32[3]{0:T(128)} %constant.60.clone) | copy-start | bytes 40
  10.7 3.9 %collective-permute-start.2 = (f32[2,2,6,192]{3,0,2,1:T(2,128)S(1)}, f32[2,2,6,192]{3,0,2,1:T(2,128)S(1)}, u32[]{:S(2)}, u32[]{:S(2)}) collective-permute-start(f32[2,2,6,192]{3,0,2,1:T(2,128)S(1)} %broadcast_select_fusion.11), channel_id=1, source_target_pairs={{0,4},{1,5},{2,6},{3,7},{4,0},{5,1},{6,2},{7,3},{8,12},{9,13},{10,... | collective-permute-start | bytes 55304 | tf_op jit(solution)/shard_map/ppermute | solution.py:329
  12.3 4.6 %collective-permute-start.3 = (bf16[2,192,128]{2,1,0:T(8,128)(2,1)S(1)}, bf16[2,192,128]{2,1,0:T(8,128)(2,1)S(1)}, u32[]{:S(2)}, u32[]{:S(2)}) collective-permute-start(bf16[2,192,128]{2,1,0:T(8,128)(2,1)S(1)} %pad_maximum_fusion.4), channel_id=1, source_target_pairs={{0,4},{1,5},{2,6},{3,7},{4,0},{5,1},{6,2},{7,3},{8,12},{9,13},{10,... | collective-permute-start | bytes 294920 | tf_op jit(solution)/shard_map/ppermute | solution.py:329
  17.0 1.6 %copy-start.11 = (s32[8]{0:T(128)S(1)}, s32[8]{0:T(128)}, u32[]{:S(2)}) copy-start(s32[8]{0:T(128)} %param.19) | copy-start | bytes 100
  17.0 1.6 %copy-start.12 = (s32[8]{0:T(128)S(1)}, s32[8]{0:T(128)}, u32[]{:S(2)}) copy-start(s32[8]{0:T(128)} %param.20) | copy-start | bytes 100
  17.0 3.9 %collective-permute-start.4 = (f32[1,2,2,6,192]{4,0,3,1,2:T(1,128)S(1)}, f32[1,2,2,6,192]{4,0,3,1,2:T(1,128)S(1)}, u32[]{:S(2)}, u32[]{:S(2)}) collective-permute-start(f32[1,2,2,6,192]{4,0,3,1,2:T(1,128)S(1)} %broadcast_select_fusion.7), channel_id=1, source_target_pairs={{0,2},{1,3},{2,0},{3,1},{4,6},{5,7},{6,4},{7,5},{8,10},{9,11},{10,... | collective-permute-start | bytes 55304 | tf_op jit(solution)/shard_map/ppermute | solution.py:329
  18.6 5.7 %collective-permute-start.5 = (bf16[2,2,192,128]{3,2,0,1:T(8,128)(2,1)S(1)}, bf16[2,2,192,128]{3,2,0,1:T(8,128)(2,1)S(1)}, u32[]{:S(2)}, u32[]{:S(2)}) collective-permute-start(bf16[2,2,192,128]{3,2,0,1:T(8,128)(2,1)S(1)} %pad_maximum_fusion.2), channel_id=1, source_target_pairs={{0,2},{1,3},{2,0},{3,1},{4,6},{5,7},{6,4},{7,5},{8,10},{9,11},{10,... | collective-permute-start | bytes 589832 | tf_op jit(solution)/shard_map/ppermute | solution.py:329
  24.4 0.8 copy-start.7
  24.4 0.8 copy-start.8
  24.5 2.0 %collective-permute-start.6 = (f32[1,2,2,2,6,192]{5,2,4,1,3,0:T(2,128)S(1)}, f32[1,2,2,2,6,192]{5,2,4,1,3,0:T(2,128)S(1)}, u32[]{:S(2)}, u32[]{:S(2)}) collective-permute-start(f32[1,2,2,2,6,192]{5,2,4,1,3,0:T(2,128)S(1)} %pad_maximum_fusion.10), channel_id=1, source_target_pairs={{0,1},{1,0},{2,3},{3,2},{4,5},{5,4},{6,7},{7,6},{8,9},{9,8},{10,11... | collective-permute-start | bytes 110600 | tf_op jit(solution)/shard_map/ppermute | solution.py:329
  26.4 1.7 %collective-permute-start.7 = (bf16[2,2,2,192,128]{4,3,0,1,2:T(8,128)(2,1)S(1)}, bf16[2,2,2,192,128]{4,3,0,1,2:T(8,128)(2,1)S(1)}, u32[]{:S(2)}, u32[]{:S(2)}) collective-permute-start(bf16[2,2,2,192,128]{4,3,0,1,2:T(8,128)(2,1)S(1)} %pad_maximum_fusion.1), channel_id=1, source_target_pairs={{0,1},{1,0},{2,3},{3,2},{4,5},{5,4},{6,7},{7,6},{8,9},{9,8},{10,11... | collective-permute-start | bytes 1179656 | tf_op jit(solution)/shard_map/ppermute | solution.py:329
  28.3 0.8 copy-start
  28.3 0.8 copy-start.1
  28.4 0.7 copy-start.2
  28.4 0.7 copy-start.3
  28.4 0.7 copy-start.4
  28.4 0.7 copy-start.5
  136.6 5.3 %collective-permute-start.8 = (f32[4,1,9,192]{3,0,2,1:T(4,128)S(1)}, f32[4,1,9,192]{3,0,2,1:T(4,128)S(1)}, u32[]{:S(2)}, u32[]{:S(2)}) collective-permute-start(f32[4,1,9,192]{3,0,2,1:T(4,128)S(1)} %select_bitcast_fusion.12), channel_id=1, source_target_pairs={{0,8},{1,9},{2,10},{3,11},{4,12},{5,13},{6,14},{7,15},{8,0},{9,1},... | collective-permute-start | bytes 82952 | tf_op jit(solution)/shard_map/ppermute | solution.py:329
  141.9 4.0 %collective-permute-start.9 = (f32[2,2,1,9,192]{4,0,3,2,1:T(2,128)S(1)}, f32[2,2,1,9,192]{4,0,3,2,1:T(2,128)S(1)}, u32[]{:S(2)}, u32[]{:S(2)}) collective-permute-start(f32[2,2,1,9,192]{4,0,3,2,1:T(2,128)S(1)} %broadcast_select_fusion.9), channel_id=1, source_target_pairs={{0,4},{1,5},{2,6},{3,7},{4,0},{5,1},{6,2},{7,3},{8,12},{9,13},{10,... | collective-permute-start | bytes 82952 | tf_op jit(solution)/shard_map/ppermute | solution.py:329
  146.1 4.0 %collective-permute-start.10 = (f32[1,2,2,1,9,192]{5,0,4,1,3,2:T(1,128)S(1)}, f32[1,2,2,1,9,192]{5,0,4,1,3,2:T(1,128)S(1)}, u32[]{:S(2)}, u32[]{:S(2)}) collective-permute-start(f32[1,2,2,1,9,192]{5,0,4,1,3,2:T(1,128)S(1)} %get-tuple-element.24), channel_id=1, source_target_pairs={{0,2},{1,3},{2,0},{3,1},{4,6},{5,7},{6,4},{7,5},{8,10},{9,11},{10,... | collective-permute-start | bytes 82952 | tf_op jit(solution)/shard_map/ppermute | solution.py:329
  (1 other events, 0.7 us)

commit v2 on v1

v2 whole, which is shorter than its diff:
```python
import functools
import math

import jax
import jax.numpy as jnp
from jax import lax
from jax.experimental import pallas as pl
from jax.experimental.pallas import tpu as pltpu
from jax.sharding import PartitionSpec as P

NA = 64
PAIR = 2 * NA
STEPS = 4
UNROLL = 4

step_time = 0.05
motion_work_lower_limit = 1e-06
LOG2E = math.log2(math.e)


def dot(a, b):
    return jnp.dot(a, b, preferred_element_type=jnp.float32)


def dot_rows(a, b):
    return lax.dot_general(a, b, (((1,), (1,)), ((), ())), preferred_element_type=jnp.float32)


def pieces(value, count):
    width = value.shape[1]
    row = lax.broadcasted_iota(jnp.int32, (16, width), 0)
    tile = jnp.zeros((16, width), jnp.float32)
    for index in range(count):
        part = value.astype(jnp.bfloat16).astype(jnp.float32)
        tile = jnp.where(row == index, part, tile)
        value = value - part
    return tile.astype(jnp.bfloat16)


def swap_halves(first, second):
    low = lax.broadcasted_iota(jnp.int32, first.shape, first.ndim - 1) < NA
    return pltpu.roll(jnp.where(low, second, first), NA, first.ndim - 1)


def basis(displacement, basis_count):
    dx, dy, dz = displacement
    rest = jnp.maximum(1.0 - (dx * dx + dy * dy + dz * dz), 0.0)
    envelope = rest * rest
    vectors = [dx * envelope, dy * envelope, dz * envelope]
    span = basis_count - 1
    rate = 2.0 * span * LOG2E
    offset = 0.5 - rest
    center = jnp.exp2((-2.0 * span * span * LOG2E) * (offset * offset)) * envelope
    slope = rate * offset
    up = jnp.exp2(slope)
    down = jnp.exp2(-slope)
    up_two = up * up
    down_two = down * down
    rising = [center * up]
    falling = [center * down]
    for _ in range(basis_count // 2 - 1):
        rising.append(rising[-1] * up_two)
        falling.append(falling[-1] * down_two)
    return falling[::-1] + rising, vectors


def prepare(
    place_ref,
    state_ref,
    feat_ref,
    first_ref,
    scale_one_ref,
    later_ref,
    scale_two_ref,
    push_ref,
    x_out,
    v_out,
    own_feat,
    table,
    message_push,
    later_push,
):
    extended = x_out.shape[0]
    cells = feat_ref.shape[0] // NA
    own_cells = 2 * (extended - 2)
    first_cell = place_ref[0] * own_cells - 2 + cells
    for p in range(extended):
        cell = lax.rem(first_cell + 2 * p, cells)
        at = pl.ds(pl.multiple_of(cell * NA, PAIR), PAIR)
        rows = state_ref[:, at]
        x = jnp.concatenate([rows[:3], jnp.zeros((5, PAIR), jnp.float32)], axis=0)
        if p == 0 or p == extended - 1:
            sub = lax.broadcasted_iota(jnp.int32, (8, PAIR), 0)
            wraps = (place_ref[0] == 0) if p == 0 else (place_ref[0] == place_ref[1] - 1)
            shift = jnp.where(wraps, float(cells), 0.0) * (-1.0 if p == 0 else 1.0)
            x = x + jnp.where(sub == 2, shift, 0.0)
        x_out[p] = x
        if 0 < p < extended - 1:
            v_out[p - 1] = jnp.concatenate([rows[3:6], jnp.zeros((5, PAIR), jnp.float32)], axis=0)
        own_feat[p * PAIR : (p + 1) * PAIR, :] = feat_ref[at, :]
    table[...] = dot(own_feat[...], first_ref[...]).astype(jnp.bfloat16)
    push = push_ref[...]
    message_push[...] = table[NA : NA + (extended - 1) * PAIR, :].astype(jnp.float32) * (push * scale_one_ref[...])
    parts = dot_rows(pieces(push * scale_two_ref[...], 3), later_ref[...])
    later_push[...] = jnp.broadcast_to(jnp.sum(parts, axis=0, keepdims=True), later_push.shape)


def advance(
    stage,
    place_ref,
    thermal_ref,
    x_ref,
    v_ref,
    g_ref,
    edge_ref,
    got_ref,
    own_feat,
    table,
    message_push,
    later_push,
    filter_ref,
    scale_one_ref,
    mix_ref,
    x_out,
    v_out,
    g_out,
    edge_out,
    e_rows,
    h_rows,
    lhs_0,
    lhs_1,
    vec_0,
    vec_1,
    vec_2,
    vec_3,
    message_0,
    message_1,
    forces,
):
    own_pairs = v_ref.shape[0]
    extended = own_pairs + 2
    pairs = own_pairs + 1
    total_cells = 2 * own_pairs * place_ref[1]
    basis_count = filter_ref.shape[0]
    channels = filter_ref.shape[1]
    sub = lax.broadcasted_iota(jnp.int32, (8, PAIR), 0)
    low = lax.broadcasted_iota(jnp.int32, (1, PAIR), 1) < NA
    span = basis_count - 1
    order = lax.broadcasted_iota(jnp.int32, (basis_count, 1), 0).astype(jnp.float32) - 0.5 * span
    filters = filter_ref[...] * jnp.exp(-2.0 * order * order)
    filters = jnp.concatenate([filters, filters], axis=1)
    scale_square = scale_one_ref[...] * scale_one_ref[...]
    scale_square = jnp.concatenate([scale_square, scale_square], axis=1)

    if stage == 0:
        e_rows[...] = x_ref[...]
        half_v = v_ref[...]
    else:
        if stage == 1:
            stretch = jnp.ones((1, 1), jnp.float32)
        else:
            kinetic = edge_ref[0, 1, 3:4, 0:1] + got_ref[0, 1, 3:4, 0:1]
            mean = kinetic / (3.0 * NA * total_cells.astype(jnp.float32)) + motion_work_lower_limit
            stretch = jnp.sqrt(thermal_ref[0] / mean)
        v = v_ref[...] * stretch
        half_v = v + (0.5 * step_time) * g_ref[...]
        e_rows[1 : own_pairs + 1] = x_ref[...] + step_time * v
        z_shift = jnp.where(sub == 2, total_cells.astype(jnp.float32), 0.0)
        left = got_ref[1, 0] + (step_time * stretch) * got_ref[1, 1]
        right = got_ref[0, 0] + (step_time * stretch) * got_ref[0, 1]
        e_rows[0] = jnp.where(place_ref[0] == 0, left - z_shift, left)
        e_rows[extended - 1] = jnp.where(place_ref[0] == place_ref[1] - 1, right + z_shift, right)
    h_rows[...] = swap_halves(e_rows[0:pairs], e_rows[1:extended])

    blank = jnp.zeros((PAIR, channels), jnp.bfloat16)
    lhs, vec = (lhs_0, lhs_1), (vec_0, vec_1, vec_2, vec_3)
    message = (message_0, message_1)

    def make_rows(q, radial, vectors_ref):
        columns = jnp.transpose(h_rows[q])
        before = e_rows[q]
        after = e_rows[q + 1]
        across = jnp.where(low, after, before)
        for chunk in range(NA // 16):
            start = chunk * 16
            own_a = [columns[start : start + 16, c : c + 1] for c in range(3)]
            own_b = [columns[NA + start : NA + start + 16, c : c + 1] for c in range(3)]
            own_a = [jnp.broadcast_to(o, (16, PAIR)) for o in own_a]
            own_b = [jnp.broadcast_to(o, (16, PAIR)) for o in own_b]
            blocks = (
                [before[c : c + 1] - own_a[c] for c in range(3)],
                [after[c : c + 1] - own_b[c] for c in range(3)],
                [across[c : c + 1] - jnp.where(low, own_a[c], own_b[c]) for c in range(3)],
            )
            for block, displacement in enumerate(blocks):
                radials, vectors = basis(displacement, basis_count)
                at = slice(block * PAIR, (block + 1) * PAIR)
                for k, value in enumerate(radials):
                    radial[k * NA + start : k * NA + start + 16, at] = value.astype(jnp.bfloat16)
                for c, value in enumerate(vectors):
                    vectors_ref[c * NA + start : c * NA + start + 16, at] = value.astype(jnp.bfloat16)

    def make_messages(q, radial, vectors_ref, out):
        if isinstance(q, int):
            near = table[q * PAIR : (q + 2) * PAIR, :]
        else:
            near = table[pl.ds(pl.multiple_of(q * PAIR, PAIR), 2 * PAIR), :]
        signals = jnp.concatenate(
            [
                jnp.concatenate([near[:PAIR], blank], axis=1),
                jnp.concatenate([blank, near[PAIR:]], axis=1),
                jnp.concatenate([near[PAIR : 3 * NA], blank[:NA]], axis=1),
                jnp.concatenate([blank[:NA], near[NA:PAIR]], axis=1),
            ],
            axis=0,
        )
        sums = dot(vectors_ref[...], signals)
        norm = sums[:NA] * sums[:NA]
        for c in range(1, 3):
            part = sums[c * NA : (c + 1) * NA]
            norm = norm + part * part
        norm = (norm * scale_square).astype(jnp.bfloat16)
        sums = dot(radial[...], signals)
        scalar = sums[:NA] * filters[0:1]
        for k in range(1, basis_count):
            scalar = scalar + sums[k * NA : (k + 1) * NA] * filters[k : k + 1]
        scalar = scalar.astype(jnp.bfloat16)
        for own in range(2):
            at = slice(own * channels, (own + 1) * channels)
            out[own * NA : (own + 1) * NA, :channels] = scalar[:, at]
            out[own * NA : (own + 1) * NA, channels:] = norm[:, at]

    def make_force(q, message_ref, vectors_ref):
        if isinstance(q, int):
            at_feat = slice(NA + q * PAIR, NA + (q + 1) * PAIR)
            at_push = slice(q * PAIR, (q + 1) * PAIR)
        else:
            at_feat = pl.ds(pl.multiple_of(q * PAIR, PAIR) + NA, PAIR)
            at_push = pl.ds(pl.multiple_of(q * PAIR, PAIR), PAIR)
        half = 0.5 * dot(message_ref[...], mix_ref[...])
        hidden = (own_feat[at_feat, :].astype(jnp.float32) + (half + half * jnp.tanh(half))).astype(jnp.bfloat16)
        pull = hidden.astype(jnp.float32) * later_push[0:1] + message_push[at_push, :]
        pull = jnp.sum(pull, axis=1, keepdims=True)
        first = jnp.broadcast_to(pull[:NA], (NA, PAIR))
        second = jnp.broadcast_to(pull[NA:], (NA, PAIR))
        weights = (first, second, jnp.where(low, first, second))
        for c in range(3):
            sums = []
            for block in range(3):
                value = vectors_ref[c * NA : (c + 1) * NA, block * PAIR : (block + 1) * PAIR].astype(jnp.float32)
                value = value * weights[block]
                total = value[:8]
                for row in range(8, NA, 8):
                    total = total + value[row : row + 8]
                sums.append(total)
            forces[q, c] = forces[q, c] - sums[0] - jnp.where(low, 0.0, sums[2])
            forces[q + 1, c] = -sums[1] - jnp.where(low, sums[2], 0.0)

    forces[0] = jnp.zeros(forces.shape[1:], jnp.float32)

    def stage_of(q, t, rows=True, before=True):
        if before:
            make_force(q - 1, message[(t + 1) % 2], vec[(t + 3) % 4])
        make_messages(q, lhs[t % 2], vec[t % 4], message[t % 2])
        if rows:
            make_rows(q + 1, lhs[(t + 1) % 2], vec[(t + 1) % 4])

    make_rows(0, lhs_0, vec_0)
    stage_of(0, 0, before=False)
    whole = (pairs - 2) // UNROLL

    if whole > 1:

        def several(i, _):
            for t in range(UNROLL):
                stage_of(i * UNROLL + t + 1, t + 1)
            return 0

        lax.fori_loop(0, whole, several, 0)
    for q in range(whole * UNROLL + 1 if whole > 1 else 1, pairs):
        stage_of(q, q, rows=q < pairs - 1)
    make_force(pairs - 1, message[(pairs - 1) % 2], vec[(pairs - 1) % 4])

    for p in range(own_pairs):
        tile = jnp.zeros((8, PAIR), jnp.float32)
        for c in range(3):
            tile = jnp.where(sub == c, jnp.sum(forces[p + 1, c], axis=0, keepdims=True), tile)
        g_out[p] = tile
    g = g_out[...]
    if stage == 0:
        v = half_v
    else:
        v = half_v + (0.5 * step_time) * g
    v_out[...] = v
    kinetic = jnp.sum(v * v, axis=0)
    kinetic = jnp.sum(jnp.sum(kinetic, axis=1, keepdims=True), axis=0, keepdims=True)
    x = e_rows[1 : own_pairs + 1]
    if stage < 3:
        x = x + (0.5 * step_time * step_time) * g
    x_out[...] = x
    for edge, p in enumerate((0, own_pairs - 1)):
        edge_out[edge, 0] = x[p]
        edge_out[edge, 1] = jnp.where(sub == 3, kinetic, v[p])


VMEM_SPEC = pl.BlockSpec(memory_space=pltpu.VMEM)
SMEM_SPEC = pl.BlockSpec(memory_space=pltpu.SMEM)


def run_prepare(place, state, features, per_replica, first, scale_one, later, scale_two, push):
    atoms, channels = features.shape
    own_pairs = atoms // per_replica // PAIR
    extended = own_pairs + 2
    return pl.pallas_call(
        prepare,
        out_shape=(
            jax.ShapeDtypeStruct((extended, 8, PAIR), jnp.float32),
            jax.ShapeDtypeStruct((own_pairs, 8, PAIR), jnp.float32),
            jax.ShapeDtypeStruct((extended * PAIR, channels), jnp.bfloat16),
            jax.ShapeDtypeStruct((extended * PAIR, channels), jnp.bfloat16),
            jax.ShapeDtypeStruct(((extended - 1) * PAIR, channels), jnp.float32),
            jax.ShapeDtypeStruct((8, channels), jnp.float32),
        ),
        in_specs=[SMEM_SPEC] + [VMEM_SPEC] * 7,
        out_specs=(VMEM_SPEC,) * 6,
        compiler_params=pltpu.CompilerParams(vmem_limit_bytes=20 * 1024 * 1024),
    )(place, state, features, first, scale_one, later, scale_two, push)


def run_advance(stage, place, thermal, x, v, g, edge, got, own_feat, table, message_push, later_push, filters, scale_one, mix):
    own_pairs = v.shape[0]
    channels = table.shape[1]
    basis_count = filters.shape[0]
    tiles = jax.ShapeDtypeStruct(v.shape, jnp.float32)
    lhs = pltpu.VMEM((basis_count * NA, 3 * PAIR), jnp.bfloat16)
    vec = pltpu.VMEM((3 * NA, 3 * PAIR), jnp.bfloat16)
    message = pltpu.VMEM((PAIR, 2 * channels), jnp.bfloat16)
    return pl.pallas_call(
        functools.partial(advance, stage),
        out_shape=(tiles, tiles, tiles, jax.ShapeDtypeStruct((2, 2, 8, PAIR), jnp.float32)),
        in_specs=[SMEM_SPEC] * 2 + [VMEM_SPEC] * 12,
        out_specs=(VMEM_SPEC,) * 4,
        scratch_shapes=[
            pltpu.VMEM((own_pairs + 2, 8, PAIR), jnp.float32),
            pltpu.VMEM((own_pairs + 1, 8, PAIR), jnp.float32),
            lhs,
            lhs,
            vec,
            vec,
            vec,
            vec,
            message,
            message,
            pltpu.VMEM((own_pairs + 2, 3, 8, PAIR), jnp.float32),
        ],
        compiler_params=pltpu.CompilerParams(vmem_limit_bytes=20 * 1024 * 1024),
    )(place, thermal, x, v, g, edge, got, own_feat, table, message_push, later_push, filters, scale_one, mix)


def run_steps(place, thermal, state, features, per_replica, exchange, weights):
    first, filters, scale_one, mix, later, scale_two, push = weights
    x, v, *fixed = run_prepare(place, state, features, per_replica, first, scale_one, later, scale_two, push)
    edge = got = jnp.zeros((2, 2, 8, PAIR), jnp.float32)
    g = v
    for step in range(STEPS + 1):
        stage = min(step, 2) if step < STEPS else 3
        x, v, g, edge = run_advance(
            stage, place, thermal, x, v, g, edge, got, *fixed, filters, scale_one, mix
        )
        if step < STEPS:
            got = exchange(edge)
    return x, v, g, edge[0, 1, 3, 0]


def on_device(
    particle_places,
    particle_speeds,
    thermal_targets,
    element_features,
    swap_counterpart_slot,
    swap_approval_flags,
    initial_signal_projector,
    initial_distance_filter,
    initial_directional_scales,
    invariant_revision_matrix,
    magnitude_revision_matrix,
    later_signal_projector,
    later_directional_scales,
    push_output_matrix,
):
    replicas = particle_places.shape[0]
    local_atoms = particle_places.shape[2]
    local_cells = local_atoms // NA
    devices = lax.axis_size("dom")
    own = lax.axis_index("dom")
    per_replica = devices // replicas
    bits = devices.bit_length() - 1
    replica_bits = replicas.bit_length() - 1

    def trade(value, mask):
        return lax.ppermute(value, "dom", [(i, i ^ mask) for i in range(devices)])

    state = jnp.concatenate([particle_places, particle_speeds], axis=1)
    features = element_features
    for level in range(bits):
        mask = devices >> (level + 1)
        upper = (own & mask) > 0
        if level < replica_bits:
            half = state.shape[0] // 2
            keep = jnp.where(upper, state[half:], state[:half])
            send = jnp.where(upper, state[:half], state[half:])
        else:
            keep = send = state
        got = trade(send, mask)
        got_features = trade(features, mask)
        axis = 1 + level
        state = jnp.stack([jnp.where(upper, got, keep), jnp.where(upper, keep, got)], axis=axis)
        features = jnp.stack(
            [jnp.where(upper, got_features, features), jnp.where(upper, features, got_features)], axis=level
        )
        if level + 1 < bits:
            state, features = lax.optimization_barrier((state, features))
    state = state.reshape(devices, 6, local_atoms).transpose(1, 0, 2).reshape(6, devices * local_atoms)
    features = features.reshape(devices * local_atoms, -1)
    thermal = lax.dynamic_slice(thermal_targets, (own // per_replica,), (1,))
    place = jnp.stack([own % per_replica, jnp.full((), per_replica, own.dtype)]).astype(jnp.int32)
    weights = (
        initial_signal_projector,
        initial_distance_filter,
        initial_directional_scales[None],
        jnp.concatenate([invariant_revision_matrix, magnitude_revision_matrix], axis=0),
        later_signal_projector,
        later_directional_scales[None],
        push_output_matrix[None],
    )

    def exchange(edge):
        if per_replica == 2:
            return trade(edge, 1)
        groups = [list(range(i, i + per_replica)) for i in range(0, devices, per_replica)]
        up = [(a, b) for g in groups for a, b in zip(g, g[1:] + g[:1])]
        kinetic = lax.psum(edge[0, 1, 3], "dom", axis_index_groups=groups) - edge[0, 1, 3]
        before = lax.ppermute(edge[1], "dom", up)
        after = lax.ppermute(edge[0], "dom", [(b, a) for a, b in up])
        return jnp.stack([after.at[1, 3].set(kinetic), before])

    x, v, g, kinetic = run_steps(place, thermal, state, features, per_replica, exchange, weights)

    state = jnp.stack([x, v, g])[:, :, :3].transpose(0, 2, 1, 3).reshape(9, -1)
    state = jnp.concatenate([state, jnp.broadcast_to(kinetic, (1, state.shape[1]))], axis=0)[:, None]
    for level in range(replica_bits, bits):
        mask = devices >> (level + 1)
        upper = (own & mask) > 0
        got = trade(state, mask)
        state = jnp.stack([jnp.where(upper, got, state), jnp.where(upper, state, got)], axis=1 + level - replica_bits)
        state = state.reshape((10,) + (2,) * (level + 1 - replica_bits) + (-1,))
    state = state.reshape(10, per_replica, -1)
    kinetic = jnp.sum(state[9, :, 0])
    stretch = jnp.sqrt(thermal[0] / (kinetic / (3.0 * devices * local_atoms) + motion_work_lower_limit))
    factor = jnp.where((jnp.arange(9) // 3) == 1, stretch, 1.0)
    state = state[:9] * factor[:, None, None]

    state = state.reshape(9, replicas, per_replica, local_atoms)
    state = lax.dynamic_index_in_dim(state, own % per_replica, 2, keepdims=False)
    state = state.transpose(1, 0, 2)[:, None]
    for level in range(replica_bits):
        mask = devices >> (level + 1)
        upper = (own & mask) > 0
        half = state.shape[0] // 2
        keep = jnp.where(upper, state[half:], state[:half])
        send = jnp.where(upper, state[:half], state[half:])
        got = trade(send, mask)
        state = jnp.stack([jnp.where(upper, got, keep), jnp.where(upper, keep, got)], axis=1 + level)
    state = state.reshape(replicas, 3, 3, local_atoms)

    ladder_slot = jnp.arange(replicas, dtype=jnp.int32)
    source = jnp.where(swap_approval_flags > 0, swap_counterpart_slot, ladder_slot)
    chosen = source[:, None] == ladder_slot[None, :]
    state = jnp.sum(jnp.where(chosen[:, :, None, None, None], state[None], 0.0), axis=1)
    thermal_source = jnp.sum(jnp.where(chosen, thermal_targets[None, :], 0.0), axis=1)
    thermal_ratio = jnp.sqrt(thermal_targets / thermal_source)
    atom_cell = (own * local_cells + jnp.arange(local_atoms, dtype=jnp.int32) // NA).astype(jnp.float32)
    cell_floor = jnp.array([0.0, 0.0, 1.0], jnp.float32)[:, None] * atom_cell[None, :]
    return (
        state[:, 0] - cell_floor[None],
        state[:, 1] * thermal_ratio[:, None, None],
        state[:, 2],
    )


def solution(mesh):
    return jax.shard_map(
        on_device,
        mesh=mesh,
        in_specs=(
            P("groups", None, "dom"),
            P("groups", None, "dom"),
            P("groups"),
            P(("groups", "dom"), None),
            P("groups"),
            P("groups"),
            P(),
            P(),
            P(),
            P(),
            P(),
            P(),
            P(),
            P(),
        ),
        out_specs=(P("groups", None, "dom"), P("groups", None, "dom"), P("groups", None, "dom")),
        check_vma=False,
    )
```

time: 153 us -> 102 us (0.67)
  Pallas kernels: 107 us -> 46.1 us
  waiting for transfers between devices: 25.3 us -> 28.5 us
  local copies, waits for them, and re-layouts: 5.97 us -> 7.71 us
  starting transfers between devices: 11.6 us -> 13.2 us
    pallas_call x1 -> x6, Pallas kernels: 107 us -> 46.1 us  [the longest x5 45.3 us: run_advance(): pl.pallas_call(functools.partial(advance, stage), out_shape=(tiles, tiles...]
    ppermute x11 -> x16, waiting for transfers between devices: 25.3 us -> 28.5 us  [trade(): return lax.ppermute(value, 'dom', [(i, i ^ mask) for i in range(devices)])]
    ppermute x11 -> x16, starting transfers between devices: 11.6 us -> 13.2 us  [trade(): return lax.ppermute(value, 'dom', [(i, i ^ mask) for i in range(devices)])]
    unnamed x33 -> x36, local copies, waits for them, and re-layouts: 4.59 us -> 5.17 us
  transfers between devices with their start and end apart: 11 -> 16, of which waited for: 10 -> 14; matrix products, arithmetic and copies ran while one was open for 1% -> 2% of each run, Pallas kernels for 0% -> 0%
where the time goes in v2:
time: 102 us; the launch traced here: 101 us
  Pallas kernels  46.1 us (45%)
  waiting for transfers between devices  28.5 us (28%)
  starting transfers between devices  13.2 us (13%)
  local copies, waits for them, and re-layouts  7.71 us (8%)
  other arithmetic  3.11 us (3%)
  between operations  2.5 us (2%)
    pallas_call x5, Pallas kernels, run_advance(): pl.pallas_call(functools.partial(advance, stage), out_shape=(tiles, tiles...  45.3 us
    ppermute x16, waiting for transfers between devices, trade(): return lax.ppermute(value, 'dom', [(i, i ^ mask) for i in range(devices)])  28.5 us
    ppermute x16, starting transfers between devices, trade(): return lax.ppermute(value, 'dom', [(i, i ^ mask) for i in range(devices)])  13.2 us
    unnamed x36, local copies, waits for them, and re-layouts  5.17 us
  transfers between devices with their start and end apart: 16, of which 14 were waited for; matrix products, arithmetic and copies ran while one was open for 2% of the time, Pallas kernels for 0%

profile of v2, /device:TPU:0, one launch (start us, length us, event | category | flops | bytes accessed | tf_op | source)
XLA Modules:
  0.0 101.1 jit_solution(12332309532414503310)
XLA Ops:
  0.6 0.7 constant_dynamic-update-slice_fusion.1
  1.4 4.1 %collective-permute-start = (f32[4,6,192]{2,0,1:T(4,128)S(1)}, f32[4,6,192]{2,0,1:T(4,128)S(1)}, u32[]{:S(2)}, u32[]{:S(2)}) collective-permute-start(f32[4,6,192]{2,0,1:T(4,128)S(1)} %slice_select_fusion.2), channel_id=1, source_target_pairs={{0,8},{1,9},{2,10},{3,11},{4,12},{5,13},{6,14},{7,15},{8,0},{9,1},... | collective-permute-start | bytes 55304 | tf_op jit(solution)/shard_map/ppermute | solution.py:401
  6.2 1.1 %collective-permute-done = f32[4,6,192]{2,0,1:T(4,128)S(1)} collective-permute-done((f32[4,6,192]{2,0,1:T(4,128)S(1)}, f32[4,6,192]{2,0,1:T(4,128)S(1)}, u32[]{:S(2)}, u32[]{:S(2)}) %collective-permute-start) | collective-permute-done | bytes 18464 | tf_op jit(solution)/shard_map/ppermute | solution.py:401
  7.4 3.3 %collective-permute-done.1 = bf16[192,128]{1,0:T(8,128)(2,1)S(1)} collective-permute-done((bf16[192,128]{1,0:T(8,128)(2,1)S(1)}, bf16[192,128]{1,0:T(8,128)(2,1)S(1)}, u32[]{:S(2)}, u32[]{:S(2)}) %collective-permute-start.1) | collective-permute-done | bytes 49184 | tf_op jit(solution)/shard_map/ppermute | solution.py:401
  10.7 1.5 %collective-permute-start.2 = (f32[2,2,6,192]{3,0,2,1:T(2,128)S(1)}, f32[2,2,6,192]{3,0,2,1:T(2,128)S(1)}, u32[]{:S(2)}, u32[]{:S(2)}) collective-permute-start(f32[2,2,6,192]{3,0,2,1:T(2,128)S(1)} %broadcast_select_fusion.9), channel_id=1, source_target_pairs={{0,4},{1,5},{2,6},{3,7},{4,0},{5,1},{6,2},{7,3},{8,12},{9,13},{10,... | collective-permute-start | bytes 55304 | tf_op jit(solution)/shard_map/ppermute | solution.py:401
  12.9 1.7 %collective-permute-done.2 = f32[2,2,6,192]{3,0,2,1:T(2,128)S(1)} collective-permute-done((f32[2,2,6,192]{3,0,2,1:T(2,128)S(1)}, f32[2,2,6,192]{3,0,2,1:T(2,128)S(1)}, u32[]{:S(2)}, u32[]{:S(2)}) %collective-permute-start.2) | collective-permute-done | bytes 18464 | tf_op jit(solution)/shard_map/ppermute | solution.py:401
  14.7 2.2 %collective-permute-done.3 = bf16[2,192,128]{2,1,0:T(8,128)(2,1)S(1)} collective-permute-done((bf16[2,192,128]{2,1,0:T(8,128)(2,1)S(1)}, bf16[2,192,128]{2,1,0:T(8,128)(2,1)S(1)}, u32[]{:S(2)}, u32[]{:S(2)}) %collective-permute-start.3) | collective-permute-done | bytes 98336 | tf_op jit(solution)/shard_map/ppermute | solution.py:401
  17.0 1.6 %collective-permute-start.4 = (f32[1,2,2,6,192]{4,0,3,1,2:T(1,128)S(1)}, f32[1,2,2,6,192]{4,0,3,1,2:T(1,128)S(1)}, u32[]{:S(2)}, u32[]{:S(2)}) collective-permute-start(f32[1,2,2,6,192]{4,0,3,1,2:T(1,128)S(1)} %broadcast_select_fusion.7), channel_id=1, source_target_pairs={{0,2},{1,3},{2,0},{3,1},{4,6},{5,7},{6,4},{7,5},{8,10},{9,11},{10,... | collective-permute-start | bytes 55304 | tf_op jit(solution)/shard_map/ppermute | solution.py:401
  19.2 1.7 %collective-permute-done.4 = f32[1,2,2,6,192]{4,0,3,1,2:T(1,128)S(1)} collective-permute-done((f32[1,2,2,6,192]{4,0,3,1,2:T(1,128)S(1)}, f32[1,2,2,6,192]{4,0,3,1,2:T(1,128)S(1)}, u32[]{:S(2)}, u32[]{:S(2)}) %collective-permute-start.4) | collective-permute-done | bytes 18464 | tf_op jit(solution)/shard_map/ppermute | solution.py:401
  21.0 3.3 %collective-permute-done.5 = bf16[2,2,192,128]{3,2,0,1:T(8,128)(2,1)S(1)} collective-permute-done((bf16[2,2,192,128]{3,2,0,1:T(8,128)(2,1)S(1)}, bf16[2,2,192,128]{3,2,0,1:T(8,128)(2,1)S(1)}, u32[]{:S(2)}, u32[]{:S(2)}) %collective-permute-start.5) | collective-permute-done | bytes 196640 | tf_op jit(solution)/shard_map/ppermute | solution.py:401
  27.6 0.8 shard_map.166
  29.1 9.0 %shard_map.167 = (f32[12,8,128]{2,1,0:T(8,128)S(1)}, f32[12,8,128]{2,1,0:T(8,128)S(1)}, f32[12,8,128]{2,1,0:T(8,128)S(1)}, f32[2,2,8,128]{3,2,1,0:T(8,128)S(1)}) custom-call(s32[2]{0:T(128)S(1)} %pad_add_fusion.place_ref, f32[1]{0:T(128)} %dynamic_slice.7.thermal_ref, f32[14,8,128]{2,1,0:T(8,128)S(1)} %get-tuple-element.41.x_ref, ...), custom_call_target="tpu_custom_call" | custom-call | tf_op jit(solution)/shard_map/pallas_call | solution.py:338
  38.3 1.1 %collective-permute-done.8.got_ref = f32[2,2,8,128]{3,2,1,0:T(8,128)S(1)} collective-permute-done((f32[2,2,8,128]{3,2,1,0:T(8,128)S(1)}, f32[2,2,8,128]{3,2,1,0:T(8,128)S(1)}, u32[]{:S(2)}, u32[]{:S(2)}) %collective-permute-start.8) | collective-permute-done | bytes 16416 | tf_op jit(solution)/shard_map/ppermute | solution.py:401
  39.4 8.9 %shard_map.168 = (f32[12,8,128]{2,1,0:T(8,128)S(1)}, f32[12,8,128]{2,1,0:T(8,128)S(1)}, f32[12,8,128]{2,1,0:T(8,128)S(1)}, f32[2,2,8,128]{3,2,1,0:T(8,128)S(1)}) custom-call(s32[2]{0:T(128)S(1)} %pad_add_fusion.place_ref, f32[1]{0:T(128)} %dynamic_slice.7.thermal_ref, f32[12,8,128]{2,1,0:T(8,128)S(1)} %get-tuple-element.47.x_ref, ...), custom_call_target="tpu_custom_call" | custom-call | tf_op jit(solution)/shard_map/pallas_call | solution.py:338
  48.5 1.0 %collective-permute-done.9.got_ref = f32[2,2,8,128]{3,2,1,0:T(8,128)S(1)} collective-permute-done((f32[2,2,8,128]{3,2,1,0:T(8,128)S(1)}, f32[2,2,8,128]{3,2,1,0:T(8,128)S(1)}, u32[]{:S(2)}, u32[]{:S(2)}) %collective-permute-start.9) | collective-permute-done | bytes 16416 | tf_op jit(solution)/shard_map/ppermute | solution.py:401
  49.5 9.2 %shard_map.169 = (f32[12,8,128]{2,1,0:T(8,128)S(1)}, f32[12,8,128]{2,1,0:T(8,128)S(1)}, f32[12,8,128]{2,1,0:T(8,128)S(1)}, f32[2,2,8,128]{3,2,1,0:T(8,128)S(1)}) custom-call(s32[2]{0:T(128)S(1)} %pad_add_fusion.place_ref, f32[1]{0:T(128)} %dynamic_slice.7.thermal_ref, f32[12,8,128]{2,1,0:T(8,128)S(1)} %get-tuple-element.51.x_ref, ...), custom_call_target="tpu_custom_call" | custom-call | tf_op jit(solution)/shard_map/pallas_call | solution.py:338
  58.8 1.0 %collective-permute-done.10.got_ref = f32[2,2,8,128]{3,2,1,0:T(8,128)S(1)} collective-permute-done((f32[2,2,8,128]{3,2,1,0:T(8,128)S(1)}, f32[2,2,8,128]{3,2,1,0:T(8,128)S(1)}, u32[]{:S(2)}, u32[]{:S(2)}) %collective-permute-start.10) | collective-permute-done | bytes 16416 | tf_op jit(solution)/shard_map/ppermute | solution.py:401
  59.8 9.0 %shard_map.170 = (f32[12,8,128]{2,1,0:T(8,128)S(1)}, f32[12,8,128]{2,1,0:T(8,128)S(1)}, f32[12,8,128]{2,1,0:T(8,128)S(1)}, f32[2,2,8,128]{3,2,1,0:T(8,128)S(1)}) custom-call(s32[2]{0:T(128)S(1)} %pad_add_fusion.place_ref, f32[1]{0:T(128)} %dynamic_slice.7.thermal_ref, f32[12,8,128]{2,1,0:T(8,128)S(1)} %get-tuple-element.55.x_ref, ...), custom_call_target="tpu_custom_call" | custom-call | tf_op jit(solution)/shard_map/pallas_call | solution.py:338
  70.0 9.2 %shard_map.171 = (f32[12,8,128]{2,1,0:T(8,128)S(1)}, f32[12,8,128]{2,1,0:T(8,128)S(1)}, f32[12,8,128]{2,1,0:T(8,128)S(1)}, f32[2,2,8,128]{3,2,1,0:T(8,128)S(1)}) custom-call(s32[2]{0:T(128)S(1)} %pad_add_fusion.place_ref, f32[1]{0:T(128)} %dynamic_slice.7.thermal_ref, f32[12,8,128]{2,1,0:T(8,128)S(1)} %get-tuple-element.59.x_ref, ...), custom_call_target="tpu_custom_call" | custom-call | tf_op jit(solution)/shard_map/pallas_call | solution.py:338
  80.7 1.1 %collective-permute-done.12 = f32[10,1,1536]{2,0,1:T(8,128)S(1)} collective-permute-done((f32[10,1,1536]{2,0,1:T(8,128)S(1)}, f32[10,1,1536]{2,0,1:T(8,128)S(1)}, u32[]{:S(2)}, u32[]{:S(2)}) %collective-permute-start.12) | collective-permute-done | bytes 61472 | tf_op jit(solution)/shard_map/ppermute | solution.py:401
  85.0 1.6 %collective-permute-start.13 = (f32[4,1,9,192]{3,0,2,1:T(4,128)S(1)}, f32[4,1,9,192]{3,0,2,1:T(4,128)S(1)}, u32[]{:S(2)}, u32[]{:S(2)}) collective-permute-start(f32[4,1,9,192]{3,0,2,1:T(4,128)S(1)} %select_bitcast_fusion.12), channel_id=1, source_target_pairs={{0,8},{1,9},{2,10},{3,11},{4,12},{5,13},{6,14},{7,15},{8,0},{9,1},... | collective-permute-start | bytes 82952 | tf_op jit(solution)/shard_map/ppermute | solution.py:401
  86.7 3.6 %collective-permute-done.13 = f32[4,1,9,192]{3,0,2,1:T(4,128)S(1)} collective-permute-done((f32[4,1,9,192]{3,0,2,1:T(4,128)S(1)}, f32[4,1,9,192]{3,0,2,1:T(4,128)S(1)}, u32[]{:S(2)}, u32[]{:S(2)}) %collective-permute-start.13) | collective-permute-done | bytes 27680 | tf_op jit(solution)/shard_map/ppermute | solution.py:401
  90.9 3.5 %collective-permute-done.14 = f32[2,2,1,9,192]{4,0,3,1,2:T(2,128)S(1)} collective-permute-done((f32[2,2,1,9,192]{4,0,3,1,2:T(2,128)S(1)}, f32[2,2,1,9,192]{4,0,3,1,2:T(2,128)S(1)}, u32[]{:S(2)}, u32[]{:S(2)}) %collective-permute-start.14) | collective-permute-done | bytes 27680 | tf_op jit(solution)/shard_map/ppermute | solution.py:401
  95.2 3.4 %collective-permute-done.15 = f32[1,2,2,1,9,192]{5,0,4,1,3,2:T(1,128)S(1)} collective-permute-done((f32[1,2,2,1,9,192]{5,0,4,1,3,2:T(1,128)S(1)}, f32[1,2,2,1,9,192]{5,0,4,1,3,2:T(1,128)S(1)}, u32[]{:S(2)}, u32[]{:S(2)}) %collective-permute-start.15) | collective-permute-done | bytes 27680 | tf_op jit(solution)/shard_map/ppermute | solution.py:401
  (113 shorter events, 14.9 us)
Async XLA Ops:
  0.6 0.8 copy-start.9
  1.4 4.1 %copy-start.6 = (bf16[192,128]{1,0:T(8,128)(2,1)S(1)}, bf16[192,128]{1,0:T(8,128)(2,1)}, u32[]{:S(2)}) copy-start(bf16[192,128]{1,0:T(8,128)(2,1)} %param.18) | copy-start | bytes 147460
  1.4 5.9 %collective-permute-start = (f32[4,6,192]{2,0,1:T(4,128)S(1)}, f32[4,6,192]{2,0,1:T(4,128)S(1)}, u32[]{:S(2)}, u32[]{:S(2)}) collective-permute-start(f32[4,6,192]{2,0,1:T(4,128)S(1)} %slice_select_fusion.2), channel_id=1, source_target_pairs={{0,8},{1,9},{2,10},{3,11},{4,12},{5,13},{6,14},{7,15},{8,0},{9,1},... | collective-permute-start | bytes 55304 | tf_op jit(solution)/shard_map/ppermute | solution.py:401
  5.5 5.1 %collective-permute-start.1 = (bf16[192,128]{1,0:T(8,128)(2,1)S(1)}, bf16[192,128]{1,0:T(8,128)(2,1)S(1)}, u32[]{:S(2)}, u32[]{:S(2)}) collective-permute-start(bf16[192,128]{1,0:T(8,128)(2,1)S(1)} %copy-done.6), channel_id=1, source_target_pairs={{0,8},{1,9},{2,10},{3,11},{4,12},{5,13},{6,14},{7,15},{8,0},{9,1},... | collective-permute-start | bytes 147464 | tf_op jit(solution)/shard_map/ppermute | solution.py:401
  10.7 1.6 %copy-start.7 = (bf16[128,128]{1,0:T(8,128)(2,1)S(1)}, bf16[128,128]{1,0:T(8,128)(2,1)}, u32[]{:S(2)}) copy-start(bf16[128,128]{1,0:T(8,128)(2,1)} %param.24) | copy-start | bytes 98308
  10.7 3.9 %collective-permute-start.2 = (f32[2,2,6,192]{3,0,2,1:T(2,128)S(1)}, f32[2,2,6,192]{3,0,2,1:T(2,128)S(1)}, u32[]{:S(2)}, u32[]{:S(2)}) collective-permute-start(f32[2,2,6,192]{3,0,2,1:T(2,128)S(1)} %broadcast_select_fusion.9), channel_id=1, source_target_pairs={{0,4},{1,5},{2,6},{3,7},{4,0},{5,1},{6,2},{7,3},{8,12},{9,13},{10,... | collective-permute-start | bytes 55304 | tf_op jit(solution)/shard_map/ppermute | solution.py:401
  12.2 4.6 %collective-permute-start.3 = (bf16[2,192,128]{2,1,0:T(8,128)(2,1)S(1)}, bf16[2,192,128]{2,1,0:T(8,128)(2,1)S(1)}, u32[]{:S(2)}, u32[]{:S(2)}) collective-permute-start(bf16[2,192,128]{2,1,0:T(8,128)(2,1)S(1)} %pad_maximum_fusion.4), channel_id=1, source_target_pairs={{0,4},{1,5},{2,6},{3,7},{4,0},{5,1},{6,2},{7,3},{8,12},{9,13},{10,... | collective-permute-start | bytes 294920 | tf_op jit(solution)/shard_map/ppermute | solution.py:401
  16.9 1.6 %copy-start.8 = (bf16[128,128]{1,0:T(8,128)(2,1)S(1)}, bf16[128,128]{1,0:T(8,128)(2,1)}, u32[]{:S(2)}) copy-start(bf16[128,128]{1,0:T(8,128)(2,1)} %param.25) | copy-start | bytes 98308
  17.0 3.9 %collective-permute-start.4 = (f32[1,2,2,6,192]{4,0,3,1,2:T(1,128)S(1)}, f32[1,2,2,6,192]{4,0,3,1,2:T(1,128)S(1)}, u32[]{:S(2)}, u32[]{:S(2)}) collective-permute-start(f32[1,2,2,6,192]{4,0,3,1,2:T(1,128)S(1)} %broadcast_select_fusion.7), channel_id=1, source_target_pairs={{0,2},{1,3},{2,0},{3,1},{4,6},{5,7},{6,4},{7,5},{8,10},{9,11},{10,... | collective-permute-start | bytes 55304 | tf_op jit(solution)/shard_map/ppermute | solution.py:401
  18.6 5.7 %collective-permute-start.5 = (bf16[2,2,192,128]{3,2,0,1:T(8,128)(2,1)S(1)}, bf16[2,2,192,128]{3,2,0,1:T(8,128)(2,1)S(1)}, u32[]{:S(2)}, u32[]{:S(2)}) collective-permute-start(bf16[2,2,192,128]{3,2,0,1:T(8,128)(2,1)S(1)} %pad_maximum_fusion.3), channel_id=1, source_target_pairs={{0,2},{1,3},{2,0},{3,1},{4,6},{5,7},{6,4},{7,5},{8,10},{9,11},{10,... | collective-permute-start | bytes 589832 | tf_op jit(solution)/shard_map/ppermute | solution.py:401
  24.4 1.9 %collective-permute-start.6 = (f32[1,2,2,2,6,192]{5,2,4,1,3,0:T(2,128)S(1)}, f32[1,2,2,2,6,192]{5,2,4,1,3,0:T(2,128)S(1)}, u32[]{:S(2)}, u32[]{:S(2)}) collective-permute-start(f32[1,2,2,2,6,192]{5,2,4,1,3,0:T(2,128)S(1)} %pad_maximum_fusion.12), channel_id=1, source_target_pairs={{0,1},{1,0},{2,3},{3,2},{4,5},{5,4},{6,7},{7,6},{8,9},{9,8},{10,11... | collective-permute-start | bytes 110600 | tf_op jit(solution)/shard_map/ppermute | solution.py:401
  24.5 2.2 %collective-permute-start.7 = (bf16[2,2,2,192,128]{4,3,0,1,2:T(8,128)(2,1)S(1)}, bf16[2,2,2,192,128]{4,3,0,1,2:T(8,128)(2,1)S(1)}, u32[]{:S(2)}, u32[]{:S(2)}) collective-permute-start(bf16[2,2,2,192,128]{4,3,0,1,2:T(8,128)(2,1)S(1)} %pad_maximum_fusion.1), channel_id=1, source_target_pairs={{0,1},{1,0},{2,3},{3,2},{4,5},{5,4},{6,7},{7,6},{8,9},{9,8},{10,11... | collective-permute-start | bytes 1179656 | tf_op jit(solution)/shard_map/ppermute | solution.py:401
  26.8 0.8 copy-start.1
  26.8 0.8 copy-start.2
  38.1 1.2 %collective-permute-start.8 = (f32[2,2,8,128]{3,2,1,0:T(8,128)S(1)}, f32[2,2,8,128]{3,2,1,0:T(8,128)S(1)}, u32[]{:S(2)}, u32[]{:S(2)}) collective-permute-start(f32[2,2,8,128]{3,2,1,0:T(8,128)S(1)} %get-tuple-element.50.edge_ref), channel_id=1, source_target_pairs={{0,1},{1,0},{2,3},{3,2},{4,5},{5,4},{6,7},{7,6},{8,9},{9,8},{10,11... | collective-permute-start | bytes 49160 | tf_op jit(solution)/shard_map/ppermute | solution.py:401
  48.3 1.2 %collective-permute-start.9 = (f32[2,2,8,128]{3,2,1,0:T(8,128)S(1)}, f32[2,2,8,128]{3,2,1,0:T(8,128)S(1)}, u32[]{:S(2)}, u32[]{:S(2)}) collective-permute-start(f32[2,2,8,128]{3,2,1,0:T(8,128)S(1)} %get-tuple-element.54.edge_ref), channel_id=1, source_target_pairs={{0,1},{1,0},{2,3},{3,2},{4,5},{5,4},{6,7},{7,6},{8,9},{9,8},{10,11... | collective-permute-start | bytes 49160 | tf_op jit(solution)/shard_map/ppermute | solution.py:401
  58.7 1.2 %collective-permute-start.10 = (f32[2,2,8,128]{3,2,1,0:T(8,128)S(1)}, f32[2,2,8,128]{3,2,1,0:T(8,128)S(1)}, u32[]{:S(2)}, u32[]{:S(2)}) collective-permute-start(f32[2,2,8,128]{3,2,1,0:T(8,128)S(1)} %get-tuple-element.58.edge_ref), channel_id=1, source_target_pairs={{0,1},{1,0},{2,3},{3,2},{4,5},{5,4},{6,7},{7,6},{8,9},{9,8},{10,11... | collective-permute-start | bytes 49160 | tf_op jit(solution)/shard_map/ppermute | solution.py:401
  68.8 1.2 %collective-permute-start.11 = (f32[2,2,8,128]{3,2,1,0:T(8,128)S(1)}, f32[2,2,8,128]{3,2,1,0:T(8,128)S(1)}, u32[]{:S(2)}, u32[]{:S(2)}) collective-permute-start(f32[2,2,8,128]{3,2,1,0:T(8,128)S(1)} %get-tuple-element.62.edge_ref), channel_id=1, source_target_pairs={{0,1},{1,0},{2,3},{3,2},{4,5},{5,4},{6,7},{7,6},{8,9},{9,8},{10,11... | collective-permute-start | bytes 49160 | tf_op jit(solution)/shard_map/ppermute | solution.py:401
  79.8 0.9 copy-start.11
  79.8 0.9 copy-start.12
  80.5 1.4 %collective-permute-start.12 = (f32[10,1,1536]{2,0,1:T(8,128)S(1)}, f32[10,1,1536]{2,0,1:T(8,128)S(1)}, u32[]{:S(2)}, u32[]{:S(2)}) collective-permute-start(f32[10,1,1536]{2,0,1:T(8,128)S(1)} %pad_bitcast_fusion), channel_id=1, source_target_pairs={{0,1},{1,0},{2,3},{3,2},{4,5},{5,4},{6,7},{7,6},{8,9},{9,8},{10,11... | collective-permute-start | bytes 184328 | tf_op jit(solution)/shard_map/ppermute | solution.py:401
  85.0 5.3 %collective-permute-start.13 = (f32[4,1,9,192]{3,0,2,1:T(4,128)S(1)}, f32[4,1,9,192]{3,0,2,1:T(4,128)S(1)}, u32[]{:S(2)}, u32[]{:S(2)}) collective-permute-start(f32[4,1,9,192]{3,0,2,1:T(4,128)S(1)} %select_bitcast_fusion.12), channel_id=1, source_target_pairs={{0,8},{1,9},{2,10},{3,11},{4,12},{5,13},{6,14},{7,15},{8,0},{9,1},... | collective-permute-start | bytes 82952 | tf_op jit(solution)/shard_map/ppermute | solution.py:401
  90.4 4.0 %collective-permute-start.14 = (f32[2,2,1,9,192]{4,0,3,1,2:T(2,128)S(1)}, f32[2,2,1,9,192]{4,0,3,1,2:T(2,128)S(1)}, u32[]{:S(2)}, u32[]{:S(2)}) collective-permute-start(f32[2,2,1,9,192]{4,0,3,1,2:T(2,128)S(1)} %bitcast_select_fusion.3), channel_id=1, source_target_pairs={{0,4},{1,5},{2,6},{3,7},{4,0},{5,1},{6,2},{7,3},{8,12},{9,13},{10,... | collective-permute-start | bytes 82952 | tf_op jit(solution)/shard_map/ppermute | solution.py:401
  94.6 4.0 %collective-permute-start.15 = (f32[1,2,2,1,9,192]{5,0,4,1,3,2:T(1,128)S(1)}, f32[1,2,2,1,9,192]{5,0,4,1,3,2:T(1,128)S(1)}, u32[]{:S(2)}, u32[]{:S(2)}) collective-permute-start(f32[1,2,2,1,9,192]{5,0,4,1,3,2:T(1,128)S(1)} %get-tuple-element.70), channel_id=1, source_target_pairs={{0,2},{1,3},{2,0},{3,1},{4,6},{5,7},{6,4},{7,5},{8,10},{9,11},{10,... | collective-permute-start | bytes 82952 | tf_op jit(solution)/shard_map/ppermute | solution.py:401
  (6 other events, 4.1 us)

commit v3 on v2

--- a/solution.py
+++ b/solution.py
@@ -11,7 +11,8 @@
 NA = 64
 PAIR = 2 * NA
 STEPS = 4
-UNROLL = 4
+UNROLL = 2
+SMALL_ROWS = 4
 
 step_time = 0.05
 motion_work_lower_limit = 1e-06
@@ -68,11 +69,8 @@
     place_ref,
     state_ref,
     feat_ref,
-    first_ref,
-    scale_one_ref,
-    later_ref,
-    scale_two_ref,
-    push_ref,
+    weight_ref,
+    small_ref,
     x_out,
     v_out,
     own_feat,
@@ -89,26 +87,27 @@
         at = pl.ds(pl.multiple_of(cell * NA, PAIR), PAIR)
         rows = state_ref[:, at]
         x = jnp.concatenate([rows[:3], jnp.zeros((5, PAIR), jnp.float32)], axis=0)
-        if p == 0 or p == extended - 1:
-            sub = lax.broadcasted_iota(jnp.int32, (8, PAIR), 0)
-            wraps = (place_ref[0] == 0) if p == 0 else (place_ref[0] == place_ref[1] - 1)
-            shift = jnp.where(wraps, float(cells), 0.0) * (-1.0 if p == 0 else 1.0)
-            x = x + jnp.where(sub == 2, shift, 0.0)
-        x_out[p] = x
+        sub = lax.broadcasted_iota(jnp.int32, (8, PAIR), 0)
+        lane = lax.broadcasted_iota(jnp.int32, (8, PAIR), 1)
+        floor = (place_ref[0] * own_cells - 2 + 2 * p + lane // NA).astype(jnp.float32)
+        x_out[p] = x + jnp.where(sub == 2, floor, 0.0)
         if 0 < p < extended - 1:
             v_out[p - 1] = jnp.concatenate([rows[3:6], jnp.zeros((5, PAIR), jnp.float32)], axis=0)
         own_feat[p * PAIR : (p + 1) * PAIR, :] = feat_ref[at, :]
-    table[...] = dot(own_feat[...], first_ref[...]).astype(jnp.bfloat16)
-    push = push_ref[...]
-    message_push[...] = table[NA : NA + (extended - 1) * PAIR, :].astype(jnp.float32) * (push * scale_one_ref[...])
-    parts = dot_rows(pieces(push * scale_two_ref[...], 3), later_ref[...])
+    channels = feat_ref.shape[1]
+    basis_count = small_ref.shape[0] - SMALL_ROWS
+    table[...] = dot(own_feat[...], weight_ref[:channels, :]).astype(jnp.bfloat16)
+    message_push[...] = (
+        table[NA : NA + (extended - 1) * PAIR, :].astype(jnp.float32) * small_ref[basis_count + 1 : basis_count + 2, :]
+    )
+    parts = dot_rows(pieces(small_ref[basis_count + 2 : basis_count + 3, :], 3), weight_ref[3 * channels :, :])
     later_push[...] = jnp.broadcast_to(jnp.sum(parts, axis=0, keepdims=True), later_push.shape)
 
 
 def advance(
     stage,
+    parts_count,
     place_ref,
-    thermal_ref,
     x_ref,
     v_ref,
     g_ref,
@@ -118,13 +117,12 @@
     table,
     message_push,
     later_push,
-    filter_ref,
-    scale_one_ref,
-    mix_ref,
+    weight_ref,
+    small_ref,
     x_out,
     v_out,
     g_out,
-    edge_out,
+    last_out,
     e_rows,
     h_rows,
     lhs_0,
@@ -141,15 +139,13 @@
     extended = own_pairs + 2
     pairs = own_pairs + 1
     total_cells = 2 * own_pairs * place_ref[1]
-    basis_count = filter_ref.shape[0]
-    channels = filter_ref.shape[1]
+    channels = small_ref.shape[1]
+    basis_count = small_ref.shape[0] - SMALL_ROWS
     sub = lax.broadcasted_iota(jnp.int32, (8, PAIR), 0)
     low = lax.broadcasted_iota(jnp.int32, (1, PAIR), 1) < NA
-    span = basis_count - 1
-    order = lax.broadcasted_iota(jnp.int32, (basis_count, 1), 0).astype(jnp.float32) - 0.5 * span
-    filters = filter_ref[...] * jnp.exp(-2.0 * order * order)
+    filters = small_ref[:basis_count, :]
     filters = jnp.concatenate([filters, filters], axis=1)
-    scale_square = scale_one_ref[...] * scale_one_ref[...]
+    scale_square = small_ref[basis_count : basis_count + 1, :]
     scale_square = jnp.concatenate([scale_square, scale_square], axis=1)
 
     if stage == 0:
@@ -161,7 +157,7 @@
         else:
             kinetic = edge_ref[0, 1, 3:4, 0:1] + got_ref[0, 1, 3:4, 0:1]
             mean = kinetic / (3.0 * NA * total_cells.astype(jnp.float32)) + motion_work_lower_limit
-            stretch = jnp.sqrt(thermal_ref[0] / mean)
+            stretch = jnp.sqrt(small_ref[basis_count + 3 : basis_count + 4, 0:1] / mean)
         v = v_ref[...] * stretch
         half_v = v + (0.5 * step_time) * g_ref[...]
         e_rows[1 : own_pairs + 1] = x_ref[...] + step_time * v
@@ -237,7 +233,7 @@
         else:
             at_feat = pl.ds(pl.multiple_of(q * PAIR, PAIR) + NA, PAIR)
             at_push = pl.ds(pl.multiple_of(q * PAIR, PAIR), PAIR)
-        half = 0.5 * dot(message_ref[...], mix_ref[...])
+        half = 0.5 * dot(message_ref[...], weight_ref[channels : 3 * channels, :])
         hidden = (own_feat[at_feat, :].astype(jnp.float32) + (half + half * jnp.tanh(half))).astype(jnp.bfloat16)
         pull = hidden.astype(jnp.float32) * later_push[0:1] + message_push[at_push, :]
         pull = jnp.sum(pull, axis=1, keepdims=True)
@@ -260,10 +256,10 @@
 
     def stage_of(q, t, rows=True, before=True):
         if before:
-            make_force(q - 1, message[(t + 1) % 2], vec[(t + 3) % 4])
-        make_messages(q, lhs[t % 2], vec[t % 4], message[t % 2])
+            make_force(q - 1, message[(t + 1) % 2], vec[(t+1)%2])
+        make_messages(q, lhs[t % 2], vec[t%2], message[t % 2])
         if rows:
-            make_rows(q + 1, lhs[(t + 1) % 2], vec[(t + 1) % 4])
+            make_rows(q + 1, lhs[(t + 1) % 2], vec[(t+1)%2])
 
     make_rows(0, lhs_0, vec_0)
     stage_of(0, 0, before=False)
@@ -296,18 +292,82 @@
     kinetic = jnp.sum(jnp.sum(kinetic, axis=1, keepdims=True), axis=0, keepdims=True)
     x = e_rows[1 : own_pairs + 1]
     if stage < 3:
-        x = x + (0.5 * step_time * step_time) * g
+        x_out[...] = x + (0.5 * step_time * step_time) * g
+        for edge, p in enumerate((0, own_pairs - 1)):
+            last_out[edge, 0] = x_out[p]
+            last_out[edge, 1] = jnp.where(sub == 3, kinetic, v[p])
+        return
     x_out[...] = x
-    for edge, p in enumerate((0, own_pairs - 1)):
-        edge_out[edge, 0] = x[p]
-        edge_out[edge, 1] = jnp.where(sub == 3, kinetic, v[p])
+    rows = jnp.concatenate(
+        [
+            jnp.concatenate([x_out[p, 0:3], v_out[p, 0:3], g_out[p, 0:3]], axis=0)
+            for p in range(own_pairs)
+        ],
+        axis=1,
+    )
+    chunks = last_out.shape[0] // parts_count
+    width = own_pairs * PAIR // chunks
+    whole = width // PAIR
+    last_out[...] = jnp.zeros(last_out.shape, jnp.float32)
+    end = last_out.shape[1] - 1
+    last_out[:, end:, :] = jnp.broadcast_to(kinetic.reshape(1, 1, 1), (last_out.shape[0], 1, PAIR))
+    first = place_ref[0] * chunks
+    for chunk in range(chunks):
+        at = chunk * width
+        for group in range(whole):
+            last_out[first + chunk, 9 * group : 9 * (group + 1), :] = rows[:, at : at + PAIR]
+            at = at + PAIR
+        if width % PAIR:
+            tail = rows[:, at : at + NA]
+            last_out[first + chunk, 9 * whole : 9 * whole + 4, :] = jnp.concatenate([tail[:4], tail[4:8]], axis=1)
+            last_out[first + chunk, 9 * whole + 4 : 9 * whole + 5, :NA] = tail[8:]
+
+
+def finish(place_ref, source_ref, got_ref, thermal_ref, x_out, v_out, g_out):
+    replicas, width = x_out.shape[1:]
+    whole = width // PAIR
+    parts = place_ref[1]
+    domain = place_ref[2]
+    domains, chunk_rows = got_ref.shape[:2]
+    part = domain // (domains // parts)
+    atoms = float(domains * width)
+    group = domains // replicas
+    outs = (x_out, v_out, g_out)
+    pieces_of = [[] for _ in range(9)]
+    factors = []
+    for r in range(replicas):
+        source = source_ref[r]
+        kinetic = got_ref[source * group, chunk_rows - 1 :, :]
+        for other in range(1, group):
+            kinetic = kinetic + got_ref[source * group + other, chunk_rows - 1 :, :]
+        mean = kinetic / (3.0 * atoms) + motion_work_lower_limit
+        source_target = jnp.full((1, PAIR), thermal_ref[source])
+        factors.append(jnp.sqrt(source_target / mean) * jnp.sqrt(jnp.full((1, PAIR), thermal_ref[r]) / source_target))
+        rows = got_ref[source * group + part]
+        for row in range(9):
+            pieces_of[row].append([rows[9 * g + row : 9 * g + row + 1] for g in range(whole)])
+            if width % PAIR:
+                at = 9 * whole + row % 4 if row < 8 else 9 * whole + 4
+                tail = rows[at : at + 1, NA:] if 4 <= row < 8 else rows[at : at + 1, :NA]
+                pieces_of[row][-1].append(tail)
+    factor = jnp.concatenate(factors, axis=0)
+    for row in range(9):
+        for index in range(len(pieces_of[row][0])):
+            value = jnp.concatenate([of_replica[index] for of_replica in pieces_of[row]], axis=0)
+            size = value.shape[1]
+            if row == 2:
+                lane = lax.broadcasted_iota(jnp.int32, value.shape, 1)
+                value = value - (domain * (width // NA) + (index * PAIR + lane) // NA).astype(jnp.float32)
+            elif row // 3 == 1:
+                value = value * factor[:, :size]
+            outs[row // 3][row % 3, :, index * PAIR : index * PAIR + size] = value
 
 
 VMEM_SPEC = pl.BlockSpec(memory_space=pltpu.VMEM)
 SMEM_SPEC = pl.BlockSpec(memory_space=pltpu.SMEM)
 
 
-def run_prepare(place, state, features, per_replica, first, scale_one, later, scale_two, push):
+def run_prepare(place, state, features, per_replica, weights, small):
     atoms, channels = features.shape
     own_pairs = atoms // per_replica // PAIR
     extended = own_pairs + 2
@@ -321,24 +381,24 @@
             jax.ShapeDtypeStruct(((extended - 1) * PAIR, channels), jnp.float32),
             jax.ShapeDtypeStruct((8, channels), jnp.float32),
         ),
-        in_specs=[SMEM_SPEC] + [VMEM_SPEC] * 7,
+        in_specs=[SMEM_SPEC] + [VMEM_SPEC] * 4,
         out_specs=(VMEM_SPEC,) * 6,
         compiler_params=pltpu.CompilerParams(vmem_limit_bytes=20 * 1024 * 1024),
-    )(place, state, features, first, scale_one, later, scale_two, push)
-
-
-def run_advance(stage, place, thermal, x, v, g, edge, got, own_feat, table, message_push, later_push, filters, scale_one, mix):
+    )(place, state, features, weights, small)
+
+
+def run_advance(stage, parts_count, last_shape, place, x, v, g, edge, got, own_feat, table, message_push, later_push, weights, small):
     own_pairs = v.shape[0]
     channels = table.shape[1]
-    basis_count = filters.shape[0]
+    basis_count = small.shape[0] - SMALL_ROWS
     tiles = jax.ShapeDtypeStruct(v.shape, jnp.float32)
     lhs = pltpu.VMEM((basis_count * NA, 3 * PAIR), jnp.bfloat16)
     vec = pltpu.VMEM((3 * NA, 3 * PAIR), jnp.bfloat16)
     message = pltpu.VMEM((PAIR, 2 * channels), jnp.bfloat16)
     return pl.pallas_call(
-        functools.partial(advance, stage),
-        out_shape=(tiles, tiles, tiles, jax.ShapeDtypeStruct((2, 2, 8, PAIR), jnp.float32)),
-        in_specs=[SMEM_SPEC] * 2 + [VMEM_SPEC] * 12,
+        functools.partial(advance, stage, parts_count),
+        out_shape=(tiles, tiles, tiles, jax.ShapeDtypeStruct(last_shape, jnp.float32)),
+        in_specs=[SMEM_SPEC] + [VMEM_SPEC] * 11,
         out_specs=(VMEM_SPEC,) * 4,
         scratch_shapes=[
             pltpu.VMEM((own_pairs + 2, 8, PAIR), jnp.float32),
@@ -354,22 +414,34 @@
             pltpu.VMEM((own_pairs + 2, 3, 8, PAIR), jnp.float32),
         ],
         compiler_params=pltpu.CompilerParams(vmem_limit_bytes=20 * 1024 * 1024),
-    )(place, thermal, x, v, g, edge, got, own_feat, table, message_push, later_push, filters, scale_one, mix)
-
-
-def run_steps(place, thermal, state, features, per_replica, exchange, weights):
-    first, filters, scale_one, mix, later, scale_two, push = weights
-    x, v, *fixed = run_prepare(place, state, features, per_replica, first, scale_one, later, scale_two, push)
-    edge = got = jnp.zeros((2, 2, 8, PAIR), jnp.float32)
+    )(place, x, v, g, edge, got, own_feat, table, message_push, later_push, weights, small)
+
+
+def run_steps(place, state, features, per_replica, chunk_shape, exchange, weights, small):
+    x, v, *fixed = run_prepare(place, state, features, per_replica, weights, small)
+    edge_shape = (2, 2, 8, PAIR)
+    edge = got = jnp.zeros(edge_shape, jnp.float32)
     g = v
     for step in range(STEPS + 1):
         stage = min(step, 2) if step < STEPS else 3
-        x, v, g, edge = run_advance(
-            stage, place, thermal, x, v, g, edge, got, *fixed, filters, scale_one, mix
-        )
+        shape = edge_shape if step < STEPS else chunk_shape
+        x, v, g, edge = run_advance(stage, per_replica, shape, place, x, v, g, edge, got, *fixed, weights, small)
         if step < STEPS:
             got = exchange(edge)
-    return x, v, g, edge[0, 1, 3, 0]
+    return edge
+
+
+def run_finish(place, source, got, thermal_targets, local_atoms):
+    replicas = thermal_targets.shape[0]
+    out = jax.ShapeDtypeStruct((3, replicas, local_atoms), jnp.float32)
+    whole = pl.BlockSpec(out.shape, lambda: (0, 0, 0))
+    outs = pl.pallas_call(
+        finish,
+        out_shape=(out, out, out),
+        in_specs=[SMEM_SPEC, SMEM_SPEC, VMEM_SPEC, SMEM_SPEC],
+        out_specs=(whole, whole, whole),
+    )(place, source, got, thermal_targets)
+    return tuple(jnp.transpose(o, (1, 0, 2)) for o in outs)
 
 
 def on_device(
@@ -400,7 +472,36 @@
     def trade(value, mask):
         return lax.ppermute(value, "dom", [(i, i ^ mask) for i in range(devices)])
 
-    state = jnp.concatenate([particle_places, particle_speeds], axis=1)
+    weights = jnp.concatenate(
+        [initial_signal_projector, invariant_revision_matrix, magnitude_revision_matrix, later_signal_projector], axis=0
+    )
+    span = initial_distance_filter.shape[0] - 1
+    order = (jnp.arange(span + 1, dtype=jnp.float32) - 0.5 * span)[:, None]
+    thermal = lax.dynamic_slice(thermal_targets, (own // per_replica,), (1,))
+    small = jnp.concatenate(
+        [
+            initial_distance_filter * jnp.exp(-2.0 * order * order),
+            (initial_directional_scales * initial_directional_scales)[None],
+            (push_output_matrix * initial_directional_scales)[None],
+            (push_output_matrix * later_directional_scales)[None],
+            jnp.broadcast_to(thermal[:, None], (1, push_output_matrix.shape[0])),
+        ],
+        axis=0,
+    )
+    place = jnp.stack([own % per_replica, jnp.full((), per_replica, own.dtype), own]).astype(jnp.int32)
+    ladder_slot = jnp.arange(replicas, dtype=jnp.int32)
+    source = jnp.where(swap_approval_flags > 0, swap_counterpart_slot, ladder_slot)
+
+    atom_cell = jnp.arange(local_atoms, dtype=jnp.int32) // NA
+    cell_floor = jnp.array([0.0, 0.0, 1.0], jnp.float32)[:, None] * (
+        own * local_cells + atom_cell
+    ).astype(jnp.float32)
+    state = jnp.concatenate([particle_places - cell_floor, particle_speeds], axis=1)
+    upper_part = lax.reduce_precision(state, 8, 7)
+    state = jnp.stack([upper_part, state - upper_part], axis=1).astype(jnp.bfloat16)
+    channels = element_features.shape[1]
+    state = state.reshape(replicas, -1, channels)
+    state_rows = state.shape[1]
     features = element_features
     for level in range(bits):
         mask = devices >> (level + 1)
@@ -411,28 +512,21 @@
             send = jnp.where(upper, state[:half], state[half:])
         else:
             keep = send = state
-        got = trade(send, mask)
-        got_features = trade(features, mask)
+        message = jnp.concatenate([features.reshape(-1, channels), send.reshape(-1, channels)], axis=0)
+        if level == 1:
+            message, weights, small, place, source = lax.optimization_barrier((message, weights, small, place, source))
+        got = trade(message, mask)
+        count = features.size // channels
+        got_features = got[:count].reshape(features.shape)
+        got = got[count:].reshape(send.shape)
         axis = 1 + level
         state = jnp.stack([jnp.where(upper, got, keep), jnp.where(upper, keep, got)], axis=axis)
         features = jnp.stack(
             [jnp.where(upper, got_features, features), jnp.where(upper, features, got_features)], axis=level
         )
-        if level + 1 < bits:
-            state, features = lax.optimization_barrier((state, features))
-    state = state.reshape(devices, 6, local_atoms).transpose(1, 0, 2).reshape(6, devices * local_atoms)
+    state = state.reshape(devices, 2, 6, local_atoms).astype(jnp.float32)
+    state = (state[:, 0] + state[:, 1]).transpose(1, 0, 2).reshape(6, devices * local_atoms)
     features = features.reshape(devices * local_atoms, -1)
-    thermal = lax.dynamic_slice(thermal_targets, (own // per_replica,), (1,))
-    place = jnp.stack([own % per_replica, jnp.full((), per_replica, own.dtype)]).astype(jnp.int32)
-    weights = (
-        initial_signal_projector,
-        initial_distance_filter,
-        initial_directional_scales[None],
-        jnp.concatenate([invariant_revision_matrix, magnitude_revision_matrix], axis=0),
-        later_signal_projector,
-        later_directional_scales[None],
-        push_output_matrix[None],
-    )
 
     def exchange(edge):
         if per_replica == 2:
@@ -444,48 +538,11 @@
         after = lax.ppermute(edge[0], "dom", [(b, a) for a, b in up])
         return jnp.stack([after.at[1, 3].set(kinetic), before])
 
-    x, v, g, kinetic = run_steps(place, thermal, state, features, per_replica, exchange, weights)
-
-    state = jnp.stack([x, v, g])[:, :, :3].transpose(0, 2, 1, 3).reshape(9, -1)
-    state = jnp.concatenate([state, jnp.broadcast_to(kinetic, (1, state.shape[1]))], axis=0)[:, None]
-    for level in range(replica_bits, bits):
-        mask = devices >> (level + 1)
-        upper = (own & mask) > 0
-        got = trade(state, mask)
-        state = jnp.stack([jnp.where(upper, got, state), jnp.where(upper, state, got)], axis=1 + level - replica_bits)
-        state = state.reshape((10,) + (2,) * (level + 1 - replica_bits) + (-1,))
-    state = state.reshape(10, per_replica, -1)
-    kinetic = jnp.sum(state[9, :, 0])
-    stretch = jnp.sqrt(thermal[0] / (kinetic / (3.0 * devices * local_atoms) + motion_work_lower_limit))
-    factor = jnp.where((jnp.arange(9) // 3) == 1, stretch, 1.0)
-    state = state[:9] * factor[:, None, None]
-
-    state = state.reshape(9, replicas, per_replica, local_atoms)
-    state = lax.dynamic_index_in_dim(state, own % per_replica, 2, keepdims=False)
-    state = state.transpose(1, 0, 2)[:, None]
-    for level in range(replica_bits):
-        mask = devices >> (level + 1)
-        upper = (own & mask) > 0
-        half = state.shape[0] // 2
-        keep = jnp.where(upper, state[half:], state[:half])
-        send = jnp.where(upper, state[:half], state[half:])
-        got = trade(send, mask)
-        state = jnp.stack([jnp.where(upper, got, keep), jnp.where(upper, keep, got)], axis=1 + level)
-    state = state.reshape(replicas, 3, 3, local_atoms)
-
-    ladder_slot = jnp.arange(replicas, dtype=jnp.int32)
-    source = jnp.where(swap_approval_flags > 0, swap_counterpart_slot, ladder_slot)
-    chosen = source[:, None] == ladder_slot[None, :]
-    state = jnp.sum(jnp.where(chosen[:, :, None, None, None], state[None], 0.0), axis=1)
-    thermal_source = jnp.sum(jnp.where(chosen, thermal_targets[None, :], 0.0), axis=1)
-    thermal_ratio = jnp.sqrt(thermal_targets / thermal_source)
-    atom_cell = (own * local_cells + jnp.arange(local_atoms, dtype=jnp.int32) // NA).astype(jnp.float32)
-    cell_floor = jnp.array([0.0, 0.0, 1.0], jnp.float32)[:, None] * atom_cell[None, :]
-    return (
-        state[:, 0] - cell_floor[None],
-        state[:, 1] * thermal_ratio[:, None, None],
-        state[:, 2],
-    )
+    chunk_rows = 9 * (local_atoms // PAIR) + (5 if local_atoms % PAIR else 0) + 1
+    chunk_rows = -(-chunk_rows // 8) * 8
+    chunks = run_steps(place, state, features, per_replica, (devices, chunk_rows, PAIR), exchange, weights, small)
+    got = lax.all_to_all(chunks, "dom", 0, 0)
+    return run_finish(place, source, got, thermal_targets, local_atoms)
 
 
 def solution(mesh):

time: 102 us -> 83.5 us (0.82)
  blocking collectives: 0 us -> 13.6 us
  waiting for transfers between devices: 28.5 us -> 15.1 us
  Pallas kernels: 46.1 us -> 39.9 us
  starting transfers between devices: 13.2 us -> 7.29 us
  local copies, waits for them, and re-layouts: 7.71 us -> 3.84 us
  between operations: 2.5 us -> 1.19 us
    all_to_all x0 -> x1, blocking collectives: none -> 13.6 us  [on_device(): got = lax.all_to_all(chunks, 'dom', 0, 0)]
    ppermute x16 -> x8, waiting for transfers between devices: 28.5 us -> 15.1 us  [trade(): return lax.ppermute(value, 'dom', [(i, i ^ mask) for i in range(devices)])]
    pallas_call x5 -> x6, Pallas kernels: 45.3 us -> 39.1 us  [the longest x5 37.4 us: run_advance(): pl.pallas_call(functools.partial(advance, stage, parts_count), out_shape=...]
    ppermute x16 -> x8, starting transfers between devices: 13.2 us -> 7.29 us  [trade(): return lax.ppermute(value, 'dom', [(i, i ^ mask) for i in range(devices)])]
    unnamed x36 -> x30, local copies, waits for them, and re-layouts: 5.17 us -> 1.83 us
    reduce_sum x3 -> x0, other arithmetic: 1.04 us -> none  [the longest x1 0.6 us: on_device(): kinetic = jnp.sum(state[9, :, 0])]
  transfers between devices with their start and end apart: 16 -> 8, of which waited for: 14 -> 8; matrix products, arithmetic and copies ran while one was open for 2% -> 3% of each run, Pallas kernels for 0% -> 0%
where the time goes in v3:
time: 83.5 us; the launch traced here: 83.1 us
  Pallas kernels  39.9 us (48%)
  waiting for transfers between devices  15.1 us (18%)
  blocking collectives  13.6 us (16%)
  starting transfers between devices  7.29 us (9%)
  local copies, waits for them, and re-layouts  3.84 us (5%)
  other arithmetic  2.17 us (3%)
  between operations  1.19 us (1%)
    pallas_call x5, Pallas kernels, run_advance(): pl.pallas_call(functools.partial(advance, stage, parts_count), out_shape=...  37.4 us
    ppermute x8, waiting for transfers between devices, trade(): return lax.ppermute(value, 'dom', [(i, i ^ mask) for i in range(devices)])  15.1 us
    all_to_all x1, blocking collectives, on_device(): got = lax.all_to_all(chunks, 'dom', 0, 0)  13.6 us
    ppermute x8, starting transfers between devices, trade(): return lax.ppermute(value, 'dom', [(i, i ^ mask) for i in range(devices)])  7.29 us
    unnamed x30, local copies, waits for them, and re-layouts  1.83 us
    pallas_call x1, Pallas kernels, run_finish(): pl.pallas_call(finish, out_shape=(out, out, out), in_specs=[SMEM_SPEC, SM...  1.71 us
  transfers between devices with their start and end apart: 8, of which 8 were waited for; matrix products, arithmetic and copies ran while one was open for 3% of the time, Pallas kernels for 0%

profile of v3, /device:TPU:0, one launch (start us, length us, event | category | flops | bytes accessed | tf_op | source)
XLA Modules:
  0.0 83.1 jit_solution(16883361326305483914)
XLA Ops:
  0.7 0.6 copy-done.12
  1.4 0.7 subtract_bitcast_fusion
  2.3 0.7 copy-done.1
  3.0 4.0 %collective-permute-start = (bf16[264,128]{1,0:T(8,128)(2,1)S(1)}, bf16[264,128]{1,0:T(8,128)(2,1)S(1)}, u32[]{:S(2)}, u32[]{:S(2)}) collective-permute-start(bf16[264,128]{1,0:T(8,128)(2,1)S(1)} %pad_maximum_fusion.11), channel_id=1, source_target_pairs={{0,8},{1,9},{2,10},{3,11},{4,12},{5,13},{6,14},{7,15},{8,0},{9,1},... | collective-permute-start | bytes 202760 | tf_op jit(solution)/shard_map/ppermute | solution.py:473
  7.8 0.6 dynamic_slice.3
  9.0 0.6 broadcast_in_dim.28
  9.8 1.0 %collective-permute-done = bf16[264,128]{1,0:T(8,128)(2,1)S(1)} collective-permute-done((bf16[264,128]{1,0:T(8,128)(2,1)S(1)}, bf16[264,128]{1,0:T(8,128)(2,1)S(1)}, u32[]{:S(2)}, u32[]{:S(2)}) %collective-permute-start) | collective-permute-done | bytes 67616 | tf_op jit(solution)/shard_map/ppermute | solution.py:473
  10.9 0.7 collective-permute-start.1
  11.6 4.2 %collective-permute-done.1 = bf16[456,128]{1,0:T(8,128)(2,1)S(1)} collective-permute-done((bf16[456,128]{1,0:T(8,128)(2,1)S(1)}, bf16[456,128]{1,0:T(8,128)(2,1)S(1)}, u32[]{:S(2)}, u32[]{:S(2)}) %collective-permute-start.1) | collective-permute-done | bytes 116768 | tf_op jit(solution)/shard_map/ppermute | solution.py:473
  16.0 1.8 %collective-permute-start.2 = (bf16[840,128]{1,0:T(8,128)(2,1)S(1)}, bf16[840,128]{1,0:T(8,128)(2,1)S(1)}, u32[]{:S(2)}, u32[]{:S(2)}) collective-permute-start(bf16[840,128]{1,0:T(8,128)(2,1)S(1)} %pad_maximum_fusion.4), channel_id=1, source_target_pairs={{0,2},{1,3},{2,0},{3,1},{4,6},{5,7},{6,4},{7,5},{8,10},{9,11},{10,... | collective-permute-start | bytes 645128 | tf_op jit(solution)/shard_map/ppermute | solution.py:473
  17.8 4.1 %collective-permute-done.2 = bf16[840,128]{1,0:T(8,128)(2,1)S(1)} collective-permute-done((bf16[840,128]{1,0:T(8,128)(2,1)S(1)}, bf16[840,128]{1,0:T(8,128)(2,1)S(1)}, u32[]{:S(2)}, u32[]{:S(2)}) %collective-permute-start.2) | collective-permute-done | bytes 215072 | tf_op jit(solution)/shard_map/ppermute | solution.py:473
  22.4 1.7 %collective-permute-done.3 = bf16[1680,128]{1,0:T(8,128)(2,1)S(1)} collective-permute-done((bf16[1680,128]{1,0:T(8,128)(2,1)S(1)}, bf16[1680,128]{1,0:T(8,128)(2,1)S(1)}, u32[]{:S(2)}, u32[]{:S(2)}) %collective-permute-start.3) | collective-permute-done | bytes 430112 | tf_op jit(solution)/shard_map/ppermute | solution.py:473
  24.8 0.8 %shard_map.166 = (f32[14,8,128]{2,1,0:T(8,128)S(1)}, f32[12,8,128]{2,1,0:T(8,128)S(1)}, bf16[1792,128]{1,0:T(8,128)(2,1)S(1)}, bf16[1792,128]{1,0:T(8,128)(2,1)S...) custom-call(s32[3]{0:T(128)S(1)} %pad_add_fusion.place_ref, f32[6,3072]{1,0:T(8,128)S(1)} %reshape.690.state_ref, ...), custom_call_target="tpu_custom_call" | custom-call | tf_op jit(solution)/shard_map/pallas_call | solution.py:374
  25.6 7.4 %shard_map.167 = (f32[12,8,128]{2,1,0:T(8,128)S(1)}, f32[12,8,128]{2,1,0:T(8,128)S(1)}, f32[12,8,128]{2,1,0:T(8,128)S(1)}, f32[2,2,8,128]{3,2,1,0:T(8,128)S(1)}) custom-call(s32[3]{0:T(128)S(1)} %pad_add_fusion.place_ref, f32[14,8,128]{2,1,0:T(8,128)S(1)} %get-tuple-element.39.x_ref, f32[12,8,128]{2,1,0:T(8,128)S(1)} %get-tuple-element.40.v_ref.g_ref, ...), custom_call_target="tpu_custom_call" | custom-call | tf_op jit(solution)/shard_map/pallas_call | solution.py:398
  33.2 1.0 %collective-permute-done.4.got_ref = f32[2,2,8,128]{3,2,1,0:T(8,128)S(1)} collective-permute-done((f32[2,2,8,128]{3,2,1,0:T(8,128)S(1)}, f32[2,2,8,128]{3,2,1,0:T(8,128)S(1)}, u32[]{:S(2)}, u32[]{:S(2)}) %collective-permute-start.4) | collective-permute-done | bytes 16416 | tf_op jit(solution)/shard_map/ppermute | solution.py:473
  34.2 7.3 %shard_map.168 = (f32[12,8,128]{2,1,0:T(8,128)S(1)}, f32[12,8,128]{2,1,0:T(8,128)S(1)}, f32[12,8,128]{2,1,0:T(8,128)S(1)}, f32[2,2,8,128]{3,2,1,0:T(8,128)S(1)}) custom-call(s32[3]{0:T(128)S(1)} %pad_add_fusion.place_ref, f32[12,8,128]{2,1,0:T(8,128)S(1)} %get-tuple-element.45.x_ref, f32[12,8,128]{2,1,0:T(8,128)S(1)} %get-tuple-element.46.v_ref, ...), custom_call_target="tpu_custom_call" | custom-call | tf_op jit(solution)/shard_map/pallas_call | solution.py:398
  41.7 1.0 %collective-permute-done.5.got_ref = f32[2,2,8,128]{3,2,1,0:T(8,128)S(1)} collective-permute-done((f32[2,2,8,128]{3,2,1,0:T(8,128)S(1)}, f32[2,2,8,128]{3,2,1,0:T(8,128)S(1)}, u32[]{:S(2)}, u32[]{:S(2)}) %collective-permute-start.5) | collective-permute-done | bytes 16416 | tf_op jit(solution)/shard_map/ppermute | solution.py:473
  42.7 7.4 %shard_map.169 = (f32[12,8,128]{2,1,0:T(8,128)S(1)}, f32[12,8,128]{2,1,0:T(8,128)S(1)}, f32[12,8,128]{2,1,0:T(8,128)S(1)}, f32[2,2,8,128]{3,2,1,0:T(8,128)S(1)}) custom-call(s32[3]{0:T(128)S(1)} %pad_add_fusion.place_ref, f32[12,8,128]{2,1,0:T(8,128)S(1)} %get-tuple-element.49.x_ref, f32[12,8,128]{2,1,0:T(8,128)S(1)} %get-tuple-element.50.v_ref, ...), custom_call_target="tpu_custom_call" | custom-call | tf_op jit(solution)/shard_map/pallas_call | solution.py:398
  50.3 1.0 %collective-permute-done.6.got_ref = f32[2,2,8,128]{3,2,1,0:T(8,128)S(1)} collective-permute-done((f32[2,2,8,128]{3,2,1,0:T(8,128)S(1)}, f32[2,2,8,128]{3,2,1,0:T(8,128)S(1)}, u32[]{:S(2)}, u32[]{:S(2)}) %collective-permute-start.6) | collective-permute-done | bytes 16416 | tf_op jit(solution)/shard_map/ppermute | solution.py:473
  51.3 7.4 %shard_map.170 = (f32[12,8,128]{2,1,0:T(8,128)S(1)}, f32[12,8,128]{2,1,0:T(8,128)S(1)}, f32[12,8,128]{2,1,0:T(8,128)S(1)}, f32[2,2,8,128]{3,2,1,0:T(8,128)S(1)}) custom-call(s32[3]{0:T(128)S(1)} %pad_add_fusion.place_ref, f32[12,8,128]{2,1,0:T(8,128)S(1)} %get-tuple-element.53.x_ref, f32[12,8,128]{2,1,0:T(8,128)S(1)} %get-tuple-element.54.v_ref, ...), custom_call_target="tpu_custom_call" | custom-call | tf_op jit(solution)/shard_map/pallas_call | solution.py:398
  58.8 1.0 %collective-permute-done.7.got_ref = f32[2,2,8,128]{3,2,1,0:T(8,128)S(1)} collective-permute-done((f32[2,2,8,128]{3,2,1,0:T(8,128)S(1)}, f32[2,2,8,128]{3,2,1,0:T(8,128)S(1)}, u32[]{:S(2)}, u32[]{:S(2)}) %collective-permute-start.7) | collective-permute-done | bytes 16416 | tf_op jit(solution)/shard_map/ppermute | solution.py:473
  59.9 7.9 %shard_map.171 = (f32[12,8,128]{2,1,0:T(8,128)}, f32[12,8,128]{2,1,0:T(8,128)}, f32[12,8,128]{2,1,0:T(8,128)}, f32[16,16,128]{2,1,0:T(8,128)S(1)}) custom-call(s32[3]{0:T(128)S(1)} %pad_add_fusion.place_ref, f32[12,8,128]{2,1,0:T(8,128)S(1)} %get-tuple-element.57.x_ref, f32[12,8,128]{2,1,0:T(8,128)S(1)} %get-tuple-element.58.v_ref, ...), custom_call_target="tpu_custom_call" | custom-call | tf_op jit(solution)/shard_map/pallas_call | solution.py:398
  67.8 13.6 %all_to_all.5.got_ref = f32[16,16,128]{2,1,0:T(8,128)} all-to-all(f32[16,16,128]{2,1,0:T(8,128)S(1)} %get-tuple-element.61), channel_id=1, replica_groups=mesh['groups'=2,'dom'=16] {'dom'}, dimensions={0} | all-to-all | bytes 262144 | tf_op jit(solution)/shard_map/all_to_all | solution.py:544
  81.4 1.7 %shard_map.172 = (f32[3,8,192]{2,1,0:T(8,128)}, f32[3,8,192]{2,1,0:T(8,128)}, f32[3,8,192]{2,1,0:T(8,128)}) custom-call(s32[3]{0:T(128)} %copy-done, s32[8]{0:T(128)} %compare_select_fusion.source_ref, f32[16,16,128]{2,1,0:T(8,128)} %all_to_all.5.got_ref, f32[8]{0:T(128)} %thermal_ref.1), custom_call_target="tpu_custom_call" | custom-call | tf_op jit(solution)/shard_map/pallas_call | solution.py:438
  (98 shorter events, 3.5 us)
Async XLA Ops:
  0.6 0.7 copy-start.12
  1.4 0.8 copy-start.6
  2.2 0.8 copy-start.1
  3.0 7.7 %collective-permute-start = (bf16[264,128]{1,0:T(8,128)(2,1)S(1)}, bf16[264,128]{1,0:T(8,128)(2,1)S(1)}, u32[]{:S(2)}, u32[]{:S(2)}) collective-permute-start(bf16[264,128]{1,0:T(8,128)(2,1)S(1)} %pad_maximum_fusion.11), channel_id=1, source_target_pairs={{0,8},{1,9},{2,10},{3,11},{4,12},{5,13},{6,14},{7,15},{8,0},{9,1},... | collective-permute-start | bytes 202760 | tf_op jit(solution)/shard_map/ppermute | solution.py:473
  7.0 0.7 copy-start.7
  7.0 0.8 copy-start.8
  7.1 1.3 %copy-start.13 = (s32[8]{0:T(128)S(1)}, s32[8]{0:T(128)}, u32[]{:S(2)}) copy-start(s32[8]{0:T(128)} %param.19) | copy-start | bytes 100
  7.1 1.3 %copy-start.14 = (s32[8]{0:T(128)S(1)}, s32[8]{0:T(128)}, u32[]{:S(2)}) copy-start(s32[8]{0:T(128)} %param.20) | copy-start | bytes 100
  7.1 1.9 %copy-start.9 = (f32[128]{0:T(128)S(1)}, f32[128]{0:T(128)}, u32[]{:S(2)}) copy-start(f32[128]{0:T(128)} %param.28) | copy-start | bytes 1540
  7.1 1.8 %copy-start.10 = (f32[128]{0:T(128)S(1)}, f32[128]{0:T(128)}, u32[]{:S(2)}) copy-start(f32[128]{0:T(128)} %param.27) | copy-start | bytes 1540
  7.1 1.8 %copy-start.11 = (f32[128]{0:T(128)S(1)}, f32[128]{0:T(128)}, u32[]{:S(2)}) copy-start(f32[128]{0:T(128)} %param.23) | copy-start | bytes 1540
  7.1 1.8 %copy-start.4 = (bf16[128,128]{1,0:T(8,128)(2,1)S(1)}, bf16[128,128]{1,0:T(8,128)(2,1)}, u32[]{:S(2)}) copy-start(bf16[128,128]{1,0:T(8,128)(2,1)} %param.24) | copy-start | bytes 98308
  7.1 1.8 %copy-start.5 = (bf16[128,128]{1,0:T(8,128)(2,1)S(1)}, bf16[128,128]{1,0:T(8,128)(2,1)}, u32[]{:S(2)}) copy-start(bf16[128,128]{1,0:T(8,128)(2,1)} %param.21) | copy-start | bytes 98308
  7.2 1.8 %copy-start.2 = (bf16[128,128]{1,0:T(8,128)(2,1)S(1)}, bf16[128,128]{1,0:T(8,128)(2,1)}, u32[]{:S(2)}) copy-start(bf16[128,128]{1,0:T(8,128)(2,1)} %param.26) | copy-start | bytes 98308
  7.2 1.8 %copy-start.3 = (bf16[128,128]{1,0:T(8,128)(2,1)S(1)}, bf16[128,128]{1,0:T(8,128)(2,1)}, u32[]{:S(2)}) copy-start(bf16[128,128]{1,0:T(8,128)(2,1)} %param.25) | copy-start | bytes 98308
  9.8 50.1 %copy-start = (s32[3]{0:T(128)}, s32[3]{0:T(128)S(1)}, u32[]{:S(2)}) copy-start(s32[3]{0:T(128)S(1)} %pad_add_fusion.place_ref) | copy-start | bytes 40
  10.9 4.9 %collective-permute-start.1 = (bf16[456,128]{1,0:T(8,128)(2,1)S(1)}, bf16[456,128]{1,0:T(8,128)(2,1)S(1)}, u32[]{:S(2)}, u32[]{:S(2)}) collective-permute-start(bf16[456,128]{1,0:T(8,128)(2,1)S(1)} %pad_maximum_fusion.8), channel_id=1, source_target_pairs={{0,4},{1,5},{2,6},{3,7},{4,0},{5,1},{6,2},{7,3},{8,12},{9,13},{10,... | collective-permute-start | bytes 350216 | tf_op jit(solution)/shard_map/ppermute | solution.py:473
  16.0 5.9 %collective-permute-start.2 = (bf16[840,128]{1,0:T(8,128)(2,1)S(1)}, bf16[840,128]{1,0:T(8,128)(2,1)S(1)}, u32[]{:S(2)}, u32[]{:S(2)}) collective-permute-start(bf16[840,128]{1,0:T(8,128)(2,1)S(1)} %pad_maximum_fusion.4), channel_id=1, source_target_pairs={{0,2},{1,3},{2,0},{3,1},{4,6},{5,7},{6,4},{7,5},{8,10},{9,11},{10,... | collective-permute-start | bytes 645128 | tf_op jit(solution)/shard_map/ppermute | solution.py:473
  22.3 1.8 %collective-permute-start.3 = (bf16[1680,128]{1,0:T(8,128)(2,1)S(1)}, bf16[1680,128]{1,0:T(8,128)(2,1)S(1)}, u32[]{:S(2)}, u32[]{:S(2)}) collective-permute-start(bf16[1680,128]{1,0:T(8,128)(2,1)S(1)} %pad_maximum_fusion.1), channel_id=1, source_target_pairs={{0,1},{1,0},{2,3},{3,2},{4,5},{5,4},{6,7},{7,6},{8,9},{9,8},{10,11... | collective-permute-start | bytes 1290248 | tf_op jit(solution)/shard_map/ppermute | solution.py:473
  33.0 1.2 %collective-permute-start.4 = (f32[2,2,8,128]{3,2,1,0:T(8,128)S(1)}, f32[2,2,8,128]{3,2,1,0:T(8,128)S(1)}, u32[]{:S(2)}, u32[]{:S(2)}) collective-permute-start(f32[2,2,8,128]{3,2,1,0:T(8,128)S(1)} %get-tuple-element.48.edge_ref), channel_id=1, source_target_pairs={{0,1},{1,0},{2,3},{3,2},{4,5},{5,4},{6,7},{7,6},{8,9},{9,8},{10,11... | collective-permute-start | bytes 49160 | tf_op jit(solution)/shard_map/ppermute | solution.py:473
  41.5 1.2 %collective-permute-start.5 = (f32[2,2,8,128]{3,2,1,0:T(8,128)S(1)}, f32[2,2,8,128]{3,2,1,0:T(8,128)S(1)}, u32[]{:S(2)}, u32[]{:S(2)}) collective-permute-start(f32[2,2,8,128]{3,2,1,0:T(8,128)S(1)} %get-tuple-element.52.edge_ref), channel_id=1, source_target_pairs={{0,1},{1,0},{2,3},{3,2},{4,5},{5,4},{6,7},{7,6},{8,9},{9,8},{10,11... | collective-permute-start | bytes 49160 | tf_op jit(solution)/shard_map/ppermute | solution.py:473
  50.1 1.2 %collective-permute-start.6 = (f32[2,2,8,128]{3,2,1,0:T(8,128)S(1)}, f32[2,2,8,128]{3,2,1,0:T(8,128)S(1)}, u32[]{:S(2)}, u32[]{:S(2)}) collective-permute-start(f32[2,2,8,128]{3,2,1,0:T(8,128)S(1)} %get-tuple-element.56.edge_ref), channel_id=1, source_target_pairs={{0,1},{1,0},{2,3},{3,2},{4,5},{5,4},{6,7},{7,6},{8,9},{9,8},{10,11... | collective-permute-start | bytes 49160 | tf_op jit(solution)/shard_map/ppermute | solution.py:473
  58.7 1.2 %collective-permute-start.7 = (f32[2,2,8,128]{3,2,1,0:T(8,128)S(1)}, f32[2,2,8,128]{3,2,1,0:T(8,128)S(1)}, u32[]{:S(2)}, u32[]{:S(2)}) collective-permute-start(f32[2,2,8,128]{3,2,1,0:T(8,128)S(1)} %get-tuple-element.60.edge_ref), channel_id=1, source_target_pairs={{0,1},{1,0},{2,3},{3,2},{4,5},{5,4},{6,7},{7,6},{8,9},{9,8},{10,11... | collective-permute-start | bytes 49160 | tf_op jit(solution)/shard_map/ppermute | solution.py:473

commit v4 on v3

--- a/solution.py
+++ b/solution.py
@@ -12,7 +12,9 @@
 PAIR = 2 * NA
 STEPS = 4
 UNROLL = 2
-SMALL_ROWS = 4
+SMALL_ROWS = 7
+CHUNK = 16
+CHUNKS = NA // CHUNK
 
 step_time = 0.05
 motion_work_lower_limit = 1e-06
@@ -107,7 +109,6 @@
 def advance(
     stage,
     parts_count,
-    place_ref,
     x_ref,
     v_ref,
     g_ref,
@@ -125,12 +126,8 @@
     last_out,
     e_rows,
     h_rows,
-    lhs_0,
-    lhs_1,
-    vec_0,
-    vec_1,
-    vec_2,
-    vec_3,
+    lhs,
+    vec,
     message_0,
     message_1,
     forces,
@@ -138,7 +135,7 @@
     own_pairs = v_ref.shape[0]
     extended = own_pairs + 2
     pairs = own_pairs + 1
-    total_cells = 2 * own_pairs * place_ref[1]
+    total_cells = float(2 * own_pairs * parts_count)
     channels = small_ref.shape[1]
     basis_count = small_ref.shape[0] - SMALL_ROWS
     sub = lax.broadcasted_iota(jnp.int32, (8, PAIR), 0)
@@ -156,77 +153,70 @@
             stretch = jnp.ones((1, 1), jnp.float32)
         else:
             kinetic = edge_ref[0, 1, 3:4, 0:1] + got_ref[0, 1, 3:4, 0:1]
-            mean = kinetic / (3.0 * NA * total_cells.astype(jnp.float32)) + motion_work_lower_limit
+            mean = kinetic / (3.0 * NA * total_cells) + motion_work_lower_limit
             stretch = jnp.sqrt(small_ref[basis_count + 3 : basis_count + 4, 0:1] / mean)
         v = v_ref[...] * stretch
         half_v = v + (0.5 * step_time) * g_ref[...]
         e_rows[1 : own_pairs + 1] = x_ref[...] + step_time * v
-        z_shift = jnp.where(sub == 2, total_cells.astype(jnp.float32), 0.0)
+        z_only = jnp.where(sub == 2, 1.0, 0.0)
         left = got_ref[1, 0] + (step_time * stretch) * got_ref[1, 1]
         right = got_ref[0, 0] + (step_time * stretch) * got_ref[0, 1]
-        e_rows[0] = jnp.where(place_ref[0] == 0, left - z_shift, left)
-        e_rows[extended - 1] = jnp.where(place_ref[0] == place_ref[1] - 1, right + z_shift, right)
+        e_rows[0] = left + z_only * small_ref[basis_count + 4 : basis_count + 5, :]
+        e_rows[extended - 1] = right + z_only * small_ref[basis_count + 5 : basis_count + 6, :]
     h_rows[...] = swap_halves(e_rows[0:pairs], e_rows[1:extended])
 
     blank = jnp.zeros((PAIR, channels), jnp.bfloat16)
-    lhs, vec = (lhs_0, lhs_1), (vec_0, vec_1, vec_2, vec_3)
+    def beside(value):
+        return jnp.concatenate([value, jnp.zeros_like(value)], axis=1)
+
     message = (message_0, message_1)
 
-    def make_rows(q, radial, vectors_ref):
-        columns = jnp.transpose(h_rows[q])
+    def make_rows(q, chunk, columns, out):
         before = e_rows[q]
         after = e_rows[q + 1]
         across = jnp.where(low, after, before)
-        for chunk in range(NA // 16):
-            start = chunk * 16
-            own_a = [columns[start : start + 16, c : c + 1] for c in range(3)]
-            own_b = [columns[NA + start : NA + start + 16, c : c + 1] for c in range(3)]
-            own_a = [jnp.broadcast_to(o, (16, PAIR)) for o in own_a]
-            own_b = [jnp.broadcast_to(o, (16, PAIR)) for o in own_b]
-            blocks = (
-                [before[c : c + 1] - own_a[c] for c in range(3)],
-                [after[c : c + 1] - own_b[c] for c in range(3)],
-                [across[c : c + 1] - jnp.where(low, own_a[c], own_b[c]) for c in range(3)],
-            )
-            for block, displacement in enumerate(blocks):
-                radials, vectors = basis(displacement, basis_count)
-                at = slice(block * PAIR, (block + 1) * PAIR)
-                for k, value in enumerate(radials):
-                    radial[k * NA + start : k * NA + start + 16, at] = value.astype(jnp.bfloat16)
-                for c, value in enumerate(vectors):
-                    vectors_ref[c * NA + start : c * NA + start + 16, at] = value.astype(jnp.bfloat16)
-
-    def make_messages(q, radial, vectors_ref, out):
+        start = chunk * CHUNK
+        own_a = [columns[start : start + CHUNK, c : c + 1] for c in range(3)]
+        own_b = [columns[NA + start : NA + start + CHUNK, c : c + 1] for c in range(3)]
+        own_a = [jnp.broadcast_to(o, (CHUNK, PAIR)) for o in own_a]
+        own_b = [jnp.broadcast_to(o, (CHUNK, PAIR)) for o in own_b]
+        blocks = (
+            [before[c : c + 1] - own_a[c] for c in range(3)],
+            [after[c : c + 1] - own_b[c] for c in range(3)],
+            [across[c : c + 1] - jnp.where(low, own_a[c], own_b[c]) for c in range(3)],
+        )
+        for block, displacement in enumerate(blocks):
+            radials, vectors = basis(displacement, basis_count)
+            for k, value in enumerate(radials + vectors):
+                out[block][k * NA + start : k * NA + start + CHUNK, :] = value.astype(jnp.bfloat16)
+
+    def make_messages(q, rows, out):
         if isinstance(q, int):
             near = table[q * PAIR : (q + 2) * PAIR, :]
         else:
             near = table[pl.ds(pl.multiple_of(q * PAIR, PAIR), 2 * PAIR), :]
-        signals = jnp.concatenate(
+        across = jnp.concatenate(
             [
-                jnp.concatenate([near[:PAIR], blank], axis=1),
-                jnp.concatenate([blank, near[PAIR:]], axis=1),
                 jnp.concatenate([near[PAIR : 3 * NA], blank[:NA]], axis=1),
                 jnp.concatenate([blank[:NA], near[NA:PAIR]], axis=1),
             ],
             axis=0,
         )
-        sums = dot(vectors_ref[...], signals)
-        norm = sums[:NA] * sums[:NA]
-        for c in range(1, 3):
-            part = sums[c * NA : (c + 1) * NA]
-            norm = norm + part * part
-        norm = (norm * scale_square).astype(jnp.bfloat16)
-        sums = dot(radial[...], signals)
-        scalar = sums[:NA] * filters[0:1]
-        for k in range(1, basis_count):
-            scalar = scalar + sums[k * NA : (k + 1) * NA] * filters[k : k + 1]
-        scalar = scalar.astype(jnp.bfloat16)
+        shared = dot(rows[2][...], across)
         for own in range(2):
             at = slice(own * channels, (own + 1) * channels)
-            out[own * NA : (own + 1) * NA, :channels] = scalar[:, at]
-            out[own * NA : (own + 1) * NA, channels:] = norm[:, at]
-
-    def make_force(q, message_ref, vectors_ref):
+            total = dot(rows[own][...], near[own * PAIR : (own + 1) * PAIR]) + shared[:, at]
+            total = [total[k * NA : (k + 1) * NA] for k in range(basis_count + 3)]
+            scalar = total[0] * filters[0:1, :channels]
+            for k in range(1, basis_count):
+                scalar = scalar + total[k] * filters[k : k + 1, :channels]
+            norm = total[basis_count] * total[basis_count]
+            for k in range(basis_count + 1, basis_count + 3):
+                norm = norm + total[k] * total[k]
+            out[own * NA : (own + 1) * NA, :channels] = scalar.astype(jnp.bfloat16)
+            out[own * NA : (own + 1) * NA, channels:] = (norm * scale_square[:, :channels]).astype(jnp.bfloat16)
+
+    def make_pull(q, message_ref):
         if isinstance(q, int):
             at_feat = slice(NA + q * PAIR, NA + (q + 1) * PAIR)
             at_push = slice(q * PAIR, (q + 1) * PAIR)
@@ -236,46 +226,56 @@
         half = 0.5 * dot(message_ref[...], weight_ref[channels : 3 * channels, :])
         hidden = (own_feat[at_feat, :].astype(jnp.float32) + (half + half * jnp.tanh(half))).astype(jnp.bfloat16)
         pull = hidden.astype(jnp.float32) * later_push[0:1] + message_push[at_push, :]
-        pull = jnp.sum(pull, axis=1, keepdims=True)
+        return jnp.sum(pull, axis=1, keepdims=True)
+
+    def make_force(q, c, pull, blocks):
         first = jnp.broadcast_to(pull[:NA], (NA, PAIR))
         second = jnp.broadcast_to(pull[NA:], (NA, PAIR))
         weights = (first, second, jnp.where(low, first, second))
-        for c in range(3):
-            sums = []
-            for block in range(3):
-                value = vectors_ref[c * NA : (c + 1) * NA, block * PAIR : (block + 1) * PAIR].astype(jnp.float32)
-                value = value * weights[block]
-                total = value[:8]
-                for row in range(8, NA, 8):
-                    total = total + value[row : row + 8]
-                sums.append(total)
-            forces[q, c] = forces[q, c] - sums[0] - jnp.where(low, 0.0, sums[2])
-            forces[q + 1, c] = -sums[1] - jnp.where(low, sums[2], 0.0)
+        totals = []
+        for ref, weight in zip(blocks, weights):
+            value = ref[c * NA : (c + 1) * NA, :].astype(jnp.float32) * weight
+            total = value[:8]
+            for row in range(8, NA, 8):
+                total = total + value[row : row + 8]
+            totals.append(total)
+        forces[q, c] = forces[q, c] - totals[0] - jnp.where(low, 0.0, totals[2])
+        forces[q + 1, c] = -totals[1] - jnp.where(low, totals[2], 0.0)
 
     forces[0] = jnp.zeros(forces.shape[1:], jnp.float32)
 
     def stage_of(q, t, rows=True, before=True):
+        here, there = t % 2, (t + 1) % 2
         if before:
-            make_force(q - 1, message[(t + 1) % 2], vec[(t+1)%2])
-        make_messages(q, lhs[t % 2], vec[t%2], message[t % 2])
+            pull = make_pull(q - 1, message[there])
+            for c in range(3):
+                make_force(q - 1, c, pull, vec[there])
+        make_messages(q, lhs[here], message[here])
+        for block in range(3):
+            vec[here][block][...] = lhs[here][block][basis_count * NA :, :]
         if rows:
-            make_rows(q + 1, lhs[(t + 1) % 2], vec[(t+1)%2])
-
-    make_rows(0, lhs_0, vec_0)
+            columns = jnp.transpose(h_rows[q + 1])
+            for chunk in range(CHUNKS):
+                make_rows(q + 1, chunk, columns, lhs[there])
+
+    columns = jnp.transpose(h_rows[0])
+    for chunk in range(CHUNKS):
+        make_rows(0, chunk, columns, lhs[0])
+    whole = (pairs - 2) // UNROLL
     stage_of(0, 0, before=False)
-    whole = (pairs - 2) // UNROLL
-
-    if whole > 1:
-
-        def several(i, _):
-            for t in range(UNROLL):
-                stage_of(i * UNROLL + t + 1, t + 1)
-            return 0
-
-        lax.fori_loop(0, whole, several, 0)
-    for q in range(whole * UNROLL + 1 if whole > 1 else 1, pairs):
+
+    def several(i, _):
+        for t in range(UNROLL):
+            stage_of(i * UNROLL + t + 1, t + 1)
+        return 0
+
+    lax.fori_loop(0, whole, several, 0)
+    for q in range(whole * UNROLL + 1, pairs):
         stage_of(q, q, rows=q < pairs - 1)
-    make_force(pairs - 1, message[(pairs - 1) % 2], vec[(pairs - 1) % 4])
+    last = pairs - 1
+    pull = make_pull(last, message[last % 2])
+    for c in range(3):
+        make_force(last, c, pull, vec[last % 2])
 
     for p in range(own_pairs):
         tile = jnp.zeros((8, PAIR), jnp.float32)
@@ -311,16 +311,17 @@
     last_out[...] = jnp.zeros(last_out.shape, jnp.float32)
     end = last_out.shape[1] - 1
     last_out[:, end:, :] = jnp.broadcast_to(kinetic.reshape(1, 1, 1), (last_out.shape[0], 1, PAIR))
-    first = place_ref[0] * chunks
-    for chunk in range(chunks):
-        at = chunk * width
+    part = small_ref[basis_count + 6 : basis_count + 7, :]
+    for chunk in range(parts_count * chunks):
+        chosen = part == float(chunk // chunks)
+        at = chunk % chunks * width
         for group in range(whole):
-            last_out[first + chunk, 9 * group : 9 * (group + 1), :] = rows[:, at : at + PAIR]
+            last_out[chunk, 9 * group : 9 * (group + 1), :] = jnp.where(chosen, rows[:, at : at + PAIR], 0.0)
             at = at + PAIR
         if width % PAIR:
-            tail = rows[:, at : at + NA]
-            last_out[first + chunk, 9 * whole : 9 * whole + 4, :] = jnp.concatenate([tail[:4], tail[4:8]], axis=1)
-            last_out[first + chunk, 9 * whole + 4 : 9 * whole + 5, :NA] = tail[8:]
+            tail = jnp.where(chosen[:, :NA], rows[:, at : at + NA], 0.0)
+            last_out[chunk, 9 * whole : 9 * whole + 4, :] = jnp.concatenate([tail[:4], tail[4:8]], axis=1)
+            last_out[chunk, 9 * whole + 4 : 9 * whole + 5, :NA] = tail[8:]
 
 
 def finish(place_ref, source_ref, got_ref, thermal_ref, x_out, v_out, g_out):
@@ -387,34 +388,30 @@
     )(place, state, features, weights, small)
 
 
-def run_advance(stage, parts_count, last_shape, place, x, v, g, edge, got, own_feat, table, message_push, later_push, weights, small):
+def run_advance(stage, parts_count, last_shape, x, v, g, edge, got, own_feat, table, message_push, later_push, weights, small):
     own_pairs = v.shape[0]
     channels = table.shape[1]
     basis_count = small.shape[0] - SMALL_ROWS
     tiles = jax.ShapeDtypeStruct(v.shape, jnp.float32)
-    lhs = pltpu.VMEM((basis_count * NA, 3 * PAIR), jnp.bfloat16)
-    vec = pltpu.VMEM((3 * NA, 3 * PAIR), jnp.bfloat16)
+    lhs = pltpu.VMEM(((basis_count + 3) * NA, PAIR), jnp.bfloat16)
+    vec = pltpu.VMEM((3 * NA, PAIR), jnp.bfloat16)
     message = pltpu.VMEM((PAIR, 2 * channels), jnp.bfloat16)
     return pl.pallas_call(
         functools.partial(advance, stage, parts_count),
         out_shape=(tiles, tiles, tiles, jax.ShapeDtypeStruct(last_shape, jnp.float32)),
-        in_specs=[SMEM_SPEC] + [VMEM_SPEC] * 11,
+        in_specs=[VMEM_SPEC] * 11,
         out_specs=(VMEM_SPEC,) * 4,
         scratch_shapes=[
             pltpu.VMEM((own_pairs + 2, 8, PAIR), jnp.float32),
             pltpu.VMEM((own_pairs + 1, 8, PAIR), jnp.float32),
-            lhs,
-            lhs,
-            vec,
-            vec,
-            vec,
-            vec,
+            [[lhs] * 3] * 2,
+            [[vec] * 3] * 2,
             message,
             message,
             pltpu.VMEM((own_pairs + 2, 3, 8, PAIR), jnp.float32),
         ],
         compiler_params=pltpu.CompilerParams(vmem_limit_bytes=20 * 1024 * 1024),
-    )(place, x, v, g, edge, got, own_feat, table, message_push, later_push, weights, small)
+    )(x, v, g, edge, got, own_feat, table, message_push, later_push, weights, small)
 
 
 def run_steps(place, state, features, per_replica, chunk_shape, exchange, weights, small):
@@ -425,7 +422,7 @@
     for step in range(STEPS + 1):
         stage = min(step, 2) if step < STEPS else 3
         shape = edge_shape if step < STEPS else chunk_shape
-        x, v, g, edge = run_advance(stage, per_replica, shape, place, x, v, g, edge, got, *fixed, weights, small)
+        x, v, g, edge = run_advance(stage, per_replica, shape, x, v, g, edge, got, *fixed, weights, small)
         if step < STEPS:
             got = exchange(edge)
     return edge
@@ -477,6 +474,9 @@
     )
     span = initial_distance_filter.shape[0] - 1
     order = (jnp.arange(span + 1, dtype=jnp.float32) - 0.5 * span)[:, None]
+    channels = element_features.shape[1]
+    part = own % per_replica
+    cells = float(devices * local_cells)
     thermal = lax.dynamic_slice(thermal_targets, (own // per_replica,), (1,))
     small = jnp.concatenate(
         [
@@ -484,11 +484,14 @@
             (initial_directional_scales * initial_directional_scales)[None],
             (push_output_matrix * initial_directional_scales)[None],
             (push_output_matrix * later_directional_scales)[None],
-            jnp.broadcast_to(thermal[:, None], (1, push_output_matrix.shape[0])),
+            jnp.broadcast_to(thermal[:, None], (1, channels)),
+            jnp.broadcast_to(jnp.where(part == 0, -cells, 0.0), (1, channels)),
+            jnp.broadcast_to(jnp.where(part == per_replica - 1, cells, 0.0), (1, channels)),
+            jnp.broadcast_to(part.astype(jnp.float32), (1, channels)),
         ],
         axis=0,
     )
-    place = jnp.stack([own % per_replica, jnp.full((), per_replica, own.dtype), own]).astype(jnp.int32)
+    place = jnp.stack([part, jnp.full((), per_replica, own.dtype), own]).astype(jnp.int32)
     ladder_slot = jnp.arange(replicas, dtype=jnp.int32)
     source = jnp.where(swap_approval_flags > 0, swap_counterpart_slot, ladder_slot)
 

time: 83.5 us -> 78.4 us (0.939)
  Pallas kernels: 39.9 us -> 34.8 us
    pallas_call x5, Pallas kernels: 37.4 us -> 32.3 us  [run_advance(): pl.pallas_call(functools.partial(advance, stage, parts_count), out_shape=...]
where the time goes in v4:
time: 78.4 us; the launch traced here: 78 us
  Pallas kernels  34.8 us (44%)
  waiting for transfers between devices  14.9 us (19%)
  blocking collectives  13.6 us (17%)
  starting transfers between devices  7.4 us (9%)
  local copies, waits for them, and re-layouts  3.92 us (5%)
  other arithmetic  2.17 us (3%)
  between operations  1.22 us (2%)
    pallas_call x5, Pallas kernels, run_advance(): pl.pallas_call(functools.partial(advance, stage, parts_count), out_shape=...  32.3 us
    ppermute x8, waiting for transfers between devices, trade(): return lax.ppermute(value, 'dom', [(i, i ^ mask) for i in range(devices)])  14.9 us
    all_to_all x1, blocking collectives, on_device(): got = lax.all_to_all(chunks, 'dom', 0, 0)  13.6 us
    ppermute x8, starting transfers between devices, trade(): return lax.ppermute(value, 'dom', [(i, i ^ mask) for i in range(devices)])  7.4 us
    unnamed x30, local copies, waits for them, and re-layouts  1.9 us
    pallas_call x1, Pallas kernels, run_finish(): pl.pallas_call(finish, out_shape=(out, out, out), in_specs=[SMEM_SPEC, SM...  1.71 us
  transfers between devices with their start and end apart: 8, of which 8 were waited for; matrix products, arithmetic and copies ran while one was open for 3% of the time, Pallas kernels for 0%

profile of v4, /device:TPU:0, one launch (start us, length us, event | category | flops | bytes accessed | tf_op | source)
XLA Modules:
  0.0 78.0 jit_solution(4617089888063089743)
XLA Ops:
  0.7 0.6 copy-done.12
  1.4 0.7 subtract_bitcast_fusion
  2.3 0.7 copy-done.1
  3.0 4.0 %collective-permute-start = (bf16[264,128]{1,0:T(8,128)(2,1)S(1)}, bf16[264,128]{1,0:T(8,128)(2,1)S(1)}, u32[]{:S(2)}, u32[]{:S(2)}) collective-permute-start(bf16[264,128]{1,0:T(8,128)(2,1)S(1)} %pad_maximum_fusion.11), channel_id=1, source_target_pairs={{0,8},{1,9},{2,10},{3,11},{4,12},{5,13},{6,14},{7,15},{8,0},{9,1},... | collective-permute-start | bytes 202760 | tf_op jit(solution)/shard_map/ppermute | solution.py:470
  7.9 0.6 dynamic_slice.3
  9.1 0.6 broadcast_in_dim.37
  9.9 0.9 %collective-permute-done = bf16[264,128]{1,0:T(8,128)(2,1)S(1)} collective-permute-done((bf16[264,128]{1,0:T(8,128)(2,1)S(1)}, bf16[264,128]{1,0:T(8,128)(2,1)S(1)}, u32[]{:S(2)}, u32[]{:S(2)}) %collective-permute-start) | collective-permute-done | bytes 67616 | tf_op jit(solution)/shard_map/ppermute | solution.py:470
  10.9 0.8 %collective-permute-start.1 = (bf16[456,128]{1,0:T(8,128)(2,1)S(1)}, bf16[456,128]{1,0:T(8,128)(2,1)S(1)}, u32[]{:S(2)}, u32[]{:S(2)}) collective-permute-start(bf16[456,128]{1,0:T(8,128)(2,1)S(1)} %pad_maximum_fusion.8), channel_id=1, source_target_pairs={{0,4},{1,5},{2,6},{3,7},{4,0},{5,1},{6,2},{7,3},{8,12},{9,13},{10,... | collective-permute-start | bytes 350216 | tf_op jit(solution)/shard_map/ppermute | solution.py:470
  11.7 4.1 %collective-permute-done.1 = bf16[456,128]{1,0:T(8,128)(2,1)S(1)} collective-permute-done((bf16[456,128]{1,0:T(8,128)(2,1)S(1)}, bf16[456,128]{1,0:T(8,128)(2,1)S(1)}, u32[]{:S(2)}, u32[]{:S(2)}) %collective-permute-start.1) | collective-permute-done | bytes 116768 | tf_op jit(solution)/shard_map/ppermute | solution.py:470
  16.0 1.8 %collective-permute-start.2 = (bf16[840,128]{1,0:T(8,128)(2,1)S(1)}, bf16[840,128]{1,0:T(8,128)(2,1)S(1)}, u32[]{:S(2)}, u32[]{:S(2)}) collective-permute-start(bf16[840,128]{1,0:T(8,128)(2,1)S(1)} %pad_maximum_fusion.4), channel_id=1, source_target_pairs={{0,2},{1,3},{2,0},{3,1},{4,6},{5,7},{6,4},{7,5},{8,10},{9,11},{10,... | collective-permute-start | bytes 645128 | tf_op jit(solution)/shard_map/ppermute | solution.py:470
  17.8 4.1 %collective-permute-done.2 = bf16[840,128]{1,0:T(8,128)(2,1)S(1)} collective-permute-done((bf16[840,128]{1,0:T(8,128)(2,1)S(1)}, bf16[840,128]{1,0:T(8,128)(2,1)S(1)}, u32[]{:S(2)}, u32[]{:S(2)}) %collective-permute-start.2) | collective-permute-done | bytes 215072 | tf_op jit(solution)/shard_map/ppermute | solution.py:470
  22.4 1.7 %collective-permute-done.3 = bf16[1680,128]{1,0:T(8,128)(2,1)S(1)} collective-permute-done((bf16[1680,128]{1,0:T(8,128)(2,1)S(1)}, bf16[1680,128]{1,0:T(8,128)(2,1)S(1)}, u32[]{:S(2)}, u32[]{:S(2)}) %collective-permute-start.3) | collective-permute-done | bytes 430112 | tf_op jit(solution)/shard_map/ppermute | solution.py:470
  24.8 0.8 %shard_map.166 = (f32[14,8,128]{2,1,0:T(8,128)S(1)}, f32[12,8,128]{2,1,0:T(8,128)S(1)}, bf16[1792,128]{1,0:T(8,128)(2,1)S(1)}, bf16[1792,128]{1,0:T(8,128)(2,1)S...) custom-call(s32[3]{0:T(128)S(1)} %pad_add_fusion.place_ref, f32[6,3072]{1,0:T(8,128)S(1)} %reshape.690.state_ref, ...), custom_call_target="tpu_custom_call" | custom-call | tf_op jit(solution)/shard_map/pallas_call | solution.py:375
  25.6 6.4 %shard_map.167 = (f32[12,8,128]{2,1,0:T(8,128)S(1)}, f32[12,8,128]{2,1,0:T(8,128)S(1)}, f32[12,8,128]{2,1,0:T(8,128)S(1)}, f32[2,2,8,128]{3,2,1,0:T(8,128)S(1)}) custom-call(f32[14,8,128]{2,1,0:T(8,128)S(1)} %get-tuple-element.39.x_ref, f32[12,8,128]{2,1,0:T(8,128)S(1)} %get-tuple-element.40.v_ref.g_ref, f32[12,8,128]{2,1,0:T(8,128)S(1)} %get-tuple-element.40.v_ref.g_ref, ...), custom_call_target="tpu_custom_call" | custom-call | tf_op jit(solution)/shard_map/pallas_call | solution.py:399
  32.2 1.1 %collective-permute-done.4.got_ref = f32[2,2,8,128]{3,2,1,0:T(8,128)S(1)} collective-permute-done((f32[2,2,8,128]{3,2,1,0:T(8,128)S(1)}, f32[2,2,8,128]{3,2,1,0:T(8,128)S(1)}, u32[]{:S(2)}, u32[]{:S(2)}) %collective-permute-start.4) | collective-permute-done | bytes 16416 | tf_op jit(solution)/shard_map/ppermute | solution.py:470
  33.3 6.3 %shard_map.168 = (f32[12,8,128]{2,1,0:T(8,128)S(1)}, f32[12,8,128]{2,1,0:T(8,128)S(1)}, f32[12,8,128]{2,1,0:T(8,128)S(1)}, f32[2,2,8,128]{3,2,1,0:T(8,128)S(1)}) custom-call(f32[12,8,128]{2,1,0:T(8,128)S(1)} %get-tuple-element.45.x_ref, f32[12,8,128]{2,1,0:T(8,128)S(1)} %get-tuple-element.46.v_ref, f32[12,8,128]{2,1,0:T(8,128)S(1)} %get-tuple-element.47.g_ref, ...), custom_call_target="tpu_custom_call" | custom-call | tf_op jit(solution)/shard_map/pallas_call | solution.py:399
  39.7 1.0 %collective-permute-done.5.got_ref = f32[2,2,8,128]{3,2,1,0:T(8,128)S(1)} collective-permute-done((f32[2,2,8,128]{3,2,1,0:T(8,128)S(1)}, f32[2,2,8,128]{3,2,1,0:T(8,128)S(1)}, u32[]{:S(2)}, u32[]{:S(2)}) %collective-permute-start.5) | collective-permute-done | bytes 16416 | tf_op jit(solution)/shard_map/ppermute | solution.py:470
  40.8 6.3 %shard_map.169 = (f32[12,8,128]{2,1,0:T(8,128)S(1)}, f32[12,8,128]{2,1,0:T(8,128)S(1)}, f32[12,8,128]{2,1,0:T(8,128)S(1)}, f32[2,2,8,128]{3,2,1,0:T(8,128)S(1)}) custom-call(f32[12,8,128]{2,1,0:T(8,128)S(1)} %get-tuple-element.49.x_ref, f32[12,8,128]{2,1,0:T(8,128)S(1)} %get-tuple-element.50.v_ref, f32[12,8,128]{2,1,0:T(8,128)S(1)} %get-tuple-element.51.g_ref, ...), custom_call_target="tpu_custom_call" | custom-call | tf_op jit(solution)/shard_map/pallas_call | solution.py:399
  47.3 1.0 %collective-permute-done.6.got_ref = f32[2,2,8,128]{3,2,1,0:T(8,128)S(1)} collective-permute-done((f32[2,2,8,128]{3,2,1,0:T(8,128)S(1)}, f32[2,2,8,128]{3,2,1,0:T(8,128)S(1)}, u32[]{:S(2)}, u32[]{:S(2)}) %collective-permute-start.6) | collective-permute-done | bytes 16416 | tf_op jit(solution)/shard_map/ppermute | solution.py:470
  48.3 6.3 %shard_map.170 = (f32[12,8,128]{2,1,0:T(8,128)S(1)}, f32[12,8,128]{2,1,0:T(8,128)S(1)}, f32[12,8,128]{2,1,0:T(8,128)S(1)}, f32[2,2,8,128]{3,2,1,0:T(8,128)S(1)}) custom-call(f32[12,8,128]{2,1,0:T(8,128)S(1)} %get-tuple-element.53.x_ref, f32[12,8,128]{2,1,0:T(8,128)S(1)} %get-tuple-element.54.v_ref, f32[12,8,128]{2,1,0:T(8,128)S(1)} %get-tuple-element.55.g_ref, ...), custom_call_target="tpu_custom_call" | custom-call | tf_op jit(solution)/shard_map/pallas_call | solution.py:399
  54.8 1.0 %collective-permute-done.7.got_ref = f32[2,2,8,128]{3,2,1,0:T(8,128)S(1)} collective-permute-done((f32[2,2,8,128]{3,2,1,0:T(8,128)S(1)}, f32[2,2,8,128]{3,2,1,0:T(8,128)S(1)}, u32[]{:S(2)}, u32[]{:S(2)}) %collective-permute-start.7) | collective-permute-done | bytes 16416 | tf_op jit(solution)/shard_map/ppermute | solution.py:470
  55.8 6.9 %shard_map.171 = (f32[12,8,128]{2,1,0:T(8,128)}, f32[12,8,128]{2,1,0:T(8,128)}, f32[12,8,128]{2,1,0:T(8,128)}, f32[16,16,128]{2,1,0:T(8,128)S(1)}) custom-call(f32[12,8,128]{2,1,0:T(8,128)S(1)} %get-tuple-element.57.x_ref, f32[12,8,128]{2,1,0:T(8,128)S(1)} %get-tuple-element.58.v_ref, f32[12,8,128]{2,1,0:T(8,128)S(1)} %get-tuple-element.59.g_ref, ...), custom_call_target="tpu_custom_call" | custom-call | tf_op jit(solution)/shard_map/pallas_call | solution.py:399
  62.7 13.6 %all_to_all.5.got_ref = f32[16,16,128]{2,1,0:T(8,128)} all-to-all(f32[16,16,128]{2,1,0:T(8,128)S(1)} %get-tuple-element.61), channel_id=1, replica_groups=mesh['groups'=2,'dom'=16] {'dom'}, dimensions={0} | all-to-all | bytes 262144 | tf_op jit(solution)/shard_map/all_to_all | solution.py:547
  76.3 1.7 %shard_map.172 = (f32[3,8,192]{2,1,0:T(8,128)}, f32[3,8,192]{2,1,0:T(8,128)}, f32[3,8,192]{2,1,0:T(8,128)}) custom-call(s32[3]{0:T(128)} %copy-done, s32[8]{0:T(128)} %compare_select_fusion.source_ref, f32[16,16,128]{2,1,0:T(8,128)} %all_to_all.5.got_ref, f32[8]{0:T(128)} %thermal_ref.1), custom_call_target="tpu_custom_call" | custom-call | tf_op jit(solution)/shard_map/pallas_call | solution.py:435
  (101 shorter events, 3.6 us)
Async XLA Ops:
  0.6 0.7 copy-start.12
  1.4 0.8 copy-start.6
  2.2 0.8 %copy-start.1 = (bf16[192,128]{1,0:T(8,128)(2,1)S(1)}, bf16[192,128]{1,0:T(8,128)(2,1)}, u32[]{:S(2)}) copy-start(bf16[192,128]{1,0:T(8,128)(2,1)} %param.18) | copy-start | bytes 147460
  3.0 7.7 %collective-permute-start = (bf16[264,128]{1,0:T(8,128)(2,1)S(1)}, bf16[264,128]{1,0:T(8,128)(2,1)S(1)}, u32[]{:S(2)}, u32[]{:S(2)}) collective-permute-start(bf16[264,128]{1,0:T(8,128)(2,1)S(1)} %pad_maximum_fusion.11), channel_id=1, source_target_pairs={{0,8},{1,9},{2,10},{3,11},{4,12},{5,13},{6,14},{7,15},{8,0},{9,1},... | collective-permute-start | bytes 202760 | tf_op jit(solution)/shard_map/ppermute | solution.py:470
  7.0 1.4 %copy-start.13 = (s32[8]{0:T(128)S(1)}, s32[8]{0:T(128)}, u32[]{:S(2)}) copy-start(s32[8]{0:T(128)} %param.19) | copy-start | bytes 100
  7.0 1.4 %copy-start.14 = (s32[8]{0:T(128)S(1)}, s32[8]{0:T(128)}, u32[]{:S(2)}) copy-start(s32[8]{0:T(128)} %param.20) | copy-start | bytes 100
  7.1 1.9 %copy-start.10 = (f32[128]{0:T(128)S(1)}, f32[128]{0:T(128)}, u32[]{:S(2)}) copy-start(f32[128]{0:T(128)} %param.27) | copy-start | bytes 1540
  7.1 1.9 %copy-start.11 = (f32[128]{0:T(128)S(1)}, f32[128]{0:T(128)}, u32[]{:S(2)}) copy-start(f32[128]{0:T(128)} %param.23) | copy-start | bytes 1540
  7.1 0.7 copy-start.7
  7.1 0.8 copy-start.8
  7.1 1.9 %copy-start.9 = (f32[128]{0:T(128)S(1)}, f32[128]{0:T(128)}, u32[]{:S(2)}) copy-start(f32[128]{0:T(128)} %param.28) | copy-start | bytes 1540
  7.1 1.9 %copy-start.4 = (bf16[128,128]{1,0:T(8,128)(2,1)S(1)}, bf16[128,128]{1,0:T(8,128)(2,1)}, u32[]{:S(2)}) copy-start(bf16[128,128]{1,0:T(8,128)(2,1)} %param.24) | copy-start | bytes 98308
  7.1 1.9 %copy-start.5 = (bf16[128,128]{1,0:T(8,128)(2,1)S(1)}, bf16[128,128]{1,0:T(8,128)(2,1)}, u32[]{:S(2)}) copy-start(bf16[128,128]{1,0:T(8,128)(2,1)} %param.21) | copy-start | bytes 98308
  7.2 1.9 %copy-start.2 = (bf16[128,128]{1,0:T(8,128)(2,1)S(1)}, bf16[128,128]{1,0:T(8,128)(2,1)}, u32[]{:S(2)}) copy-start(bf16[128,128]{1,0:T(8,128)(2,1)} %param.26) | copy-start | bytes 98308
  7.2 1.9 %copy-start.3 = (bf16[128,128]{1,0:T(8,128)(2,1)S(1)}, bf16[128,128]{1,0:T(8,128)(2,1)}, u32[]{:S(2)}) copy-start(bf16[128,128]{1,0:T(8,128)(2,1)} %param.25) | copy-start | bytes 98308
  9.9 14.9 %copy-start = (s32[3]{0:T(128)}, s32[3]{0:T(128)S(1)}, u32[]{:S(2)}) copy-start(s32[3]{0:T(128)S(1)} %pad_add_fusion.place_ref) | copy-start | bytes 40
  10.9 4.9 %collective-permute-start.1 = (bf16[456,128]{1,0:T(8,128)(2,1)S(1)}, bf16[456,128]{1,0:T(8,128)(2,1)S(1)}, u32[]{:S(2)}, u32[]{:S(2)}) collective-permute-start(bf16[456,128]{1,0:T(8,128)(2,1)S(1)} %pad_maximum_fusion.8), channel_id=1, source_target_pairs={{0,4},{1,5},{2,6},{3,7},{4,0},{5,1},{6,2},{7,3},{8,12},{9,13},{10,... | collective-permute-start | bytes 350216 | tf_op jit(solution)/shard_map/ppermute | solution.py:470
  16.0 5.9 %collective-permute-start.2 = (bf16[840,128]{1,0:T(8,128)(2,1)S(1)}, bf16[840,128]{1,0:T(8,128)(2,1)S(1)}, u32[]{:S(2)}, u32[]{:S(2)}) collective-permute-start(bf16[840,128]{1,0:T(8,128)(2,1)S(1)} %pad_maximum_fusion.4), channel_id=1, source_target_pairs={{0,2},{1,3},{2,0},{3,1},{4,6},{5,7},{6,4},{7,5},{8,10},{9,11},{10,... | collective-permute-start | bytes 645128 | tf_op jit(solution)/shard_map/ppermute | solution.py:470
  22.3 1.8 %collective-permute-start.3 = (bf16[1680,128]{1,0:T(8,128)(2,1)S(1)}, bf16[1680,128]{1,0:T(8,128)(2,1)S(1)}, u32[]{:S(2)}, u32[]{:S(2)}) collective-permute-start(bf16[1680,128]{1,0:T(8,128)(2,1)S(1)} %pad_maximum_fusion.1), channel_id=1, source_target_pairs={{0,1},{1,0},{2,3},{3,2},{4,5},{5,4},{6,7},{7,6},{8,9},{9,8},{10,11... | collective-permute-start | bytes 1290248 | tf_op jit(solution)/shard_map/ppermute | solution.py:470
  32.0 1.2 %collective-permute-start.4 = (f32[2,2,8,128]{3,2,1,0:T(8,128)S(1)}, f32[2,2,8,128]{3,2,1,0:T(8,128)S(1)}, u32[]{:S(2)}, u32[]{:S(2)}) collective-permute-start(f32[2,2,8,128]{3,2,1,0:T(8,128)S(1)} %get-tuple-element.48.edge_ref), channel_id=1, source_target_pairs={{0,1},{1,0},{2,3},{3,2},{4,5},{5,4},{6,7},{7,6},{8,9},{9,8},{10,11... | collective-permute-start | bytes 49160 | tf_op jit(solution)/shard_map/ppermute | solution.py:470
  39.6 1.2 %collective-permute-start.5 = (f32[2,2,8,128]{3,2,1,0:T(8,128)S(1)}, f32[2,2,8,128]{3,2,1,0:T(8,128)S(1)}, u32[]{:S(2)}, u32[]{:S(2)}) collective-permute-start(f32[2,2,8,128]{3,2,1,0:T(8,128)S(1)} %get-tuple-element.52.edge_ref), channel_id=1, source_target_pairs={{0,1},{1,0},{2,3},{3,2},{4,5},{5,4},{6,7},{7,6},{8,9},{9,8},{10,11... | collective-permute-start | bytes 49160 | tf_op jit(solution)/shard_map/ppermute | solution.py:470
  47.1 1.2 %collective-permute-start.6 = (f32[2,2,8,128]{3,2,1,0:T(8,128)S(1)}, f32[2,2,8,128]{3,2,1,0:T(8,128)S(1)}, u32[]{:S(2)}, u32[]{:S(2)}) collective-permute-start(f32[2,2,8,128]{3,2,1,0:T(8,128)S(1)} %get-tuple-element.56.edge_ref), channel_id=1, source_target_pairs={{0,1},{1,0},{2,3},{3,2},{4,5},{5,4},{6,7},{7,6},{8,9},{9,8},{10,11... | collective-permute-start | bytes 49160 | tf_op jit(solution)/shard_map/ppermute | solution.py:470
  54.6 1.2 %collective-permute-start.7 = (f32[2,2,8,128]{3,2,1,0:T(8,128)S(1)}, f32[2,2,8,128]{3,2,1,0:T(8,128)S(1)}, u32[]{:S(2)}, u32[]{:S(2)}) collective-permute-start(f32[2,2,8,128]{3,2,1,0:T(8,128)S(1)} %get-tuple-element.60.edge_ref), channel_id=1, source_target_pairs={{0,1},{1,0},{2,3},{3,2},{4,5},{5,4},{6,7},{7,6},{8,9},{9,8},{10,11... | collective-permute-start | bytes 49160 | tf_op jit(solution)/shard_map/ppermute | solution.py:470

commit v5 on v4

--- a/solution.py
+++ b/solution.py
@@ -19,6 +19,7 @@
 step_time = 0.05
 motion_work_lower_limit = 1e-06
 LOG2E = math.log2(math.e)
+VMEM_SPEC = pl.BlockSpec(memory_space=pltpu.VMEM)
 
 
 def dot(a, b):
@@ -68,7 +69,7 @@
 
 
 def prepare(
-    place_ref,
+    parts_count,
     state_ref,
     feat_ref,
     weight_ref,
@@ -83,7 +84,8 @@
     extended = x_out.shape[0]
     cells = feat_ref.shape[0] // NA
     own_cells = 2 * (extended - 2)
-    first_cell = place_ref[0] * own_cells - 2 + cells
+    part = lax.rem(lax.axis_index("dom"), parts_count)
+    first_cell = part * own_cells - 2 + cells
     for p in range(extended):
         cell = lax.rem(first_cell + 2 * p, cells)
         at = pl.ds(pl.multiple_of(cell * NA, PAIR), PAIR)
@@ -91,7 +93,7 @@
         x = jnp.concatenate([rows[:3], jnp.zeros((5, PAIR), jnp.float32)], axis=0)
         sub = lax.broadcasted_iota(jnp.int32, (8, PAIR), 0)
         lane = lax.broadcasted_iota(jnp.int32, (8, PAIR), 1)
-        floor = (place_ref[0] * own_cells - 2 + 2 * p + lane // NA).astype(jnp.float32)
+        floor = (part * own_cells - 2 + 2 * p + lane // NA).astype(jnp.float32)
         x_out[p] = x + jnp.where(sub == 2, floor, 0.0)
         if 0 < p < extended - 1:
             v_out[p - 1] = jnp.concatenate([rows[3:6], jnp.zeros((5, PAIR), jnp.float32)], axis=0)
@@ -324,34 +326,46 @@
             last_out[chunk, 9 * whole + 4 : 9 * whole + 5, :NA] = tail[8:]
 
 
-def finish(place_ref, source_ref, got_ref, thermal_ref, x_out, v_out, g_out):
+def finish(ladder_ref, got_ref, x_out, v_out, g_out):
     replicas, width = x_out.shape[1:]
     whole = width // PAIR
-    parts = place_ref[1]
-    domain = place_ref[2]
     domains, chunk_rows = got_ref.shape[:2]
-    part = domain // (domains // parts)
+    group = domains // replicas
+    domain = lax.axis_index("dom")
+    part = domain // (domains // group)
     atoms = float(domains * width)
-    group = domains // replicas
     outs = (x_out, v_out, g_out)
     pieces_of = [[] for _ in range(9)]
     factors = []
+    sources = [got_ref[s * group + part] for s in range(replicas)]
+    kinetics = []
+    for s in range(replicas):
+        kinetic = got_ref[s * group, chunk_rows - 1 :, :]
+        for other in range(1, group):
+            kinetic = kinetic + got_ref[s * group + other, chunk_rows - 1 :, :]
+        kinetics.append(kinetic)
+    targets = [jnp.broadcast_to(ladder_ref[0:1, r : r + 1], (1, PAIR)) for r in range(replicas)]
+    source_targets = []
     for r in range(replicas):
-        source = source_ref[r]
-        kinetic = got_ref[source * group, chunk_rows - 1 :, :]
-        for other in range(1, group):
-            kinetic = kinetic + got_ref[source * group + other, chunk_rows - 1 :, :]
-        mean = kinetic / (3.0 * atoms) + motion_work_lower_limit
-        source_target = jnp.full((1, PAIR), thermal_ref[source])
-        factors.append(jnp.sqrt(source_target / mean) * jnp.sqrt(jnp.full((1, PAIR), thermal_ref[r]) / source_target))
-        rows = got_ref[source * group + part]
+        own_source = jnp.broadcast_to(ladder_ref[1:2, r : r + 1], (1, PAIR))
+        rows, kinetic, source_target = sources[0], kinetics[0], targets[0]
+        for s in range(1, replicas):
+            chosen = own_source == float(s)
+            rows = jnp.where(chosen, sources[s], rows)
+            kinetic = jnp.where(chosen, kinetics[s], kinetic)
+            source_target = jnp.where(chosen, targets[s], source_target)
+        source_targets.append(source_target)
+        factors.append(kinetic)
         for row in range(9):
             pieces_of[row].append([rows[9 * g + row : 9 * g + row + 1] for g in range(whole)])
             if width % PAIR:
                 at = 9 * whole + row % 4 if row < 8 else 9 * whole + 4
                 tail = rows[at : at + 1, NA:] if 4 <= row < 8 else rows[at : at + 1, :NA]
                 pieces_of[row][-1].append(tail)
-    factor = jnp.concatenate(factors, axis=0)
+    mean = jnp.concatenate(factors, axis=0) / (3.0 * atoms) + motion_work_lower_limit
+    source_target = jnp.concatenate(source_targets, axis=0)
+    target = jnp.concatenate(targets, axis=0)
+    factor = jnp.sqrt(source_target / mean) * jnp.sqrt(target / source_target)
     for row in range(9):
         for index in range(len(pieces_of[row][0])):
             value = jnp.concatenate([of_replica[index] for of_replica in pieces_of[row]], axis=0)
@@ -364,16 +378,12 @@
             outs[row // 3][row % 3, :, index * PAIR : index * PAIR + size] = value
 
 
-VMEM_SPEC = pl.BlockSpec(memory_space=pltpu.VMEM)
-SMEM_SPEC = pl.BlockSpec(memory_space=pltpu.SMEM)
-
-
-def run_prepare(place, state, features, per_replica, weights, small):
+def run_prepare(state, features, per_replica, weights, small):
     atoms, channels = features.shape
     own_pairs = atoms // per_replica // PAIR
     extended = own_pairs + 2
     return pl.pallas_call(
-        prepare,
+        functools.partial(prepare, per_replica),
         out_shape=(
             jax.ShapeDtypeStruct((extended, 8, PAIR), jnp.float32),
             jax.ShapeDtypeStruct((own_pairs, 8, PAIR), jnp.float32),
@@ -382,10 +392,10 @@
             jax.ShapeDtypeStruct(((extended - 1) * PAIR, channels), jnp.float32),
             jax.ShapeDtypeStruct((8, channels), jnp.float32),
         ),
-        in_specs=[SMEM_SPEC] + [VMEM_SPEC] * 4,
+        in_specs=[VMEM_SPEC] * 4,
         out_specs=(VMEM_SPEC,) * 6,
         compiler_params=pltpu.CompilerParams(vmem_limit_bytes=20 * 1024 * 1024),
-    )(place, state, features, weights, small)
+    )(state, features, weights, small)
 
 
 def run_advance(stage, parts_count, last_shape, x, v, g, edge, got, own_feat, table, message_push, later_push, weights, small):
@@ -414,8 +424,8 @@
     )(x, v, g, edge, got, own_feat, table, message_push, later_push, weights, small)
 
 
-def run_steps(place, state, features, per_replica, chunk_shape, exchange, weights, small):
-    x, v, *fixed = run_prepare(place, state, features, per_replica, weights, small)
+def run_steps(state, features, per_replica, chunk_shape, exchange, weights, small):
+    x, v, *fixed = run_prepare(state, features, per_replica, weights, small)
     edge_shape = (2, 2, 8, PAIR)
     edge = got = jnp.zeros(edge_shape, jnp.float32)
     g = v
@@ -428,16 +438,17 @@
     return edge
 
 
-def run_finish(place, source, got, thermal_targets, local_atoms):
-    replicas = thermal_targets.shape[0]
+def run_finish(ladder, got, local_atoms):
+    replicas = ladder.shape[1]
     out = jax.ShapeDtypeStruct((3, replicas, local_atoms), jnp.float32)
     whole = pl.BlockSpec(out.shape, lambda: (0, 0, 0))
     outs = pl.pallas_call(
         finish,
         out_shape=(out, out, out),
-        in_specs=[SMEM_SPEC, SMEM_SPEC, VMEM_SPEC, SMEM_SPEC],
+        in_specs=[VMEM_SPEC] * 2,
         out_specs=(whole, whole, whole),
-    )(place, source, got, thermal_targets)
+        compiler_params=pltpu.CompilerParams(vmem_limit_bytes=8 * 1024 * 1024),
+    )(ladder, got)
     return tuple(jnp.transpose(o, (1, 0, 2)) for o in outs)
 
 
@@ -491,9 +502,10 @@
         ],
         axis=0,
     )
-    place = jnp.stack([part, jnp.full((), per_replica, own.dtype), own]).astype(jnp.int32)
-    ladder_slot = jnp.arange(replicas, dtype=jnp.int32)
-    source = jnp.where(swap_approval_flags > 0, swap_counterpart_slot, ladder_slot)
+
+    slots = jnp.arange(replicas, dtype=jnp.int32)
+    source = jnp.where(swap_approval_flags > 0, swap_counterpart_slot, slots)
+    ladder = jnp.stack([thermal_targets, source.astype(jnp.float32)])
 
     atom_cell = jnp.arange(local_atoms, dtype=jnp.int32) // NA
     cell_floor = jnp.array([0.0, 0.0, 1.0], jnp.float32)[:, None] * (
@@ -517,7 +529,7 @@
             keep = send = state
         message = jnp.concatenate([features.reshape(-1, channels), send.reshape(-1, channels)], axis=0)
         if level == 1:
-            message, weights, small, place, source = lax.optimization_barrier((message, weights, small, place, source))
+            message, weights, small, ladder = lax.optimization_barrier((message, weights, small, ladder))
         got = trade(message, mask)
         count = features.size // channels
         got_features = got[:count].reshape(features.shape)
@@ -543,9 +555,9 @@
 
     chunk_rows = 9 * (local_atoms // PAIR) + (5 if local_atoms % PAIR else 0) + 1
     chunk_rows = -(-chunk_rows // 8) * 8
-    chunks = run_steps(place, state, features, per_replica, (devices, chunk_rows, PAIR), exchange, weights, small)
+    chunks = run_steps(state, features, per_replica, (devices, chunk_rows, PAIR), exchange, weights, small)
     got = lax.all_to_all(chunks, "dom", 0, 0)
-    return run_finish(place, source, got, thermal_targets, local_atoms)
+    return run_finish(ladder, got, local_atoms)
 
 
 def solution(mesh):

time: 78.4 us -> 76.9 us (0.981)
  Pallas kernels: 34.8 us -> 33.5 us
    pallas_call x2, Pallas kernels: 2.54 us -> 1.21 us  [the longest x1 0.91 us: run_finish(): pl.pallas_call(finish, out_shape=(out, out, out), in_specs=[VMEM_SPEC] *...]
    unnamed x30 -> x28, local copies, waits for them, and re-layouts: 1.9 us -> 1.89 us
  transfers between devices with their start and end apart: 8 -> 8, of which waited for: 8 -> 8; matrix products, arithmetic and copies ran while one was open for 3% -> 2% of each run, Pallas kernels for 0% -> 0%
where the time goes in v5:
time: 76.9 us; the launch traced here: 76.6 us
  Pallas kernels  33.5 us (44%)
  waiting for transfers between devices  15.6 us (20%)
  blocking collectives  13.5 us (18%)
  starting transfers between devices  7.26 us (9%)
  local copies, waits for them, and re-layouts  3.92 us (5%)
  other arithmetic  1.57 us (2%)
  between operations  1.25 us (2%)
    pallas_call x5, Pallas kernels, run_advance(): pl.pallas_call(functools.partial(advance, stage, parts_count), out_shape=...  32.3 us
    ppermute x8, waiting for transfers between devices, trade(): return lax.ppermute(value, 'dom', [(i, i ^ mask) for i in range(devices)])  15.6 us
    all_to_all x1, blocking collectives, on_device(): got = lax.all_to_all(chunks, 'dom', 0, 0)  13.5 us
    ppermute x8, starting transfers between devices, trade(): return lax.ppermute(value, 'dom', [(i, i ^ mask) for i in range(devices)])  7.26 us
    unnamed x28, local copies, waits for them, and re-layouts  1.89 us
  transfers between devices with their start and end apart: 8, of which 8 were waited for; matrix products, arithmetic and copies ran while one was open for 2% of the time, Pallas kernels for 0%

profile of v5, /device:TPU:0, one launch (start us, length us, event | category | flops | bytes accessed | tf_op | source)
XLA Modules:
  0.0 76.6 jit_solution(4184004294413937043)
XLA Ops:
  0.7 0.6 copy-done.11
  1.4 0.7 subtract_bitcast_fusion
  2.3 0.7 copy-done
  3.0 4.0 %collective-permute-start = (bf16[264,128]{1,0:T(8,128)(2,1)S(1)}, bf16[264,128]{1,0:T(8,128)(2,1)S(1)}, u32[]{:S(2)}, u32[]{:S(2)}) collective-permute-start(bf16[264,128]{1,0:T(8,128)(2,1)S(1)} %pad_maximum_fusion.11), channel_id=1, source_target_pairs={{0,8},{1,9},{2,10},{3,11},{4,12},{5,13},{6,14},{7,15},{8,0},{9,1},... | collective-permute-start | bytes 202760 | tf_op jit(solution)/shard_map/ppermute | solution.py:481
  7.3 0.5 copy-done.6
  7.9 0.6 dynamic_slice.3
  8.6 0.6 broadcast_in_dim.37
  9.3 1.4 %collective-permute-done = bf16[264,128]{1,0:T(8,128)(2,1)S(1)} collective-permute-done((bf16[264,128]{1,0:T(8,128)(2,1)S(1)}, bf16[264,128]{1,0:T(8,128)(2,1)S(1)}, u32[]{:S(2)}, u32[]{:S(2)}) %collective-permute-start) | collective-permute-done | bytes 67616 | tf_op jit(solution)/shard_map/ppermute | solution.py:481
  10.9 0.7 collective-permute-start.1
  11.6 4.2 %collective-permute-done.1 = bf16[456,128]{1,0:T(8,128)(2,1)S(1)} collective-permute-done((bf16[456,128]{1,0:T(8,128)(2,1)S(1)}, bf16[456,128]{1,0:T(8,128)(2,1)S(1)}, u32[]{:S(2)}, u32[]{:S(2)}) %collective-permute-start.1) | collective-permute-done | bytes 116768 | tf_op jit(solution)/shard_map/ppermute | solution.py:481
  16.0 1.8 %collective-permute-start.2 = (bf16[840,128]{1,0:T(8,128)(2,1)S(1)}, bf16[840,128]{1,0:T(8,128)(2,1)S(1)}, u32[]{:S(2)}, u32[]{:S(2)}) collective-permute-start(bf16[840,128]{1,0:T(8,128)(2,1)S(1)} %pad_maximum_fusion.4), channel_id=1, source_target_pairs={{0,2},{1,3},{2,0},{3,1},{4,6},{5,7},{6,4},{7,5},{8,10},{9,11},{10,... | collective-permute-start | bytes 645128 | tf_op jit(solution)/shard_map/ppermute | solution.py:481
  17.8 4.1 %collective-permute-done.2 = bf16[840,128]{1,0:T(8,128)(2,1)S(1)} collective-permute-done((bf16[840,128]{1,0:T(8,128)(2,1)S(1)}, bf16[840,128]{1,0:T(8,128)(2,1)S(1)}, u32[]{:S(2)}, u32[]{:S(2)}) %collective-permute-start.2) | collective-permute-done | bytes 215072 | tf_op jit(solution)/shard_map/ppermute | solution.py:481
  22.4 1.7 %collective-permute-done.3 = bf16[1680,128]{1,0:T(8,128)(2,1)S(1)} collective-permute-done((bf16[1680,128]{1,0:T(8,128)(2,1)S(1)}, bf16[1680,128]{1,0:T(8,128)(2,1)S(1)}, u32[]{:S(2)}, u32[]{:S(2)}) %collective-permute-start.3) | collective-permute-done | bytes 430112 | tf_op jit(solution)/shard_map/ppermute | solution.py:481
  25.1 6.4 %shard_map.167 = (f32[12,8,128]{2,1,0:T(8,128)S(1)}, f32[12,8,128]{2,1,0:T(8,128)S(1)}, f32[12,8,128]{2,1,0:T(8,128)S(1)}, f32[2,2,8,128]{3,2,1,0:T(8,128)S(1)}) custom-call(f32[14,8,128]{2,1,0:T(8,128)S(1)} %get-tuple-element.37.x_ref, f32[12,8,128]{2,1,0:T(8,128)S(1)} %get-tuple-element.38.v_ref.g_ref, f32[12,8,128]{2,1,0:T(8,128)S(1)} %get-tuple-element.38.v_ref.g_ref, ...), custom_call_target="tpu_custom_call" | custom-call | tf_op jit(solution)/shard_map/pallas_call | solution.py:409
  31.7 1.1 %collective-permute-done.4.got_ref = f32[2,2,8,128]{3,2,1,0:T(8,128)S(1)} collective-permute-done((f32[2,2,8,128]{3,2,1,0:T(8,128)S(1)}, f32[2,2,8,128]{3,2,1,0:T(8,128)S(1)}, u32[]{:S(2)}, u32[]{:S(2)}) %collective-permute-start.4) | collective-permute-done | bytes 16416 | tf_op jit(solution)/shard_map/ppermute | solution.py:481
  32.7 6.3 %shard_map.168 = (f32[12,8,128]{2,1,0:T(8,128)S(1)}, f32[12,8,128]{2,1,0:T(8,128)S(1)}, f32[12,8,128]{2,1,0:T(8,128)S(1)}, f32[2,2,8,128]{3,2,1,0:T(8,128)S(1)}) custom-call(f32[12,8,128]{2,1,0:T(8,128)S(1)} %get-tuple-element.43.x_ref, f32[12,8,128]{2,1,0:T(8,128)S(1)} %get-tuple-element.44.v_ref, f32[12,8,128]{2,1,0:T(8,128)S(1)} %get-tuple-element.45.g_ref, ...), custom_call_target="tpu_custom_call" | custom-call | tf_op jit(solution)/shard_map/pallas_call | solution.py:409
  39.2 1.0 %collective-permute-done.5.got_ref = f32[2,2,8,128]{3,2,1,0:T(8,128)S(1)} collective-permute-done((f32[2,2,8,128]{3,2,1,0:T(8,128)S(1)}, f32[2,2,8,128]{3,2,1,0:T(8,128)S(1)}, u32[]{:S(2)}, u32[]{:S(2)}) %collective-permute-start.5) | collective-permute-done | bytes 16416 | tf_op jit(solution)/shard_map/ppermute | solution.py:481
  40.2 6.3 %shard_map.169 = (f32[12,8,128]{2,1,0:T(8,128)S(1)}, f32[12,8,128]{2,1,0:T(8,128)S(1)}, f32[12,8,128]{2,1,0:T(8,128)S(1)}, f32[2,2,8,128]{3,2,1,0:T(8,128)S(1)}) custom-call(f32[12,8,128]{2,1,0:T(8,128)S(1)} %get-tuple-element.47.x_ref, f32[12,8,128]{2,1,0:T(8,128)S(1)} %get-tuple-element.48.v_ref, f32[12,8,128]{2,1,0:T(8,128)S(1)} %get-tuple-element.49.g_ref, ...), custom_call_target="tpu_custom_call" | custom-call | tf_op jit(solution)/shard_map/pallas_call | solution.py:409
  46.7 1.0 %collective-permute-done.6.got_ref = f32[2,2,8,128]{3,2,1,0:T(8,128)S(1)} collective-permute-done((f32[2,2,8,128]{3,2,1,0:T(8,128)S(1)}, f32[2,2,8,128]{3,2,1,0:T(8,128)S(1)}, u32[]{:S(2)}, u32[]{:S(2)}) %collective-permute-start.6) | collective-permute-done | bytes 16416 | tf_op jit(solution)/shard_map/ppermute | solution.py:481
  47.7 6.3 %shard_map.170 = (f32[12,8,128]{2,1,0:T(8,128)S(1)}, f32[12,8,128]{2,1,0:T(8,128)S(1)}, f32[12,8,128]{2,1,0:T(8,128)S(1)}, f32[2,2,8,128]{3,2,1,0:T(8,128)S(1)}) custom-call(f32[12,8,128]{2,1,0:T(8,128)S(1)} %get-tuple-element.51.x_ref, f32[12,8,128]{2,1,0:T(8,128)S(1)} %get-tuple-element.52.v_ref, f32[12,8,128]{2,1,0:T(8,128)S(1)} %get-tuple-element.53.g_ref, ...), custom_call_target="tpu_custom_call" | custom-call | tf_op jit(solution)/shard_map/pallas_call | solution.py:409
  54.2 1.0 %collective-permute-done.7.got_ref = f32[2,2,8,128]{3,2,1,0:T(8,128)S(1)} collective-permute-done((f32[2,2,8,128]{3,2,1,0:T(8,128)S(1)}, f32[2,2,8,128]{3,2,1,0:T(8,128)S(1)}, u32[]{:S(2)}, u32[]{:S(2)}) %collective-permute-start.7) | collective-permute-done | bytes 16416 | tf_op jit(solution)/shard_map/ppermute | solution.py:481
  55.3 6.9 %shard_map.171 = (f32[12,8,128]{2,1,0:T(8,128)}, f32[12,8,128]{2,1,0:T(8,128)}, f32[12,8,128]{2,1,0:T(8,128)}, f32[16,16,128]{2,1,0:T(8,128)S(1)}) custom-call(f32[12,8,128]{2,1,0:T(8,128)S(1)} %get-tuple-element.55.x_ref, f32[12,8,128]{2,1,0:T(8,128)S(1)} %get-tuple-element.56.v_ref, f32[12,8,128]{2,1,0:T(8,128)S(1)} %get-tuple-element.57.g_ref, ...), custom_call_target="tpu_custom_call" | custom-call | tf_op jit(solution)/shard_map/pallas_call | solution.py:409
  62.2 13.5 %all_to_all.5.got_ref = f32[16,16,128]{2,1,0:T(8,128)S(1)} all-to-all(f32[16,16,128]{2,1,0:T(8,128)S(1)} %get-tuple-element.59), channel_id=1, replica_groups=mesh['groups'=2,'dom'=16] {'dom'}, dimensions={0} | all-to-all | bytes 262144 | tf_op jit(solution)/shard_map/all_to_all | solution.py:559
  75.7 0.9 %shard_map.172 = (f32[3,8,192]{2,1,0:T(8,128)}, f32[3,8,192]{2,1,0:T(8,128)}, f32[3,8,192]{2,1,0:T(8,128)}) custom-call(f32[2,8]{1,0:T(2,128)S(1)} %pad_maximum_fusion.18.ladder_ref, f32[16,16,128]{2,1,0:T(8,128)S(1)} %all_to_all.5.got_ref), custom_call_target="tpu_custom_call" | custom-call | tf_op jit(solution)/shard_map/pallas_call | solution.py:445
  (99 shorter events, 2.8 us)
Async XLA Ops:
  0.6 0.7 copy-start.11
  1.4 0.8 copy-start.5
  2.2 0.8 %copy-start = (bf16[192,128]{1,0:T(8,128)(2,1)S(1)}, bf16[192,128]{1,0:T(8,128)(2,1)}, u32[]{:S(2)}) copy-start(bf16[192,128]{1,0:T(8,128)(2,1)} %param.18) | copy-start | bytes 147460
  3.0 7.7 %collective-permute-start = (bf16[264,128]{1,0:T(8,128)(2,1)S(1)}, bf16[264,128]{1,0:T(8,128)(2,1)S(1)}, u32[]{:S(2)}, u32[]{:S(2)}) collective-permute-start(bf16[264,128]{1,0:T(8,128)(2,1)S(1)} %pad_maximum_fusion.11), channel_id=1, source_target_pairs={{0,8},{1,9},{2,10},{3,11},{4,12},{5,13},{6,14},{7,15},{8,0},{9,1},... | collective-permute-start | bytes 202760 | tf_op jit(solution)/shard_map/ppermute | solution.py:481
  7.0 0.8 %copy-start.10 = (f32[8]{0:T(128)S(1)}, f32[8]{0:T(128)}, u32[]{:S(2)}) copy-start(f32[8]{0:T(128)} %param.17) | copy-start | bytes 100
  7.0 1.4 %copy-start.12 = (s32[8]{0:T(128)S(1)}, s32[8]{0:T(128)}, u32[]{:S(2)}) copy-start(s32[8]{0:T(128)} %param.19) | copy-start | bytes 100
  7.1 1.4 %copy-start.13 = (s32[8]{0:T(128)S(1)}, s32[8]{0:T(128)}, u32[]{:S(2)}) copy-start(s32[8]{0:T(128)} %param.20) | copy-start | bytes 100
  7.1 1.4 %copy-start.9 = (f32[128]{0:T(128)S(1)}, f32[128]{0:T(128)}, u32[]{:S(2)}) copy-start(f32[128]{0:T(128)} %param.23) | copy-start | bytes 1540
  7.1 0.7 copy-start.6
  7.1 1.4 %copy-start.7 = (f32[128]{0:T(128)S(1)}, f32[128]{0:T(128)}, u32[]{:S(2)}) copy-start(f32[128]{0:T(128)} %param.28) | copy-start | bytes 1540
  7.1 1.4 %copy-start.8 = (f32[128]{0:T(128)S(1)}, f32[128]{0:T(128)}, u32[]{:S(2)}) copy-start(f32[128]{0:T(128)} %param.27) | copy-start | bytes 1540
  7.1 1.4 %copy-start.3 = (bf16[128,128]{1,0:T(8,128)(2,1)S(1)}, bf16[128,128]{1,0:T(8,128)(2,1)}, u32[]{:S(2)}) copy-start(bf16[128,128]{1,0:T(8,128)(2,1)} %param.24) | copy-start | bytes 98308
  7.1 1.4 %copy-start.4 = (bf16[128,128]{1,0:T(8,128)(2,1)S(1)}, bf16[128,128]{1,0:T(8,128)(2,1)}, u32[]{:S(2)}) copy-start(bf16[128,128]{1,0:T(8,128)(2,1)} %param.21) | copy-start | bytes 98308
  7.2 1.4 %copy-start.1 = (bf16[128,128]{1,0:T(8,128)(2,1)S(1)}, bf16[128,128]{1,0:T(8,128)(2,1)}, u32[]{:S(2)}) copy-start(bf16[128,128]{1,0:T(8,128)(2,1)} %param.26) | copy-start | bytes 98308
  7.2 1.4 %copy-start.2 = (bf16[128,128]{1,0:T(8,128)(2,1)S(1)}, bf16[128,128]{1,0:T(8,128)(2,1)}, u32[]{:S(2)}) copy-start(bf16[128,128]{1,0:T(8,128)(2,1)} %param.25) | copy-start | bytes 98308
  10.9 4.9 %collective-permute-start.1 = (bf16[456,128]{1,0:T(8,128)(2,1)S(1)}, bf16[456,128]{1,0:T(8,128)(2,1)S(1)}, u32[]{:S(2)}, u32[]{:S(2)}) collective-permute-start(bf16[456,128]{1,0:T(8,128)(2,1)S(1)} %pad_maximum_fusion.8), channel_id=1, source_target_pairs={{0,4},{1,5},{2,6},{3,7},{4,0},{5,1},{6,2},{7,3},{8,12},{9,13},{10,... | collective-permute-start | bytes 350216 | tf_op jit(solution)/shard_map/ppermute | solution.py:481
  16.0 5.9 %collective-permute-start.2 = (bf16[840,128]{1,0:T(8,128)(2,1)S(1)}, bf16[840,128]{1,0:T(8,128)(2,1)S(1)}, u32[]{:S(2)}, u32[]{:S(2)}) collective-permute-start(bf16[840,128]{1,0:T(8,128)(2,1)S(1)} %pad_maximum_fusion.4), channel_id=1, source_target_pairs={{0,2},{1,3},{2,0},{3,1},{4,6},{5,7},{6,4},{7,5},{8,10},{9,11},{10,... | collective-permute-start | bytes 645128 | tf_op jit(solution)/shard_map/ppermute | solution.py:481
  22.3 1.8 %collective-permute-start.3 = (bf16[1680,128]{1,0:T(8,128)(2,1)S(1)}, bf16[1680,128]{1,0:T(8,128)(2,1)S(1)}, u32[]{:S(2)}, u32[]{:S(2)}) collective-permute-start(bf16[1680,128]{1,0:T(8,128)(2,1)S(1)} %pad_maximum_fusion.1), channel_id=1, source_target_pairs={{0,1},{1,0},{2,3},{3,2},{4,5},{5,4},{6,7},{7,6},{8,9},{9,8},{10,11... | collective-permute-start | bytes 1290248 | tf_op jit(solution)/shard_map/ppermute | solution.py:481
  31.5 1.2 %collective-permute-start.4 = (f32[2,2,8,128]{3,2,1,0:T(8,128)S(1)}, f32[2,2,8,128]{3,2,1,0:T(8,128)S(1)}, u32[]{:S(2)}, u32[]{:S(2)}) collective-permute-start(f32[2,2,8,128]{3,2,1,0:T(8,128)S(1)} %get-tuple-element.46.edge_ref), channel_id=1, source_target_pairs={{0,1},{1,0},{2,3},{3,2},{4,5},{5,4},{6,7},{7,6},{8,9},{9,8},{10,11... | collective-permute-start | bytes 49160 | tf_op jit(solution)/shard_map/ppermute | solution.py:481
  39.0 1.2 %collective-permute-start.5 = (f32[2,2,8,128]{3,2,1,0:T(8,128)S(1)}, f32[2,2,8,128]{3,2,1,0:T(8,128)S(1)}, u32[]{:S(2)}, u32[]{:S(2)}) collective-permute-start(f32[2,2,8,128]{3,2,1,0:T(8,128)S(1)} %get-tuple-element.50.edge_ref), channel_id=1, source_target_pairs={{0,1},{1,0},{2,3},{3,2},{4,5},{5,4},{6,7},{7,6},{8,9},{9,8},{10,11... | collective-permute-start | bytes 49160 | tf_op jit(solution)/shard_map/ppermute | solution.py:481
  46.5 1.2 %collective-permute-start.6 = (f32[2,2,8,128]{3,2,1,0:T(8,128)S(1)}, f32[2,2,8,128]{3,2,1,0:T(8,128)S(1)}, u32[]{:S(2)}, u32[]{:S(2)}) collective-permute-start(f32[2,2,8,128]{3,2,1,0:T(8,128)S(1)} %get-tuple-element.54.edge_ref), channel_id=1, source_target_pairs={{0,1},{1,0},{2,3},{3,2},{4,5},{5,4},{6,7},{7,6},{8,9},{9,8},{10,11... | collective-permute-start | bytes 49160 | tf_op jit(solution)/shard_map/ppermute | solution.py:481
  54.1 1.2 %collective-permute-start.7 = (f32[2,2,8,128]{3,2,1,0:T(8,128)S(1)}, f32[2,2,8,128]{3,2,1,0:T(8,128)S(1)}, u32[]{:S(2)}, u32[]{:S(2)}) collective-permute-start(f32[2,2,8,128]{3,2,1,0:T(8,128)S(1)} %get-tuple-element.58.edge_ref), channel_id=1, source_target_pairs={{0,1},{1,0},{2,3},{3,2},{4,5},{5,4},{6,7},{7,6},{8,9},{9,8},{10,11... | collective-permute-start | bytes 49160 | tf_op jit(solution)/shard_map/ppermute | solution.py:481

commit v6 on v5

--- a/solution.py
+++ b/solution.py
@@ -19,6 +19,7 @@
 step_time = 0.05
 motion_work_lower_limit = 1e-06
 LOG2E = math.log2(math.e)
+STEP_INPUTS = 11
 VMEM_SPEC = pl.BlockSpec(memory_space=pltpu.VMEM)
 
 
@@ -398,6 +399,11 @@
     )(state, features, weights, small)
 
 
+def advance_last(stage, parts_count, *refs):
+    inputs, last, state, rest = refs[:STEP_INPUTS], refs[STEP_INPUTS], refs[STEP_INPUTS + 1 :][:3], refs[STEP_INPUTS + 4 :]
+    advance(stage, parts_count, *inputs, *state, last, *rest)
+
+
 def run_advance(stage, parts_count, last_shape, x, v, g, edge, got, own_feat, table, message_push, later_push, weights, small):
     own_pairs = v.shape[0]
     channels = table.shape[1]
@@ -406,12 +412,15 @@
     lhs = pltpu.VMEM(((basis_count + 3) * NA, PAIR), jnp.bfloat16)
     vec = pltpu.VMEM((3 * NA, PAIR), jnp.bfloat16)
     message = pltpu.VMEM((PAIR, 2 * channels), jnp.bfloat16)
-    return pl.pallas_call(
-        functools.partial(advance, stage, parts_count),
-        out_shape=(tiles, tiles, tiles, jax.ShapeDtypeStruct(last_shape, jnp.float32)),
-        in_specs=[VMEM_SPEC] * 11,
-        out_specs=(VMEM_SPEC,) * 4,
-        scratch_shapes=[
+    last = stage == 3
+    state = [] if last else [tiles] * 3
+    outs = pl.pallas_call(
+        functools.partial(advance_last if last else advance, stage, parts_count),
+        out_shape=(*state, jax.ShapeDtypeStruct(last_shape, jnp.float32)),
+        in_specs=[VMEM_SPEC] * STEP_INPUTS,
+        out_specs=(VMEM_SPEC,) * (len(state) + 1),
+        scratch_shapes=([pltpu.VMEM(v.shape, jnp.float32)] * 3 if last else [])
+        + [
             pltpu.VMEM((own_pairs + 2, 8, PAIR), jnp.float32),
             pltpu.VMEM((own_pairs + 1, 8, PAIR), jnp.float32),
             [[lhs] * 3] * 2,
@@ -422,6 +431,7 @@
         ],
         compiler_params=pltpu.CompilerParams(vmem_limit_bytes=20 * 1024 * 1024),
     )(x, v, g, edge, got, own_feat, table, message_push, later_push, weights, small)
+    return (None, None, None, *outs) if last else outs
 
 
 def run_steps(state, features, per_replica, chunk_shape, exchange, weights, small):

time: 76.9 us -> 76.3 us (level)
  no operation moved by 1% of the time
where the time goes in v6:
time: 76.3 us; the launch traced here: 76 us
  Pallas kernels  32.9 us (43%)
  waiting for transfers between devices  15.6 us (20%)
  blocking collectives  13.5 us (18%)
  starting transfers between devices  7.26 us (10%)
  local copies, waits for them, and re-layouts  3.92 us (5%)
  other arithmetic  1.57 us (2%)
  between operations  1.25 us (2%)
    pallas_call x5, Pallas kernels, run_advance(): pl.pallas_call(functools.partial(advance_last if last else advance, stage...  31.7 us
    ppermute x8, waiting for transfers between devices, trade(): return lax.ppermute(value, 'dom', [(i, i ^ mask) for i in range(devices)])  15.6 us
    all_to_all x1, blocking collectives, on_device(): got = lax.all_to_all(chunks, 'dom', 0, 0)  13.5 us
    ppermute x8, starting transfers between devices, trade(): return lax.ppermute(value, 'dom', [(i, i ^ mask) for i in range(devices)])  7.26 us
    unnamed x28, local copies, waits for them, and re-layouts  1.89 us
  transfers between devices with their start and end apart: 8, of which 8 were waited for; matrix products, arithmetic and copies ran while one was open for 2% of the time, Pallas kernels for 0%

profile of v6, /device:TPU:0, one launch (start us, length us, event | category | flops | bytes accessed | tf_op | source)
XLA Modules:
  0.0 76.0 jit_solution(9052591800405087612)
XLA Ops:
  0.7 0.6 copy-done.11
  1.4 0.7 subtract_bitcast_fusion
  2.3 0.7 copy-done
  3.0 4.0 %collective-permute-start = (bf16[264,128]{1,0:T(8,128)(2,1)S(1)}, bf16[264,128]{1,0:T(8,128)(2,1)S(1)}, u32[]{:S(2)}, u32[]{:S(2)}) collective-permute-start(bf16[264,128]{1,0:T(8,128)(2,1)S(1)} %pad_maximum_fusion.11), channel_id=1, source_target_pairs={{0,8},{1,9},{2,10},{3,11},{4,12},{5,13},{6,14},{7,15},{8,0},{9,1},... | collective-permute-start | bytes 202760 | tf_op jit(solution)/shard_map/ppermute | solution.py:491
  7.3 0.5 copy-done.6
  7.9 0.6 dynamic_slice.3
  8.6 0.6 broadcast_in_dim.37
  9.3 1.4 %collective-permute-done = bf16[264,128]{1,0:T(8,128)(2,1)S(1)} collective-permute-done((bf16[264,128]{1,0:T(8,128)(2,1)S(1)}, bf16[264,128]{1,0:T(8,128)(2,1)S(1)}, u32[]{:S(2)}, u32[]{:S(2)}) %collective-permute-start) | collective-permute-done | bytes 67616 | tf_op jit(solution)/shard_map/ppermute | solution.py:491
  10.9 0.7 collective-permute-start.1
  11.6 4.2 %collective-permute-done.1 = bf16[456,128]{1,0:T(8,128)(2,1)S(1)} collective-permute-done((bf16[456,128]{1,0:T(8,128)(2,1)S(1)}, bf16[456,128]{1,0:T(8,128)(2,1)S(1)}, u32[]{:S(2)}, u32[]{:S(2)}) %collective-permute-start.1) | collective-permute-done | bytes 116768 | tf_op jit(solution)/shard_map/ppermute | solution.py:491
  16.0 1.8 %collective-permute-start.2 = (bf16[840,128]{1,0:T(8,128)(2,1)S(1)}, bf16[840,128]{1,0:T(8,128)(2,1)S(1)}, u32[]{:S(2)}, u32[]{:S(2)}) collective-permute-start(bf16[840,128]{1,0:T(8,128)(2,1)S(1)} %pad_maximum_fusion.4), channel_id=1, source_target_pairs={{0,2},{1,3},{2,0},{3,1},{4,6},{5,7},{6,4},{7,5},{8,10},{9,11},{10,... | collective-permute-start | bytes 645128 | tf_op jit(solution)/shard_map/ppermute | solution.py:491
  17.8 4.1 %collective-permute-done.2 = bf16[840,128]{1,0:T(8,128)(2,1)S(1)} collective-permute-done((bf16[840,128]{1,0:T(8,128)(2,1)S(1)}, bf16[840,128]{1,0:T(8,128)(2,1)S(1)}, u32[]{:S(2)}, u32[]{:S(2)}) %collective-permute-start.2) | collective-permute-done | bytes 215072 | tf_op jit(solution)/shard_map/ppermute | solution.py:491
  22.4 1.7 %collective-permute-done.3 = bf16[1680,128]{1,0:T(8,128)(2,1)S(1)} collective-permute-done((bf16[1680,128]{1,0:T(8,128)(2,1)S(1)}, bf16[1680,128]{1,0:T(8,128)(2,1)S(1)}, u32[]{:S(2)}, u32[]{:S(2)}) %collective-permute-start.3) | collective-permute-done | bytes 430112 | tf_op jit(solution)/shard_map/ppermute | solution.py:491
  25.1 6.4 %shard_map.167 = (f32[12,8,128]{2,1,0:T(8,128)S(1)}, f32[12,8,128]{2,1,0:T(8,128)S(1)}, f32[12,8,128]{2,1,0:T(8,128)S(1)}, f32[2,2,8,128]{3,2,1,0:T(8,128)S(1)}) custom-call(f32[14,8,128]{2,1,0:T(8,128)S(1)} %get-tuple-element.36.x_ref, f32[12,8,128]{2,1,0:T(8,128)S(1)} %get-tuple-element.37.v_ref.g_ref, f32[12,8,128]{2,1,0:T(8,128)S(1)} %get-tuple-element.37.v_ref.g_ref, ...), custom_call_target="tpu_custom_call" | custom-call | tf_op jit(solution)/shard_map/pallas_call | solution.py:417
  31.7 1.1 %collective-permute-done.4.got_ref = f32[2,2,8,128]{3,2,1,0:T(8,128)S(1)} collective-permute-done((f32[2,2,8,128]{3,2,1,0:T(8,128)S(1)}, f32[2,2,8,128]{3,2,1,0:T(8,128)S(1)}, u32[]{:S(2)}, u32[]{:S(2)}) %collective-permute-start.4) | collective-permute-done | bytes 16416 | tf_op jit(solution)/shard_map/ppermute | solution.py:491
  32.7 6.3 %shard_map.168 = (f32[12,8,128]{2,1,0:T(8,128)S(1)}, f32[12,8,128]{2,1,0:T(8,128)S(1)}, f32[12,8,128]{2,1,0:T(8,128)S(1)}, f32[2,2,8,128]{3,2,1,0:T(8,128)S(1)}) custom-call(f32[12,8,128]{2,1,0:T(8,128)S(1)} %get-tuple-element.42.x_ref, f32[12,8,128]{2,1,0:T(8,128)S(1)} %get-tuple-element.43.v_ref, f32[12,8,128]{2,1,0:T(8,128)S(1)} %get-tuple-element.44.g_ref, ...), custom_call_target="tpu_custom_call" | custom-call | tf_op jit(solution)/shard_map/pallas_call | solution.py:417
  39.2 1.0 %collective-permute-done.5.got_ref = f32[2,2,8,128]{3,2,1,0:T(8,128)S(1)} collective-permute-done((f32[2,2,8,128]{3,2,1,0:T(8,128)S(1)}, f32[2,2,8,128]{3,2,1,0:T(8,128)S(1)}, u32[]{:S(2)}, u32[]{:S(2)}) %collective-permute-start.5) | collective-permute-done | bytes 16416 | tf_op jit(solution)/shard_map/ppermute | solution.py:491
  40.2 6.3 %shard_map.169 = (f32[12,8,128]{2,1,0:T(8,128)S(1)}, f32[12,8,128]{2,1,0:T(8,128)S(1)}, f32[12,8,128]{2,1,0:T(8,128)S(1)}, f32[2,2,8,128]{3,2,1,0:T(8,128)S(1)}) custom-call(f32[12,8,128]{2,1,0:T(8,128)S(1)} %get-tuple-element.46.x_ref, f32[12,8,128]{2,1,0:T(8,128)S(1)} %get-tuple-element.47.v_ref, f32[12,8,128]{2,1,0:T(8,128)S(1)} %get-tuple-element.48.g_ref, ...), custom_call_target="tpu_custom_call" | custom-call | tf_op jit(solution)/shard_map/pallas_call | solution.py:417
  46.7 1.0 %collective-permute-done.6.got_ref = f32[2,2,8,128]{3,2,1,0:T(8,128)S(1)} collective-permute-done((f32[2,2,8,128]{3,2,1,0:T(8,128)S(1)}, f32[2,2,8,128]{3,2,1,0:T(8,128)S(1)}, u32[]{:S(2)}, u32[]{:S(2)}) %collective-permute-start.6) | collective-permute-done | bytes 16416 | tf_op jit(solution)/shard_map/ppermute | solution.py:491
  47.7 6.3 %shard_map.170 = (f32[12,8,128]{2,1,0:T(8,128)S(1)}, f32[12,8,128]{2,1,0:T(8,128)S(1)}, f32[12,8,128]{2,1,0:T(8,128)S(1)}, f32[2,2,8,128]{3,2,1,0:T(8,128)S(1)}) custom-call(f32[12,8,128]{2,1,0:T(8,128)S(1)} %get-tuple-element.50.x_ref, f32[12,8,128]{2,1,0:T(8,128)S(1)} %get-tuple-element.51.v_ref, f32[12,8,128]{2,1,0:T(8,128)S(1)} %get-tuple-element.52.g_ref, ...), custom_call_target="tpu_custom_call" | custom-call | tf_op jit(solution)/shard_map/pallas_call | solution.py:417
  54.2 1.0 %collective-permute-done.7.refs_4_ = f32[2,2,8,128]{3,2,1,0:T(8,128)S(1)} collective-permute-done((f32[2,2,8,128]{3,2,1,0:T(8,128)S(1)}, f32[2,2,8,128]{3,2,1,0:T(8,128)S(1)}, u32[]{:S(2)}, u32[]{:S(2)}) %collective-permute-start.7) | collective-permute-done | bytes 16416 | tf_op jit(solution)/shard_map/ppermute | solution.py:491
  55.2 6.4 %shard_map.171 = f32[16,16,128]{2,1,0:T(8,128)S(1)} custom-call(f32[12,8,128]{2,1,0:T(8,128)S(1)} %get-tuple-element.54.refs_0_, f32[12,8,128]{2,1,0:T(8,128)S(1)} %get-tuple-element.55.refs_1_, f32[12,8,128]{2,1,0:T(8,128)S(1)} %get-tuple-element.56.refs_2_, f32[2,2,8,128]{3,2,1,0:T(8,128)S(1)} %get-tuple-element.57.refs_3_, ...), custom_call_target="tpu_custom_call" | custom-call | tf_op jit(solution)/shard_map/pallas_call | solution.py:417
  61.6 13.5 %all_to_all.5.got_ref = f32[16,16,128]{2,1,0:T(8,128)S(1)} all-to-all(f32[16,16,128]{2,1,0:T(8,128)S(1)} %shard_map.171), channel_id=1, replica_groups=mesh['groups'=2,'dom'=16] {'dom'}, dimensions={0} | all-to-all | bytes 262144 | tf_op jit(solution)/shard_map/all_to_all | solution.py:569
  75.1 0.9 %shard_map.172 = (f32[3,8,192]{2,1,0:T(8,128)}, f32[3,8,192]{2,1,0:T(8,128)}, f32[3,8,192]{2,1,0:T(8,128)}) custom-call(f32[2,8]{1,0:T(2,128)S(1)} %pad_maximum_fusion.18.ladder_ref, f32[16,16,128]{2,1,0:T(8,128)S(1)} %all_to_all.5.got_ref), custom_call_target="tpu_custom_call" | custom-call | tf_op jit(solution)/shard_map/pallas_call | solution.py:455
  (99 shorter events, 2.8 us)
Async XLA Ops:
  0.6 0.7 copy-start.11
  1.4 0.8 copy-start.5
  2.2 0.8 %copy-start = (bf16[192,128]{1,0:T(8,128)(2,1)S(1)}, bf16[192,128]{1,0:T(8,128)(2,1)}, u32[]{:S(2)}) copy-start(bf16[192,128]{1,0:T(8,128)(2,1)} %param.18) | copy-start | bytes 147460
  3.0 7.7 %collective-permute-start = (bf16[264,128]{1,0:T(8,128)(2,1)S(1)}, bf16[264,128]{1,0:T(8,128)(2,1)S(1)}, u32[]{:S(2)}, u32[]{:S(2)}) collective-permute-start(bf16[264,128]{1,0:T(8,128)(2,1)S(1)} %pad_maximum_fusion.11), channel_id=1, source_target_pairs={{0,8},{1,9},{2,10},{3,11},{4,12},{5,13},{6,14},{7,15},{8,0},{9,1},... | collective-permute-start | bytes 202760 | tf_op jit(solution)/shard_map/ppermute | solution.py:491
  7.0 0.8 %copy-start.10 = (f32[8]{0:T(128)S(1)}, f32[8]{0:T(128)}, u32[]{:S(2)}) copy-start(f32[8]{0:T(128)} %param.17) | copy-start | bytes 100
  7.0 1.4 %copy-start.12 = (s32[8]{0:T(128)S(1)}, s32[8]{0:T(128)}, u32[]{:S(2)}) copy-start(s32[8]{0:T(128)} %param.19) | copy-start | bytes 100
  7.1 1.4 %copy-start.13 = (s32[8]{0:T(128)S(1)}, s32[8]{0:T(128)}, u32[]{:S(2)}) copy-start(s32[8]{0:T(128)} %param.20) | copy-start | bytes 100
  7.1 1.4 %copy-start.9 = (f32[128]{0:T(128)S(1)}, f32[128]{0:T(128)}, u32[]{:S(2)}) copy-start(f32[128]{0:T(128)} %param.23) | copy-start | bytes 1540
  7.1 0.7 copy-start.6
  7.1 1.4 %copy-start.7 = (f32[128]{0:T(128)S(1)}, f32[128]{0:T(128)}, u32[]{:S(2)}) copy-start(f32[128]{0:T(128)} %param.28) | copy-start | bytes 1540
  7.1 1.4 %copy-start.8 = (f32[128]{0:T(128)S(1)}, f32[128]{0:T(128)}, u32[]{:S(2)}) copy-start(f32[128]{0:T(128)} %param.27) | copy-start | bytes 1540
  7.1 1.4 %copy-start.3 = (bf16[128,128]{1,0:T(8,128)(2,1)S(1)}, bf16[128,128]{1,0:T(8,128)(2,1)}, u32[]{:S(2)}) copy-start(bf16[128,128]{1,0:T(8,128)(2,1)} %param.24) | copy-start | bytes 98308
  7.1 1.4 %copy-start.4 = (bf16[128,128]{1,0:T(8,128)(2,1)S(1)}, bf16[128,128]{1,0:T(8,128)(2,1)}, u32[]{:S(2)}) copy-start(bf16[128,128]{1,0:T(8,128)(2,1)} %param.21) | copy-start | bytes 98308
  7.2 1.4 %copy-start.1 = (bf16[128,128]{1,0:T(8,128)(2,1)S(1)}, bf16[128,128]{1,0:T(8,128)(2,1)}, u32[]{:S(2)}) copy-start(bf16[128,128]{1,0:T(8,128)(2,1)} %param.26) | copy-start | bytes 98308
  7.2 1.4 %copy-start.2 = (bf16[128,128]{1,0:T(8,128)(2,1)S(1)}, bf16[128,128]{1,0:T(8,128)(2,1)}, u32[]{:S(2)}) copy-start(bf16[128,128]{1,0:T(8,128)(2,1)} %param.25) | copy-start | bytes 98308
  10.9 4.9 %collective-permute-start.1 = (bf16[456,128]{1,0:T(8,128)(2,1)S(1)}, bf16[456,128]{1,0:T(8,128)(2,1)S(1)}, u32[]{:S(2)}, u32[]{:S(2)}) collective-permute-start(bf16[456,128]{1,0:T(8,128)(2,1)S(1)} %pad_maximum_fusion.8), channel_id=1, source_target_pairs={{0,4},{1,5},{2,6},{3,7},{4,0},{5,1},{6,2},{7,3},{8,12},{9,13},{10,... | collective-permute-start | bytes 350216 | tf_op jit(solution)/shard_map/ppermute | solution.py:491
  16.0 5.9 %collective-permute-start.2 = (bf16[840,128]{1,0:T(8,128)(2,1)S(1)}, bf16[840,128]{1,0:T(8,128)(2,1)S(1)}, u32[]{:S(2)}, u32[]{:S(2)}) collective-permute-start(bf16[840,128]{1,0:T(8,128)(2,1)S(1)} %pad_maximum_fusion.4), channel_id=1, source_target_pairs={{0,2},{1,3},{2,0},{3,1},{4,6},{5,7},{6,4},{7,5},{8,10},{9,11},{10,... | collective-permute-start | bytes 645128 | tf_op jit(solution)/shard_map/ppermute | solution.py:491
  22.3 1.8 %collective-permute-start.3 = (bf16[1680,128]{1,0:T(8,128)(2,1)S(1)}, bf16[1680,128]{1,0:T(8,128)(2,1)S(1)}, u32[]{:S(2)}, u32[]{:S(2)}) collective-permute-start(bf16[1680,128]{1,0:T(8,128)(2,1)S(1)} %pad_maximum_fusion.1), channel_id=1, source_target_pairs={{0,1},{1,0},{2,3},{3,2},{4,5},{5,4},{6,7},{7,6},{8,9},{9,8},{10,11... | collective-permute-start | bytes 1290248 | tf_op jit(solution)/shard_map/ppermute | solution.py:491
  31.5 1.2 %collective-permute-start.4 = (f32[2,2,8,128]{3,2,1,0:T(8,128)S(1)}, f32[2,2,8,128]{3,2,1,0:T(8,128)S(1)}, u32[]{:S(2)}, u32[]{:S(2)}) collective-permute-start(f32[2,2,8,128]{3,2,1,0:T(8,128)S(1)} %get-tuple-element.45.edge_ref), channel_id=1, source_target_pairs={{0,1},{1,0},{2,3},{3,2},{4,5},{5,4},{6,7},{7,6},{8,9},{9,8},{10,11... | collective-permute-start | bytes 49160 | tf_op jit(solution)/shard_map/ppermute | solution.py:491
  39.0 1.2 %collective-permute-start.5 = (f32[2,2,8,128]{3,2,1,0:T(8,128)S(1)}, f32[2,2,8,128]{3,2,1,0:T(8,128)S(1)}, u32[]{:S(2)}, u32[]{:S(2)}) collective-permute-start(f32[2,2,8,128]{3,2,1,0:T(8,128)S(1)} %get-tuple-element.49.edge_ref), channel_id=1, source_target_pairs={{0,1},{1,0},{2,3},{3,2},{4,5},{5,4},{6,7},{7,6},{8,9},{9,8},{10,11... | collective-permute-start | bytes 49160 | tf_op jit(solution)/shard_map/ppermute | solution.py:491
  46.5 1.2 %collective-permute-start.6 = (f32[2,2,8,128]{3,2,1,0:T(8,128)S(1)}, f32[2,2,8,128]{3,2,1,0:T(8,128)S(1)}, u32[]{:S(2)}, u32[]{:S(2)}) collective-permute-start(f32[2,2,8,128]{3,2,1,0:T(8,128)S(1)} %get-tuple-element.53.edge_ref), channel_id=1, source_target_pairs={{0,1},{1,0},{2,3},{3,2},{4,5},{5,4},{6,7},{7,6},{8,9},{9,8},{10,11... | collective-permute-start | bytes 49160 | tf_op jit(solution)/shard_map/ppermute | solution.py:491
  54.0 1.2 %collective-permute-start.7 = (f32[2,2,8,128]{3,2,1,0:T(8,128)S(1)}, f32[2,2,8,128]{3,2,1,0:T(8,128)S(1)}, u32[]{:S(2)}, u32[]{:S(2)}) collective-permute-start(f32[2,2,8,128]{3,2,1,0:T(8,128)S(1)} %get-tuple-element.57.refs_3_), channel_id=1, source_target_pairs={{0,1},{1,0},{2,3},{3,2},{4,5},{5,4},{6,7},{7,6},{8,9},{9,8},{10,11... | collective-permute-start | bytes 49160 | tf_op jit(solution)/shard_map/ppermute | solution.py:491

commit v7 on v6

--- a/solution.py
+++ b/solution.py
@@ -301,6 +301,12 @@
             last_out[edge, 1] = jnp.where(sub == 3, kinetic, v[p])
         return
     x_out[...] = x
+    part = small_ref[basis_count + 6 : basis_count + 7, :]
+    for p in range(own_pairs):
+        floor = part * float(2 * own_pairs) + float(2 * p) + jnp.where(low, 0.0, 1.0)
+        x_out[p] = x_out[p] - jnp.where(sub == 2, floor, 0.0)
+    kinetic_high = kinetic.astype(jnp.bfloat16).astype(jnp.float32)
+    kinetic = jnp.where(low, kinetic_high, kinetic - kinetic_high)
     rows = jnp.concatenate(
         [
             jnp.concatenate([x_out[p, 0:3], v_out[p, 0:3], g_out[p, 0:3]], axis=0)
@@ -313,8 +319,7 @@
     whole = width // PAIR
     last_out[...] = jnp.zeros(last_out.shape, jnp.float32)
     end = last_out.shape[1] - 1
-    last_out[:, end:, :] = jnp.broadcast_to(kinetic.reshape(1, 1, 1), (last_out.shape[0], 1, PAIR))
-    part = small_ref[basis_count + 6 : basis_count + 7, :]
+    last_out[:, end:, :] = jnp.broadcast_to(kinetic.reshape(1, 1, PAIR), (last_out.shape[0], 1, PAIR))
     for chunk in range(parts_count * chunks):
         chosen = part == float(chunk // chunks)
         at = chunk % chunks * width
@@ -338,13 +343,13 @@
     outs = (x_out, v_out, g_out)
     pieces_of = [[] for _ in range(9)]
     factors = []
-    sources = [got_ref[s * group + part] for s in range(replicas)]
+    sources = [got_ref[s * group + part].astype(jnp.float32) for s in range(replicas)]
     kinetics = []
     for s in range(replicas):
-        kinetic = got_ref[s * group, chunk_rows - 1 :, :]
+        kinetic = got_ref[s * group].astype(jnp.float32)[chunk_rows - 1 :]
         for other in range(1, group):
-            kinetic = kinetic + got_ref[s * group + other, chunk_rows - 1 :, :]
-        kinetics.append(kinetic)
+            kinetic = kinetic + got_ref[s * group + other].astype(jnp.float32)[chunk_rows - 1 :]
+        kinetics.append(kinetic + pltpu.roll(kinetic, NA, 1))
     targets = [jnp.broadcast_to(ladder_ref[0:1, r : r + 1], (1, PAIR)) for r in range(replicas)]
     source_targets = []
     for r in range(replicas):
@@ -371,10 +376,7 @@
         for index in range(len(pieces_of[row][0])):
             value = jnp.concatenate([of_replica[index] for of_replica in pieces_of[row]], axis=0)
             size = value.shape[1]
-            if row == 2:
-                lane = lax.broadcasted_iota(jnp.int32, value.shape, 1)
-                value = value - (domain * (width // NA) + (index * PAIR + lane) // NA).astype(jnp.float32)
-            elif row // 3 == 1:
+            if row // 3 == 1:
                 value = value * factor[:, :size]
             outs[row // 3][row % 3, :, index * PAIR : index * PAIR + size] = value
 
@@ -566,7 +568,7 @@
     chunk_rows = 9 * (local_atoms // PAIR) + (5 if local_atoms % PAIR else 0) + 1
     chunk_rows = -(-chunk_rows // 8) * 8
     chunks = run_steps(state, features, per_replica, (devices, chunk_rows, PAIR), exchange, weights, small)
-    got = lax.all_to_all(chunks, "dom", 0, 0)
+    got = lax.all_to_all(chunks.astype(jnp.bfloat16), "dom", 0, 0)
     return run_finish(ladder, got, local_atoms)
 
 

time: 76.3 us -> 75.3 us (0.987)
  blocking collectives: 13.5 us -> 12.4 us
    all_to_all x1, blocking collectives: 13.5 us -> 12.4 us  [on_device(): got = lax.all_to_all(chunks.astype(jnp.bfloat16), 'dom', 0, 0)]
where the time goes in v7:
time: 75.3 us; the launch traced here: 75 us
  Pallas kernels  32.9 us (44%)
  waiting for transfers between devices  15.6 us (21%)
  blocking collectives  12.4 us (16%)
  starting transfers between devices  7.26 us (10%)
  local copies, waits for them, and re-layouts  3.92 us (5%)
  other arithmetic  1.58 us (2%)
  between operations  1.25 us (2%)
    pallas_call x5, Pallas kernels, run_advance(): pl.pallas_call(functools.partial(advance_last if last else advance, stage...  31.7 us
    ppermute x8, waiting for transfers between devices, trade(): return lax.ppermute(value, 'dom', [(i, i ^ mask) for i in range(devices)])  15.6 us
    all_to_all x1, blocking collectives, on_device(): got = lax.all_to_all(chunks.astype(jnp.bfloat16), 'dom', 0, 0)  12.4 us
    ppermute x8, starting transfers between devices, trade(): return lax.ppermute(value, 'dom', [(i, i ^ mask) for i in range(devices)])  7.26 us
    unnamed x28, local copies, waits for them, and re-layouts  1.89 us
  transfers between devices with their start and end apart: 8, of which 8 were waited for; matrix products, arithmetic and copies ran while one was open for 2% of the time, Pallas kernels for 0%

profile of v7, /device:TPU:0, one launch (start us, length us, event | category | flops | bytes accessed | tf_op | source)
XLA Modules:
  0.0 75.0 jit_solution(10031495262622468203)
XLA Ops:
  0.7 0.6 copy-done.11
  1.4 0.7 subtract_bitcast_fusion
  2.3 0.7 copy-done
  3.0 4.0 %collective-permute-start = (bf16[264,128]{1,0:T(8,128)(2,1)S(1)}, bf16[264,128]{1,0:T(8,128)(2,1)S(1)}, u32[]{:S(2)}, u32[]{:S(2)}) collective-permute-start(bf16[264,128]{1,0:T(8,128)(2,1)S(1)} %pad_maximum_fusion.11), channel_id=1, source_target_pairs={{0,8},{1,9},{2,10},{3,11},{4,12},{5,13},{6,14},{7,15},{8,0},{9,1},... | collective-permute-start | bytes 202760 | tf_op jit(solution)/shard_map/ppermute | solution.py:493
  7.3 0.5 copy-done.6
  7.9 0.6 dynamic_slice.3
  8.6 0.6 broadcast_in_dim.37
  9.3 1.4 %collective-permute-done = bf16[264,128]{1,0:T(8,128)(2,1)S(1)} collective-permute-done((bf16[264,128]{1,0:T(8,128)(2,1)S(1)}, bf16[264,128]{1,0:T(8,128)(2,1)S(1)}, u32[]{:S(2)}, u32[]{:S(2)}) %collective-permute-start) | collective-permute-done | bytes 67616 | tf_op jit(solution)/shard_map/ppermute | solution.py:493
  10.9 0.7 collective-permute-start.1
  11.6 4.2 %collective-permute-done.1 = bf16[456,128]{1,0:T(8,128)(2,1)S(1)} collective-permute-done((bf16[456,128]{1,0:T(8,128)(2,1)S(1)}, bf16[456,128]{1,0:T(8,128)(2,1)S(1)}, u32[]{:S(2)}, u32[]{:S(2)}) %collective-permute-start.1) | collective-permute-done | bytes 116768 | tf_op jit(solution)/shard_map/ppermute | solution.py:493
  16.0 1.8 %collective-permute-start.2 = (bf16[840,128]{1,0:T(8,128)(2,1)S(1)}, bf16[840,128]{1,0:T(8,128)(2,1)S(1)}, u32[]{:S(2)}, u32[]{:S(2)}) collective-permute-start(bf16[840,128]{1,0:T(8,128)(2,1)S(1)} %pad_maximum_fusion.4), channel_id=1, source_target_pairs={{0,2},{1,3},{2,0},{3,1},{4,6},{5,7},{6,4},{7,5},{8,10},{9,11},{10,... | collective-permute-start | bytes 645128 | tf_op jit(solution)/shard_map/ppermute | solution.py:493
  17.8 4.1 %collective-permute-done.2 = bf16[840,128]{1,0:T(8,128)(2,1)S(1)} collective-permute-done((bf16[840,128]{1,0:T(8,128)(2,1)S(1)}, bf16[840,128]{1,0:T(8,128)(2,1)S(1)}, u32[]{:S(2)}, u32[]{:S(2)}) %collective-permute-start.2) | collective-permute-done | bytes 215072 | tf_op jit(solution)/shard_map/ppermute | solution.py:493
  22.4 1.7 %collective-permute-done.3 = bf16[1680,128]{1,0:T(8,128)(2,1)S(1)} collective-permute-done((bf16[1680,128]{1,0:T(8,128)(2,1)S(1)}, bf16[1680,128]{1,0:T(8,128)(2,1)S(1)}, u32[]{:S(2)}, u32[]{:S(2)}) %collective-permute-start.3) | collective-permute-done | bytes 430112 | tf_op jit(solution)/shard_map/ppermute | solution.py:493
  25.1 6.4 %shard_map.167 = (f32[12,8,128]{2,1,0:T(8,128)S(1)}, f32[12,8,128]{2,1,0:T(8,128)S(1)}, f32[12,8,128]{2,1,0:T(8,128)S(1)}, f32[2,2,8,128]{3,2,1,0:T(8,128)S(1)}) custom-call(f32[14,8,128]{2,1,0:T(8,128)S(1)} %get-tuple-element.36.x_ref, f32[12,8,128]{2,1,0:T(8,128)S(1)} %get-tuple-element.37.v_ref.g_ref, f32[12,8,128]{2,1,0:T(8,128)S(1)} %get-tuple-element.37.v_ref.g_ref, ...), custom_call_target="tpu_custom_call" | custom-call | tf_op jit(solution)/shard_map/pallas_call | solution.py:419
  31.7 1.1 %collective-permute-done.4.got_ref = f32[2,2,8,128]{3,2,1,0:T(8,128)S(1)} collective-permute-done((f32[2,2,8,128]{3,2,1,0:T(8,128)S(1)}, f32[2,2,8,128]{3,2,1,0:T(8,128)S(1)}, u32[]{:S(2)}, u32[]{:S(2)}) %collective-permute-start.4) | collective-permute-done | bytes 16416 | tf_op jit(solution)/shard_map/ppermute | solution.py:493
  32.7 6.3 %shard_map.168 = (f32[12,8,128]{2,1,0:T(8,128)S(1)}, f32[12,8,128]{2,1,0:T(8,128)S(1)}, f32[12,8,128]{2,1,0:T(8,128)S(1)}, f32[2,2,8,128]{3,2,1,0:T(8,128)S(1)}) custom-call(f32[12,8,128]{2,1,0:T(8,128)S(1)} %get-tuple-element.42.x_ref, f32[12,8,128]{2,1,0:T(8,128)S(1)} %get-tuple-element.43.v_ref, f32[12,8,128]{2,1,0:T(8,128)S(1)} %get-tuple-element.44.g_ref, ...), custom_call_target="tpu_custom_call" | custom-call | tf_op jit(solution)/shard_map/pallas_call | solution.py:419
  39.2 1.0 %collective-permute-done.5.got_ref = f32[2,2,8,128]{3,2,1,0:T(8,128)S(1)} collective-permute-done((f32[2,2,8,128]{3,2,1,0:T(8,128)S(1)}, f32[2,2,8,128]{3,2,1,0:T(8,128)S(1)}, u32[]{:S(2)}, u32[]{:S(2)}) %collective-permute-start.5) | collective-permute-done | bytes 16416 | tf_op jit(solution)/shard_map/ppermute | solution.py:493
  40.2 6.3 %shard_map.169 = (f32[12,8,128]{2,1,0:T(8,128)S(1)}, f32[12,8,128]{2,1,0:T(8,128)S(1)}, f32[12,8,128]{2,1,0:T(8,128)S(1)}, f32[2,2,8,128]{3,2,1,0:T(8,128)S(1)}) custom-call(f32[12,8,128]{2,1,0:T(8,128)S(1)} %get-tuple-element.46.x_ref, f32[12,8,128]{2,1,0:T(8,128)S(1)} %get-tuple-element.47.v_ref, f32[12,8,128]{2,1,0:T(8,128)S(1)} %get-tuple-element.48.g_ref, ...), custom_call_target="tpu_custom_call" | custom-call | tf_op jit(solution)/shard_map/pallas_call | solution.py:419
  46.7 1.0 %collective-permute-done.6.got_ref = f32[2,2,8,128]{3,2,1,0:T(8,128)S(1)} collective-permute-done((f32[2,2,8,128]{3,2,1,0:T(8,128)S(1)}, f32[2,2,8,128]{3,2,1,0:T(8,128)S(1)}, u32[]{:S(2)}, u32[]{:S(2)}) %collective-permute-start.6) | collective-permute-done | bytes 16416 | tf_op jit(solution)/shard_map/ppermute | solution.py:493
  47.7 6.3 %shard_map.170 = (f32[12,8,128]{2,1,0:T(8,128)S(1)}, f32[12,8,128]{2,1,0:T(8,128)S(1)}, f32[12,8,128]{2,1,0:T(8,128)S(1)}, f32[2,2,8,128]{3,2,1,0:T(8,128)S(1)}) custom-call(f32[12,8,128]{2,1,0:T(8,128)S(1)} %get-tuple-element.50.x_ref, f32[12,8,128]{2,1,0:T(8,128)S(1)} %get-tuple-element.51.v_ref, f32[12,8,128]{2,1,0:T(8,128)S(1)} %get-tuple-element.52.g_ref, ...), custom_call_target="tpu_custom_call" | custom-call | tf_op jit(solution)/shard_map/pallas_call | solution.py:419
  54.2 1.0 %collective-permute-done.7.refs_4_ = f32[2,2,8,128]{3,2,1,0:T(8,128)S(1)} collective-permute-done((f32[2,2,8,128]{3,2,1,0:T(8,128)S(1)}, f32[2,2,8,128]{3,2,1,0:T(8,128)S(1)}, u32[]{:S(2)}, u32[]{:S(2)}) %collective-permute-start.7) | collective-permute-done | bytes 16416 | tf_op jit(solution)/shard_map/ppermute | solution.py:493
  55.2 6.4 %shard_map.171 = f32[16,16,128]{2,1,0:T(8,128)S(1)} custom-call(f32[12,8,128]{2,1,0:T(8,128)S(1)} %get-tuple-element.54.refs_0_, f32[12,8,128]{2,1,0:T(8,128)S(1)} %get-tuple-element.55.refs_1_, f32[12,8,128]{2,1,0:T(8,128)S(1)} %get-tuple-element.56.refs_2_, f32[2,2,8,128]{3,2,1,0:T(8,128)S(1)} %get-tuple-element.57.refs_3_, ...), custom_call_target="tpu_custom_call" | custom-call | tf_op jit(solution)/shard_map/pallas_call | solution.py:419
  61.6 12.4 %all_to_all.5.got_ref = bf16[16,16,128]{2,1,0:T(8,128)(2,1)S(1)} all-to-all(bf16[16,16,128]{2,1,0:T(8,128)(2,1)S(1)} %convert_element_type.28), channel_id=1, replica_groups=mesh['groups'=2,'dom'=16] {'dom'}, dimensions={0} | all-to-all | bytes 131072 | tf_op jit(solution)/shard_map/all_to_all | solution.py:571
  74.1 0.9 %shard_map.172 = (f32[3,8,192]{2,1,0:T(8,128)}, f32[3,8,192]{2,1,0:T(8,128)}, f32[3,8,192]{2,1,0:T(8,128)}) custom-call(f32[2,8]{1,0:T(2,128)S(1)} %pad_maximum_fusion.18.ladder_ref, bf16[16,16,128]{2,1,0:T(8,128)(2,1)S(1)} %all_to_all.5.got_ref), custom_call_target="tpu_custom_call" | custom-call | tf_op jit(solution)/shard_map/pallas_call | solution.py:457
  (100 shorter events, 2.8 us)
Async XLA Ops:
  0.6 0.7 copy-start.11
  1.4 0.8 %copy-start.5 = (f32[8,3,192]{2,0,1:T(8,128)S(1)}, f32[8,3,192]{2,0,1:T(8,128)}, u32[]{:S(2)}) copy-start(f32[8,3,192]{2,0,1:T(8,128)} %param.16) | copy-start | bytes 55300
  2.2 0.8 %copy-start = (bf16[192,128]{1,0:T(8,128)(2,1)S(1)}, bf16[192,128]{1,0:T(8,128)(2,1)}, u32[]{:S(2)}) copy-start(bf16[192,128]{1,0:T(8,128)(2,1)} %param.18) | copy-start | bytes 147460
  3.0 7.7 %collective-permute-start = (bf16[264,128]{1,0:T(8,128)(2,1)S(1)}, bf16[264,128]{1,0:T(8,128)(2,1)S(1)}, u32[]{:S(2)}, u32[]{:S(2)}) collective-permute-start(bf16[264,128]{1,0:T(8,128)(2,1)S(1)} %pad_maximum_fusion.11), channel_id=1, source_target_pairs={{0,8},{1,9},{2,10},{3,11},{4,12},{5,13},{6,14},{7,15},{8,0},{9,1},... | collective-permute-start | bytes 202760 | tf_op jit(solution)/shard_map/ppermute | solution.py:493
  7.0 0.8 %copy-start.10 = (f32[8]{0:T(128)S(1)}, f32[8]{0:T(128)}, u32[]{:S(2)}) copy-start(f32[8]{0:T(128)} %param.17) | copy-start | bytes 100
  7.0 1.4 %copy-start.12 = (s32[8]{0:T(128)S(1)}, s32[8]{0:T(128)}, u32[]{:S(2)}) copy-start(s32[8]{0:T(128)} %param.19) | copy-start | bytes 100
  7.1 1.4 %copy-start.13 = (s32[8]{0:T(128)S(1)}, s32[8]{0:T(128)}, u32[]{:S(2)}) copy-start(s32[8]{0:T(128)} %param.20) | copy-start | bytes 100
  7.1 1.4 %copy-start.9 = (f32[128]{0:T(128)S(1)}, f32[128]{0:T(128)}, u32[]{:S(2)}) copy-start(f32[128]{0:T(128)} %param.23) | copy-start | bytes 1540
  7.1 0.7 copy-start.6
  7.1 1.4 %copy-start.7 = (f32[128]{0:T(128)S(1)}, f32[128]{0:T(128)}, u32[]{:S(2)}) copy-start(f32[128]{0:T(128)} %param.28) | copy-start | bytes 1540
  7.1 1.4 %copy-start.8 = (f32[128]{0:T(128)S(1)}, f32[128]{0:T(128)}, u32[]{:S(2)}) copy-start(f32[128]{0:T(128)} %param.27) | copy-start | bytes 1540
  7.1 1.4 %copy-start.3 = (bf16[128,128]{1,0:T(8,128)(2,1)S(1)}, bf16[128,128]{1,0:T(8,128)(2,1)}, u32[]{:S(2)}) copy-start(bf16[128,128]{1,0:T(8,128)(2,1)} %param.24) | copy-start | bytes 98308
  7.1 1.4 %copy-start.4 = (bf16[128,128]{1,0:T(8,128)(2,1)S(1)}, bf16[128,128]{1,0:T(8,128)(2,1)}, u32[]{:S(2)}) copy-start(bf16[128,128]{1,0:T(8,128)(2,1)} %param.21) | copy-start | bytes 98308
  7.2 1.4 %copy-start.1 = (bf16[128,128]{1,0:T(8,128)(2,1)S(1)}, bf16[128,128]{1,0:T(8,128)(2,1)}, u32[]{:S(2)}) copy-start(bf16[128,128]{1,0:T(8,128)(2,1)} %param.26) | copy-start | bytes 98308
  7.2 1.4 %copy-start.2 = (bf16[128,128]{1,0:T(8,128)(2,1)S(1)}, bf16[128,128]{1,0:T(8,128)(2,1)}, u32[]{:S(2)}) copy-start(bf16[128,128]{1,0:T(8,128)(2,1)} %param.25) | copy-start | bytes 98308
  10.9 4.9 %collective-permute-start.1 = (bf16[456,128]{1,0:T(8,128)(2,1)S(1)}, bf16[456,128]{1,0:T(8,128)(2,1)S(1)}, u32[]{:S(2)}, u32[]{:S(2)}) collective-permute-start(bf16[456,128]{1,0:T(8,128)(2,1)S(1)} %pad_maximum_fusion.8), channel_id=1, source_target_pairs={{0,4},{1,5},{2,6},{3,7},{4,0},{5,1},{6,2},{7,3},{8,12},{9,13},{10,... | collective-permute-start | bytes 350216 | tf_op jit(solution)/shard_map/ppermute | solution.py:493
  16.0 5.9 %collective-permute-start.2 = (bf16[840,128]{1,0:T(8,128)(2,1)S(1)}, bf16[840,128]{1,0:T(8,128)(2,1)S(1)}, u32[]{:S(2)}, u32[]{:S(2)}) collective-permute-start(bf16[840,128]{1,0:T(8,128)(2,1)S(1)} %pad_maximum_fusion.4), channel_id=1, source_target_pairs={{0,2},{1,3},{2,0},{3,1},{4,6},{5,7},{6,4},{7,5},{8,10},{9,11},{10,... | collective-permute-start | bytes 645128 | tf_op jit(solution)/shard_map/ppermute | solution.py:493
  22.3 1.8 %collective-permute-start.3 = (bf16[1680,128]{1,0:T(8,128)(2,1)S(1)}, bf16[1680,128]{1,0:T(8,128)(2,1)S(1)}, u32[]{:S(2)}, u32[]{:S(2)}) collective-permute-start(bf16[1680,128]{1,0:T(8,128)(2,1)S(1)} %pad_maximum_fusion.1), channel_id=1, source_target_pairs={{0,1},{1,0},{2,3},{3,2},{4,5},{5,4},{6,7},{7,6},{8,9},{9,8},{10,11... | collective-permute-start | bytes 1290248 | tf_op jit(solution)/shard_map/ppermute | solution.py:493
  31.5 1.2 %collective-permute-start.4 = (f32[2,2,8,128]{3,2,1,0:T(8,128)S(1)}, f32[2,2,8,128]{3,2,1,0:T(8,128)S(1)}, u32[]{:S(2)}, u32[]{:S(2)}) collective-permute-start(f32[2,2,8,128]{3,2,1,0:T(8,128)S(1)} %get-tuple-element.45.edge_ref), channel_id=1, source_target_pairs={{0,1},{1,0},{2,3},{3,2},{4,5},{5,4},{6,7},{7,6},{8,9},{9,8},{10,11... | collective-permute-start | bytes 49160 | tf_op jit(solution)/shard_map/ppermute | solution.py:493
  39.0 1.2 %collective-permute-start.5 = (f32[2,2,8,128]{3,2,1,0:T(8,128)S(1)}, f32[2,2,8,128]{3,2,1,0:T(8,128)S(1)}, u32[]{:S(2)}, u32[]{:S(2)}) collective-permute-start(f32[2,2,8,128]{3,2,1,0:T(8,128)S(1)} %get-tuple-element.49.edge_ref), channel_id=1, source_target_pairs={{0,1},{1,0},{2,3},{3,2},{4,5},{5,4},{6,7},{7,6},{8,9},{9,8},{10,11... | collective-permute-start | bytes 49160 | tf_op jit(solution)/shard_map/ppermute | solution.py:493
  46.5 1.2 %collective-permute-start.6 = (f32[2,2,8,128]{3,2,1,0:T(8,128)S(1)}, f32[2,2,8,128]{3,2,1,0:T(8,128)S(1)}, u32[]{:S(2)}, u32[]{:S(2)}) collective-permute-start(f32[2,2,8,128]{3,2,1,0:T(8,128)S(1)} %get-tuple-element.53.edge_ref), channel_id=1, source_target_pairs={{0,1},{1,0},{2,3},{3,2},{4,5},{5,4},{6,7},{7,6},{8,9},{9,8},{10,11... | collective-permute-start | bytes 49160 | tf_op jit(solution)/shard_map/ppermute | solution.py:493
  54.0 1.2 %collective-permute-start.7 = (f32[2,2,8,128]{3,2,1,0:T(8,128)S(1)}, f32[2,2,8,128]{3,2,1,0:T(8,128)S(1)}, u32[]{:S(2)}, u32[]{:S(2)}) collective-permute-start(f32[2,2,8,128]{3,2,1,0:T(8,128)S(1)} %get-tuple-element.57.refs_3_), channel_id=1, source_target_pairs={{0,1},{1,0},{2,3},{3,2},{4,5},{5,4},{6,7},{7,6},{8,9},{9,8},{10,11... | collective-permute-start | bytes 49160 | tf_op jit(solution)/shard_map/ppermute | solution.py:493
